TPU v7x, 256 devices: a whole 4x4x8 slice. The times are simulated.
256 devices in a mesh: ctx: 64 (over y, z, core), head: 4 (over x).
Axes of the slice: x: 4, y: 4, z: 8, core: 2. Of those that a mesh axis runs over, the one named last changes fastest.
Arguments:
- queries: bfloat16 [16384, 4096], P(('ctx', 'head')), may hold values from -9 to 9
- keys: bfloat16 [16384, 1024], P(('ctx', 'head')), may hold values from -9 to 9
- values: bfloat16 [16384, 1024], P(('ctx', 'head')), may hold values from -6 to 6
- output_cotangent: bfloat16 [16384, 4096], P(('ctx', 'head')), may hold values from -6 to 6
- tile_order: int32 [256], P('ctx'), may hold values from 0 to 255, each once
- doc_lengths: int32 [4], replicated, may hold values from 1 to 8192, 16384 in all
- read_peer: int32 [4096, 1], replicated, may hold values from 0 to 63; in each aligned block of 64 rows (0 to 63, 64 to 127, ...) at most 2 rows name the same one
- read_slot: int32 [4096], replicated, may hold values from 0 to 3
Outputs:
- attended: bfloat16 [16384, 4096], P(('ctx', 'head'))
- grad_queries: bfloat16 [16384, 4096], P(('ctx', 'head'))
- grad_keys: bfloat16 [16384, 1024], P(('ctx', 'head'))
- grad_values: bfloat16 [16384, 1024], P(('ctx', 'head'))
Inputs may be any that keep to these rules, and one draw needn't show every extreme that they name: `read_peer`: the 64 rows of one group (an aligned block) name any one group at most 2 times; some block names some group exactly 2 times.
All inputs are finite; a program needn't handle non-finite values.
Results may differ from a plain program's by a relative error of at most 0.028.
Values may be sent and summed in bfloat16 or wider, within the bound.
No kernel may reach another device: no remote copies, remote signals or barrier semaphores. Data moves between devices by JAX's collectives and lax.ppermute only.
A program may use at most 192 MiB of HBM per device.

v0:
```python
import jax
import jax.numpy as jnp
from jax import lax
from jax.sharding import PartitionSpec as P

HEAD_SIZE = 128
MOST = 2


def read_table(peer_column, slot_column, groups, read_count, tiles_each):
    peer_rows = peer_column.reshape(groups, read_count)
    base_rows = slot_column.reshape(groups, read_count)
    entry_ids = jnp.arange(read_count, dtype=jnp.int32)
    same_peer = peer_rows[:, :, None] == peer_rows[:, None, :]
    earlier = entry_ids[None, None, :] < entry_ids[None, :, None]
    occurrence = jnp.sum((same_peer & earlier).astype(jnp.int32), axis=2)
    first_entry = jnp.min(jnp.where(same_peer, entry_ids[None, None, :], read_count), axis=2)
    first_base = jnp.take_along_axis(base_rows, first_entry, axis=1)
    return (peer_rows, occurrence, (first_base + occurrence) % tiles_each)


def document_of(positions, doc_lengths):
    doc_ends = jnp.cumsum(doc_lengths, dtype=jnp.int32)
    return jnp.sum((positions[..., None] >= doc_ends).astype(jnp.int32), axis=-1)


def per_device(
    queries, keys, values, output_cotangent, tile_order, doc_lengths, read_peer, read_slot
):
    groups = lax.axis_size("ctx")
    my_group = lax.axis_index("ctx")
    local_q, local_k, local_v, local_g = (
        lax.all_to_all(queries, "head", split_axis=1, concat_axis=0, tiled=True),
        lax.all_to_all(keys, "head", split_axis=1, concat_axis=0, tiled=True),
        lax.all_to_all(values, "head", split_axis=1, concat_axis=0, tiled=True),
        lax.all_to_all(output_cotangent, "head", split_axis=1, concat_axis=0, tiled=True),
    )
    count_of_rows = local_q.shape[0]
    tiles_each = tile_order.shape[0]
    tile_len = count_of_rows // tiles_each
    key_value_width = local_k.shape[1]
    kv_heads = key_value_width // HEAD_SIZE
    q_heads = local_q.shape[1] // HEAD_SIZE
    group_width = q_heads // kv_heads
    read_count = read_peer.shape[0] // groups
    score_scale = HEAD_SIZE ** (-0.5)
    peer_rows, occurrence, slot_ids = read_table(
        read_peer[:, 0], read_slot, groups, read_count, tiles_each
    )
    within = jnp.arange(tile_len, dtype=jnp.int32)
    query_pos = (tile_order[:, None] * tile_len + within[None, :]).reshape(count_of_rows)
    query_doc = document_of(query_pos, doc_lengths)
    reader_ids = jnp.arange(groups, dtype=jnp.int32)
    capacity = jnp.arange(MOST, dtype=jnp.int32)
    asked_for = (peer_rows == my_group) & (reader_ids[:, None] != my_group)
    matched = asked_for[:, :, None] & (occurrence[:, :, None] == capacity[None, None, :])
    wanted = jnp.sum(jnp.where(matched, slot_ids[:, :, None] + 1, 0), axis=1) - 1
    chosen = wanted[:, :, None] == jnp.arange(tiles_each, dtype=jnp.int32)[None, None, :]
    local_kv = jnp.concatenate([local_k, local_v], axis=1)
    kv_tiles = local_kv.reshape(tiles_each, tile_len * 2 * key_value_width)
    outgoing = jnp.einsum(
        "got,tx->gox", chosen.astype(jnp.bfloat16), kv_tiles, preferred_element_type=jnp.float32
    )
    outgoing = outgoing.astype(jnp.bfloat16).reshape(groups, MOST, tile_len, 2 * key_value_width)
    outgoing_ids = jnp.sum(jnp.where(chosen, tile_order[None, None, :], 0), axis=2)
    my_peers = lax.dynamic_index_in_dim(peer_rows, my_group, 0, keepdims=False)
    my_occurrence = lax.dynamic_index_in_dim(occurrence, my_group, 0, keepdims=False)
    usable = my_peers != my_group
    cell_of = my_peers * MOST + my_occurrence
    arrived, arrived_ids = (
        lax.all_to_all(outgoing, "ctx", split_axis=0, concat_axis=0, tiled=True),
        lax.all_to_all(outgoing_ids, "ctx", split_axis=0, concat_axis=0, tiled=True),
    )
    read_ids = jnp.take(arrived_ids.reshape(groups * MOST), cell_of, axis=0)
    key_pos = jnp.concatenate(
        [query_pos, (read_ids[:, None] * tile_len + within[None, :]).reshape(-1)]
    )
    key_ok = jnp.concatenate([jnp.ones((count_of_rows,), jnp.bool_), jnp.repeat(usable, tile_len)])
    key_doc = document_of(key_pos, doc_lengths)
    allowed = (
        key_ok[None, :]
        & (key_doc[None, :] == query_doc[:, None])
        & (key_pos[None, :] <= query_pos[:, None])
    )
    flat_tiles = arrived.reshape(groups * MOST, tile_len * 2 * key_value_width)
    all_kv = jnp.concatenate(
        [
            local_kv,
            jnp.take(flat_tiles, cell_of, axis=0).reshape(
                read_count * tile_len, 2 * key_value_width
            ),
        ],
        axis=0,
    )
    key_count = all_kv.shape[0]

    def head_pair(source, pair_index):
        return source[:, 2 * pair_index * HEAD_SIZE : (2 * pair_index + 2) * HEAD_SIZE].reshape(
            count_of_rows, 2, HEAD_SIZE
        )

    def kv_head(source, pair_index, second):
        column = second * key_value_width + 2 * pair_index // group_width * HEAD_SIZE
        return source[:, column : column + HEAD_SIZE]

    pair_total = q_heads // 2
    outputs = []
    query_grads = []
    key_grads = [jnp.zeros((key_count, HEAD_SIZE), jnp.float32)] * kv_heads
    value_grads = [jnp.zeros((key_count, HEAD_SIZE), jnp.float32)] * kv_heads
    for pair_index in range(pair_total):
        scores = (
            jnp.einsum(
                "qhd,kd->hqk",
                head_pair(local_q, pair_index),
                kv_head(all_kv, pair_index, 0),
                preferred_element_type=jnp.float32,
            )
            * score_scale
        )
        scores = jnp.where(allowed[None], scores, -jnp.inf)
        shifted = jnp.exp(scores - jnp.max(scores, axis=2, keepdims=True))
        probability = shifted / jnp.sum(shifted, axis=2, keepdims=True)
        forward_rounded = probability.astype(jnp.bfloat16)
        forward_output = jnp.einsum(
            "hqk,kd->qhd",
            forward_rounded,
            kv_head(all_kv, pair_index, 1),
            preferred_element_type=jnp.float32,
        )
        output = forward_output.astype(jnp.bfloat16)
        outputs.append(output)
        grad_pair = head_pair(local_g, pair_index)
        row_delta = jnp.sum(grad_pair.astype(jnp.float32) * output.astype(jnp.float32), axis=2).T
        dprobs = jnp.einsum(
            "qhd,kd->hqk",
            grad_pair,
            kv_head(all_kv, pair_index, 1),
            preferred_element_type=jnp.float32,
        )
        dscores = (probability * (dprobs - row_delta[:, :, None])).astype(jnp.bfloat16)
        grad_q = jnp.einsum(
            "hqk,kd->qhd",
            dscores,
            kv_head(all_kv, pair_index, 0),
            preferred_element_type=jnp.float32,
        )
        grad_k = (
            jnp.einsum(
                "hqk,qhd->kd",
                dscores,
                head_pair(local_q, pair_index),
                preferred_element_type=jnp.float32,
            )
            * score_scale
        )
        grad_v = jnp.einsum(
            "hqk,qhd->kd", forward_rounded, grad_pair, preferred_element_type=jnp.float32
        )
        grad_q, grad_k, grad_v = ((grad_q * score_scale).astype(jnp.bfloat16), grad_k, grad_v)
        query_grads.append(grad_q)
        target = 2 * pair_index // group_width
        key_grads[target] = key_grads[target] + grad_k
        value_grads[target] = value_grads[target] + grad_v
    attended = jnp.concatenate(outputs, axis=1).reshape(count_of_rows, q_heads * HEAD_SIZE)
    grad_queries = jnp.concatenate(query_grads, axis=1).reshape(count_of_rows, q_heads * HEAD_SIZE)
    key_total = jnp.concatenate(key_grads, axis=1)
    value_total = jnp.concatenate(value_grads, axis=1)
    own_terms = jnp.concatenate([key_total[:count_of_rows], value_total[:count_of_rows]], axis=1)
    read_terms = jnp.concatenate([key_total[count_of_rows:], value_total[count_of_rows:]], axis=1)
    read_terms = read_terms.reshape(read_count, tile_len * 2 * key_value_width)
    read_terms = jnp.where(usable[:, None], read_terms, 0.0).astype(jnp.bfloat16)
    cell_ids = jnp.arange(groups * MOST, dtype=jnp.int32)
    filled = (cell_of[None, :] == cell_ids[:, None]) & usable[None, :]
    entry_of = (
        jnp.sum(jnp.where(filled, jnp.arange(read_count, dtype=jnp.int32)[None, :] + 1, 0), axis=1)
        - 1
    )
    returning = jnp.where(
        (entry_of >= 0)[:, None],
        jnp.take(read_terms, jnp.maximum(entry_of, 0), axis=0),
        jnp.zeros_like(read_terms[:1]),
    )
    returning = returning.reshape(groups, MOST, tile_len, 2 * key_value_width)
    returned = lax.all_to_all(returning, "ctx", split_axis=0, concat_axis=0, tiled=True)
    collected = jnp.einsum(
        "got,gox->tx",
        chosen.astype(jnp.bfloat16),
        returned.reshape(groups, MOST, tile_len * 2 * key_value_width),
        preferred_element_type=jnp.float32,
    )
    own_total = (own_terms + collected.reshape(count_of_rows, 2 * key_value_width)).astype(
        jnp.bfloat16
    )
    return (
        lax.all_to_all(attended, "head", split_axis=0, concat_axis=1, tiled=True),
        lax.all_to_all(grad_queries, "head", split_axis=0, concat_axis=1, tiled=True),
        lax.all_to_all(
            own_total[:, :key_value_width], "head", split_axis=0, concat_axis=1, tiled=True
        ),
        lax.all_to_all(
            own_total[:, key_value_width:], "head", split_axis=0, concat_axis=1, tiled=True
        ),
    )


def solution(mesh):
    in_specs = (
        P(("ctx", "head"), None),
        P(("ctx", "head"), None),
        P(("ctx", "head"), None),
        P(("ctx", "head"), None),
        P("ctx"),
        P(),
        P(),
        P(),
    )
    out_specs = (
        P(("ctx", "head"), None),
        P(("ctx", "head"), None),
        P(("ctx", "head"), None),
        P(("ctx", "head"), None),
    )
    return jax.shard_map(
        per_device, mesh=mesh, in_specs=in_specs, out_specs=out_specs, check_vma=False
    )
```

profile of v0, /device:TPU:6, one launch (start us, length us, event | category | flops | bytes accessed | tf_op | source)
XLA Modules:
  0.0 762.0 jit_solution(7168933076158187032)
XLA Ops:
  3.5 2.9 fusion.28
  6.6 26.7 %gather_fusion.3 = s32[4096]{0:T(1024)S(1)} fusion(s32[64,64]{1,0:T(8,128)S(1)} %reshape.435, s32[4096]{0:T(1024)S(1)} %reshape.478), kind=kCustom, calls=%fused_computation.3 | custom fusion | bytes 65536 | tf_op jit(solution)/shard_map/jit(take_along_axis)/gather | solution.py:18
  34.3 12.1 %all-to-all-start.3 = ((s32[64,1,2]{2,1,0:T(1,128)}), s32[64,1,2]{2,1,0:T(1,128)S(1)}, u32[]{:S(2)}, u32[]{:S(2)}) async-start(s32[64,1,2]{2,1,0:T(1,128)} %copy.228), calls=%async_computation.3 | async-start | bytes 65536 | tf_op jit(solution)/shard_map/all_to_all | solution.py:72
  47.1 8.7 %all-to-all-done.3 = s32[64,1,2]{2,1,0:T(1,128)S(1)} async-done(((s32[64,1,2]{2,1,0:T(1,128)}), s32[64,1,2]{2,1,0:T(1,128)S(1)}, u32[]{:S(2)}, u32[]{:S(2)}) %all-to-all-start.3) | async-done | bytes 544 | tf_op jit(solution)/shard_map/all_to_all | solution.py:72
  55.9 4.8 all-to-all-start
  61.3 3.2 all-to-all-done
  64.6 5.4 all-to-all-start.1
  70.8 3.1 all-to-all-done.1
  73.8 5.5 all-to-all-start.4
  80.4 5.0 all-to-all-done.4
  85.4 5.5 all-to-all-start.6
  90.9 5.6 convolution_convert_fusion
  96.5 10.1 %copy.331 = bf16[16,8,64,512]{3,2,1,0:T(8,128)(2,1)} copy(bf16[16,8,64,512]{3,1,2,0:T(8,128)(2,1)} %bitcast.246) | data formatting | bytes 16777216
  106.6 7.7 %copy.227 = bf16[64,2,64,512]{3,2,1,0:T(8,128)(2,1)} copy(bf16[64,2,64,512]{3,2,0,1:T(8,128)(2,1)} %bitcast.247) | data formatting | bytes 16777216 | tf_op jit(solution)/shard_map/reshape | solution.py:64
  114.3 5.9 all-to-all-start.2
  125.3 12.4 %compare_and_fusion = pred[256,4352]{0,1:T(8,128)(4,1)S(1)} fusion(s32[256]{0:T(256)S(1)} %add.215, s32[256]{0:T(256)S(1)} %convert_reduce_fusion.2, s32[4352]{0:T(1024)S(1)} %constant_dynamic-update-slice_fusion, s32[4352]{0:T(1024)S(1)} %convert_reduce_fusion.1, pred[4352]{0:T(1024)(128)(4,1)S(1)} %concatenate.32), kind=kLoop, calls=%fused_computation.59 | loop fusion | flops 4456448 | bytes 1155328 | tf_op jit(solution)/shard_map/and | solution.py:81
  138.6 166.5 %all-to-all-done.2 = bf16[64,2,64,512]{3,2,1,0:T(8,128)(2,1)} async-done(((bf16[64,2,64,512]{3,2,1,0:T(8,128)(2,1)}), bf16[64,2,64,512]{3,2,1,0:T(8,128)(2,1)}, u32[]{:S(2)}, u32[]{:S(2)}) %all-to-all-start.2) | async-done | bytes 8388640 | tf_op jit(solution)/shard_map/all_to_all | solution.py:71
  305.1 12.4 %copy.332 = bf16[16,8,64,512]{3,1,2,0:T(8,128)(2,1)} copy(bf16[16,8,64,512]{3,2,1,0:T(8,128)(2,1)} %bitcast.99) | data formatting | bytes 16777216
  317.6 13.4 %gather_fusion = bf16[64,32768]{1,0:T(8,128)(2,1)} fusion(bf16[128,32768]{1,0:T(8,128)(2,1)} %bitcast.244, s32[1024]{0:T(1024)S(1)} %pad_clamp_fusion.1), kind=kCustom, calls=%fused_computation | custom fusion | bytes 8388864 | tf_op jit(solution)/shard_map/jit(_take)/gather | solution.py:89
  330.9 7.4 gather.22
  338.4 2.6 broadcast_select_fusion
  342.3 4.8 bitcast_select_fusion
  347.0 8.4 %exponential_reduce_fusion = (f32[2,256]{1,0:T(2,128)S(1)}, f32[2,256,4352]{1,2,0:T(8,128)S(1)}) fusion(f32[2,256,4352]{1,2,0:T(8,128)} %bitcast_select_fusion), kind=kOutput, calls=%fused_computation.37 | output fusion | flops 4460799 | bytes 17827840 | tf_op jit(solution)/shard_map/sub | solution.py:122
  355.4 2.6 fusion.27
  359.4 2.9 convolution_bitcast_fusion.1
  362.3 2.4 fusion.9
  364.8 3.0 convolution_bitcast_fusion.5
  367.8 4.7 bitcast_select_fusion.2
  372.5 8.4 %exponential_reduce_fusion.2 = (f32[2,256]{1,0:T(2,128)S(1)}, f32[2,256,4352]{1,2,0:T(8,128)S(1)}) fusion(f32[2,256,4352]{1,2,0:T(8,128)} %bitcast_select_fusion.2), kind=kOutput, calls=%fused_computation.41 | output fusion | flops 4460799 | bytes 17827840 | tf_op jit(solution)/shard_map/sub | solution.py:122
  380.9 2.6 fusion.25
  384.9 2.9 convolution_bitcast_fusion.3
  387.8 2.2 fusion.13
  390.0 3.0 convolution_bitcast_fusion.7
  393.0 4.7 bitcast_select_fusion.1
  397.7 8.4 %exponential_reduce_fusion.1 = (f32[2,256]{1,0:T(2,128)S(1)}, f32[2,256,4352]{1,2,0:T(8,128)S(1)}) fusion(f32[2,256,4352]{1,2,0:T(8,128)} %bitcast_select_fusion.1), kind=kOutput, calls=%fused_computation.39 | output fusion | flops 4460799 | bytes 17827840 | tf_op jit(solution)/shard_map/sub | solution.py:122
  406.1 2.6 fusion.26
  410.3 2.9 fusion.23
  413.2 3.6 fusion.11
  416.8 4.7 bitcast_select_fusion.3
  421.5 8.4 %exponential_reduce_fusion.3 = (f32[2,256]{1,0:T(2,128)S(1)}, f32[2,256,4352]{1,2,0:T(8,128)S(1)}) fusion(f32[2,256,4352]{1,2,0:T(8,128)} %bitcast_select_fusion.3), kind=kOutput, calls=%fused_computation.43 | output fusion | flops 4460799 | bytes 17827840 | tf_op jit(solution)/shard_map/sub | solution.py:122
  429.9 2.6 fusion.24
  435.8 3.4 fusion.15
  445.4 2.4 fusion.16
  447.8 6.5 copy.275
  454.2 7.8 %reshape.451 = bf16[64,32768]{1,0:T(8,128)(2,1)} reshape(bf16[4096,512]{1,0:T(8,128)(2,1)} %copy.275) | data formatting | bytes 8388608 | tf_op jit(solution)/shard_map/reshape | solution.py:171
  462.0 4.9 select_convert_fusion
  466.9 19.2 %gather_fusion.2 = bf16[128,32768]{1,0:T(8,128)(2,1)} fusion(bf16[64,32768]{1,0:T(8,128)(2,1)} %select_convert_fusion, s32[1024]{0:T(1024)} %pad_clamp_fusion), kind=kCustom, calls=%fused_computation.2 | custom fusion | bytes 16777728 | tf_op jit(solution)/shard_map/jit(_take)/gather | solution.py:181
  486.1 10.2 %copy.333 = bf16[16,8,64,512]{3,2,1,0:T(8,128)(2,1)} copy(bf16[16,8,64,512]{3,1,2,0:T(8,128)(2,1)} %bitcast.248) | data formatting | bytes 16777216
  496.3 7.4 select_select_fusion
  503.7 7.0 all-to-all-start.8
  510.6 3.5 fusion.37
  514.2 3.4 fusion.39
  517.6 3.4 fusion.38
  521.1 2.1 fusion.40
  527.1 168.5 %all-to-all-done.8 = bf16[64,2,64,512]{3,2,1,0:T(8,128)(2,1)} async-done(((bf16[64,2,64,512]{3,2,1,0:T(8,128)(2,1)}), bf16[64,2,64,512]{3,2,1,0:T(8,128)(2,1)}, u32[]{:S(2)}, u32[]{:S(2)}) %all-to-all-start.8) | async-done | bytes 8388640 | tf_op jit(solution)/shard_map/all_to_all | solution.py:185
  695.5 5.0 all-to-all-start.7
  700.6 14.6 %reshape.508 = bf16[64,2,32768]{2,1,0:T(2,128)(2,1)} reshape(bf16[64,2,64,512]{3,2,1,0:T(8,128)(2,1)} %all-to-all-done.8) | data formatting | bytes 16777216 | tf_op jit(solution)/shard_map/reshape | solution.py:189
  715.1 12.2 %convolution_bitcast_fusion = f32[4,32768]{1,0:T(4,128)S(1)} fusion(bf16[64,2,32768]{2,1,0:T(2,128)(2,1)} %reshape.508, s32[64,2]{0,1:T(2,128)S(1)} %copy-done.18), kind=kOutput, calls=%fused_computation.9 | convolution fusion | flops 33554944 | bytes 8913408 | tf_op jit(solution)/shard_map/got,gox->tx/dot_general | solution.py:186
  729.8 4.8 all-to-all-start.5
  736.5 6.1 all-to-all-done.5
  742.6 5.4 all-to-all-start.10
  748.7 3.1 all-to-all-done.10
  751.9 5.4 all-to-all-start.9
  758.1 1.9 copy.327
  (147 shorter events, 39.7 us)
Async XLA Ops:
  6.5 27.0 %copy-start.23 = (s32[4]{0:T(128)S(1)}, s32[4]{0:T(128)}, u32[]{:S(2)}) copy-start(s32[4]{0:T(128)} %param.12) | copy-start | bytes 52
  6.6 39.9 %copy-start.15 = (bf16[64,1024]{1,0:T(8,128)(2,1)S(1)}, bf16[64,1024]{1,0:T(8,128)(2,1)}, u32[]{:S(2)}) copy-start(bf16[64,1024]{1,0:T(8,128)(2,1)} %param.9) | copy-start | bytes 393220
  6.6 54.1 %copy-start.16 = (bf16[64,1024]{1,0:T(8,128)(2,1)S(1)}, bf16[64,1024]{1,0:T(8,128)(2,1)}, u32[]{:S(2)}) copy-start(bf16[64,1024]{1,0:T(8,128)(2,1)} %param.10) | copy-start | bytes 393220
  6.6 63.4 %copy-start.13 = (bf16[64,4096]{1,0:T(8,128)(2,1)S(1)}, bf16[64,4096]{1,0:T(8,128)(2,1)}, u32[]{:S(2)}) copy-start(bf16[64,4096]{1,0:T(8,128)(2,1)} %param.8) | copy-start | bytes 1572868
  6.6 72.8 %copy-start.14 = (bf16[64,4096]{1,0:T(8,128)(2,1)S(1)}, bf16[64,4096]{1,0:T(8,128)(2,1)}, u32[]{:S(2)}) copy-start(bf16[64,4096]{1,0:T(8,128)(2,1)} %param.11) | copy-start | bytes 1572868
  33.5 63.0 %copy-start.17 = (s32[64,2]{0,1:T(2,128)}, s32[64,2]{0,1:T(2,128)S(1)}, u32[]{:S(2)}) copy-start(s32[64,2]{0,1:T(2,128)S(1)} %broadcast_add_fusion) | copy-start | bytes 1540
  34.3 21.5 %all-to-all-start.3 = ((s32[64,1,2]{2,1,0:T(1,128)}), s32[64,1,2]{2,1,0:T(1,128)S(1)}, u32[]{:S(2)}, u32[]{:S(2)}) async-start(s32[64,1,2]{2,1,0:T(1,128)} %copy.228), calls=%async_computation.3 | async-start | bytes 65536 | tf_op jit(solution)/shard_map/all_to_all | solution.py:72
  55.9 8.7 %all-to-all-start = ((bf16[64,4,256]{2,0,1:T(8,128)(2,1)}), bf16[64,4,256]{2,0,1:T(8,128)(2,1)S(1)}, u32[]{:S(2)}, u32[]{:S(2)}) async-start(bf16[64,4,256]{2,0,1:T(8,128)(2,1)} %bitcast.243), calls=%async_computation | async-start | bytes 262144 | tf_op jit(solution)/shard_map/all_to_all | solution.py:34
  64.6 9.3 %all-to-all-start.1 = ((bf16[64,4,256]{2,0,1:T(8,128)(2,1)}), bf16[64,4,256]{2,0,1:T(8,128)(2,1)S(1)}, u32[]{:S(2)}, u32[]{:S(2)}) async-start(bf16[64,4,256]{2,0,1:T(8,128)(2,1)} %bitcast.242), calls=%async_computation.1 | async-start | bytes 262144 | tf_op jit(solution)/shard_map/all_to_all | solution.py:35
  73.8 11.5 %all-to-all-start.4 = ((bf16[64,4,1024]{2,0,1:T(8,128)(2,1)}), bf16[64,4,1024]{2,0,1:T(8,128)(2,1)S(1)}, u32[]{:S(2)}, u32[]{:S(2)}) async-start(bf16[64,4,1024]{2,0,1:T(8,128)(2,1)} %bitcast.241), calls=%async_computation.4 | async-start | bytes 1048576 | tf_op jit(solution)/shard_map/all_to_all | solution.py:33
  85.4 29.0 %all-to-all-start.6 = ((bf16[64,4,1024]{2,0,1:T(8,128)(2,1)}), bf16[64,4,1024]{2,0,1:T(8,128)(2,1)S(1)}, u32[]{:S(2)}, u32[]{:S(2)}) async-start(bf16[64,4,1024]{2,0,1:T(8,128)(2,1)} %bitcast.240), calls=%async_computation.6 | async-start | bytes 1048576 | tf_op jit(solution)/shard_map/all_to_all | solution.py:36
  114.3 5.9 copy-start.24
  114.3 190.8 %all-to-all-start.2 = ((bf16[64,2,64,512]{3,2,1,0:T(8,128)(2,1)}), bf16[64,2,64,512]{3,2,1,0:T(8,128)(2,1)}, u32[]{:S(2)}, u32[]{:S(2)}) async-start(bf16[64,2,64,512]{3,2,1,0:T(8,128)(2,1)} %copy.227), calls=%async_computation.2 | async-start | bytes 16777216 | tf_op jit(solution)/shard_map/all_to_all | solution.py:71
  120.6 17.1 %copy-start.21 = (pred[64]{0:T(512)(128)(4,1)}, pred[64]{0:T(512)(128)(4,1)S(1)}, u32[]{:S(2)}) copy-start(pred[64]{0:T(512)(128)(4,1)S(1)} %compare_bitcast_fusion) | copy-start | bytes 196
  342.3 93.5 %copy-start = (bf16[4352,512]{1,0:T(8,128)(2,1)}, bf16[4352,512]{1,0:T(8,128)(2,1)S(1)}, u32[]{:S(2)}) copy-start(bf16[4352,512]{1,0:T(8,128)(2,1)S(1)} %pad_maximum_fusion.2) | copy-start | bytes 13369348
  364.7 3.0 copy-start.6
  390.0 3.0 copy-start.7
  408.7 1.6 copy-start.10
  432.5 1.6 copy-start.11
  434.1 5.0 slice-start
  435.7 8.2 %copy-start.2 = (f32[4352,128]{0,1:T(8,128)}, f32[4352,128]{0,1:T(8,128)S(1)}, u32[]{:S(2)}) copy-start(f32[4352,128]{0,1:T(8,128)S(1)} %fusion.22) | copy-start | bytes 6684676
  435.7 3.4 slice-start.1
  435.7 3.6 copy-start.8
  439.4 2.3 copy-start.5
  439.4 3.0 copy-start.9
  442.4 1.6 copy-start.3
  442.4 3.0 copy-start.1
  444.0 1.4 copy-start.4
  454.2 7.8 %copy-start.22 = (pred[64]{0:T(512)(128)(4,1)S(1)}, pred[64]{0:T(512)(128)(4,1)}, u32[]{:S(2)}) copy-start(pred[64]{0:T(512)(128)(4,1)} %copy-done.21) | copy-start | bytes 196
  486.1 10.2 %copy-start.19 = (pred[64,2]{1,0:T(8,128)(4,1)S(1)}, pred[64,2]{1,0:T(8,128)(4,1)}, u32[]{:S(2)}) copy-start(pred[64,2]{1,0:T(8,128)(4,1)} %ge.82) | copy-start | bytes 388
  486.1 10.2 %copy-start.20 = (pred[64,2]{1,0:T(8,128)(4,1)S(1)}, pred[64,2]{1,0:T(8,128)(4,1)}, u32[]{:S(2)}) copy-start(pred[64,2]{1,0:T(8,128)(4,1)} %le.75) | copy-start | bytes 388
  503.7 191.9 %all-to-all-start.8 = ((bf16[64,2,64,512]{3,2,1,0:T(8,128)(2,1)}), bf16[64,2,64,512]{3,2,1,0:T(8,128)(2,1)}, u32[]{:S(2)}, u32[]{:S(2)}) async-start(bf16[64,2,64,512]{3,2,1,0:T(8,128)(2,1)} %select_select_fusion), calls=%async_computation.8 | async-start | bytes 16777216 | tf_op jit(solution)/shard_map/all_to_all | solution.py:185
  510.6 10.4 %slice-start.2 = ((s8[4456448]{0:T(1024)(128)(4,1)}), s8[4194304]{0:T(1024)(128)(4,1)S(1)}, s32[]{:S(2)}) async-start(s8[4456448]{0:T(1024)(128)(4,1)} %bitcast.251), calls=%async_computation.13 | async-start | bytes 8388608
  514.2 6.9 slice-start.3
  521.1 3.5 copy-start.12
  695.5 34.3 %all-to-all-start.7 = ((bf16[4,64,1024]{2,1,0:T(8,128)(2,1)}), bf16[4,64,1024]{2,1,0:T(8,128)(2,1)S(1)}, u32[]{:S(2)}, u32[]{:S(2)}) async-start(bf16[4,64,1024]{2,1,0:T(8,128)(2,1)} %all_to_all.147), calls=%async_computation.7 | async-start | bytes 1048576 | tf_op jit(solution)/shard_map/all_to_all | solution.py:197
  700.5 14.6 %copy-start.18 = (s32[64,2]{0,1:T(2,128)S(1)}, s32[64,2]{0,1:T(2,128)}, u32[]{:S(2)}) copy-start(s32[64,2]{0,1:T(2,128)} %copy-done.17) | copy-start | bytes 1540
  729.8 12.8 %all-to-all-start.5 = ((bf16[4,64,1024]{2,1,0:T(8,128)(2,1)}), bf16[4,64,1024]{2,1,0:T(8,128)(2,1)}, u32[]{:S(2)}, u32[]{:S(2)}) async-start(bf16[4,64,1024]{2,1,0:T(8,128)(2,1)} %all_to_all.139), calls=%async_computation.5 | async-start | bytes 1048576 | tf_op jit(solution)/shard_map/all_to_all | solution.py:196
  742.6 9.3 %all-to-all-start.10 = ((bf16[4,64,256]{2,1,0:T(8,128)(2,1)}), bf16[4,64,256]{2,1,0:T(8,128)(2,1)S(1)}, u32[]{:S(2)}, u32[]{:S(2)}) async-start(bf16[4,64,256]{2,1,0:T(8,128)(2,1)} %bitcast.71), calls=%async_computation.10 | async-start | bytes 262144 | tf_op jit(solution)/shard_map/all_to_all | solution.py:201
  751.9 9.3 %all-to-all-start.9 = ((bf16[4,64,256]{2,1,0:T(8,128)(2,1)}), bf16[4,64,256]{2,1,0:T(8,128)(2,1)S(1)}, u32[]{:S(2)}, u32[]{:S(2)}) async-start(bf16[4,64,256]{2,1,0:T(8,128)(2,1)} %bitcast.69), calls=%async_computation.9 | async-start | bytes 262144 | tf_op jit(solution)/shard_map/all_to_all | solution.py:198
where the time goes:
time: 775 us; the launch traced here: 762 us
  waiting for transfers between devices  365 us (47%)
  local copies, waits for them, and re-layouts  159 us (21%)
  matrix products  86 us (11%)
  other arithmetic  83.7 us (11%)
  starting transfers between devices  66.7 us (9%)
    all_to_all x1, waiting for transfers between devices, per_device(): lax.all_to_all(returning, 'ctx', split_axis=0, concat_axis=0, tiled=True)  168 us
    all_to_all x1, waiting for transfers between devices, per_device(): lax.all_to_all(outgoing, 'ctx', split_axis=0, concat_axis=0, tiled=True)  166 us
    unnamed x63, local copies, waits for them, and re-layouts  36.7 us
    sub x4, other arithmetic, per_device(): shifted = jnp.exp(scores - jnp.max(scores, axis=2, keepdims=True))  33.5 us
    gather x3, local copies, waits for them, and re-layouts, read_table(): first_base = jnp.take_along_axis(base_rows, first_entry, axis=1)  26.8 us
    gather x2, local copies, waits for them, and re-layouts, per_device(): jnp.take(flat_tiles, cell_of, axis=0)  20.8 us
    gather x1, local copies, waits for them, and re-layouts, per_device(): jnp.take(read_terms, jnp.maximum(entry_of, 0), axis=0)  19.2 us
    dot_general x4, matrix products, per_device(): jnp.einsum('qhd,kd->hqk', head_pair(local_q, pair_index), kv_head(all_kv,...  19 us
  transfers between devices with their start and end apart: 11, of which 9 were waited for; matrix products, arithmetic and copies ran while one was open for 12% of the time, Pallas kernels for 0%

commit v1 on v0

v1 whole, which is shorter than its diff:
```python
import jax
import jax.numpy as jnp
from jax import lax
from jax.experimental import pallas as pl
from jax.experimental.pallas import tpu as pltpu
from jax.sharding import Mesh, PartitionSpec as P

HEAD = 128
TILE = 64
SLOTS = 4
KV_HEADS = 8
REP = 4
NX, NY, NZ, NC = 4, 4, 8, 2
GROUPS = NY * NZ * NC
TILES = GROUPS * SLOTS
READS = 64
CHUNK = 4
MOST_TILES = 68
MOST_CHUNKS = MOST_TILES // CHUNK
ROWS = REP * TILE
SCALE = HEAD ** -0.5
LOG2E = 1.4426950408889634
AXES = ("y", "z", "core", "x")
NEG = -1e30


def plan(tile_order, doc_lengths, read_peer, read_slot):
    x, y, core = lax.axis_index("x"), lax.axis_index("y"), lax.axis_index("core")
    ends = jnp.cumsum(doc_lengths, dtype=jnp.int32)

    def mine(table):
        table = table.reshape(NY, NZ, NC, READS)
        table = lax.dynamic_index_in_dim(table, y, 0, keepdims=False)
        return lax.dynamic_index_in_dim(table, core, 1, keepdims=False)

    peers, bases = mine(read_peer), mine(read_slot)
    group = (y * NZ + jnp.arange(NZ, dtype=jnp.int32)) * NC + core
    all_groups = jnp.arange(GROUPS, dtype=jnp.int32)
    same = peers[:, :, None] == all_groups[None, None, :]
    count = jnp.sum(same.astype(jnp.int32), axis=1)
    entry = jnp.arange(READS, dtype=jnp.int32)
    first = jnp.min(jnp.where(same, (entry[None, :] * SLOTS + bases)[:, :, None], READS * SLOTS), axis=1)
    slot = jnp.arange(SLOTS, dtype=jnp.int32)
    listed = ((slot[None, None, :] - first[:, :, None]) & (SLOTS - 1)) < count[:, :, None]
    listed = listed | (all_groups[None, :] == group[:, None])[:, :, None]
    listed = listed.reshape(NZ, TILES)
    order = tile_order.reshape(NY, NZ, NC, SLOTS)
    own = lax.dynamic_index_in_dim(order, y, 0, keepdims=False)
    own = lax.dynamic_index_in_dim(own, core, 1, keepdims=False)
    own = lax.dynamic_index_in_dim(own, x, 1, keepdims=False)
    start = jnp.max(jnp.where(ends[None, :] <= own[:, None] * TILE, ends[None, :], 0), axis=1)
    need = (
        listed
        & (tile_order[None, :] <= own[:, None])
        & (tile_order[None, :] * TILE + (TILE - 1) >= start[:, None])
    )
    rank = jnp.cumsum(need.astype(jnp.int32), axis=1)
    t = jnp.arange(TILES, dtype=jnp.int32)
    tx, tc, tz, ty = t % 4, (t // 4) % 2, (t // 8) % 8, t // 64
    place = ((tx * NY + ty) * NC + tc) * NZ + tz
    code = place + TILES * (tile_order + 1)
    wanted = jnp.where(need, rank, 0)[:, :, None] == 1 + jnp.arange(MOST_TILES, dtype=jnp.int32)
    codes = jnp.sum(jnp.where(wanted, code[None, :, None], 0), axis=1)
    return codes, rank[:, -1], own, ends


def attend(codes, counts, own, ends, q_ref, g_ref, kv_ref, o_ref, dq_ref, dkv_ref, acc, st):
    acc[...] = jnp.zeros_like(acc)
    key_at = lax.broadcasted_iota(jnp.int32, (TILE, ROWS), 0)
    lane = lax.broadcasted_iota(jnp.int32, (1, ROWS), 1) & (TILE - 1)

    def stacked(ref, s):
        return jnp.concatenate([ref[s, :, h * HEAD:(h + 1) * HEAD] for h in range(REP)], axis=0)

    def one_tile(s, carry):
        q = stacked(q_ref, s)
        g = stacked(g_ref, s)
        q_pos = own[s] * TILE + lane
        low = jnp.zeros_like(q_pos)
        for k in range(4):
            low = jnp.where(q_pos >= ends[k], ends[k], low)
        chunks = (counts[s] + (CHUNK - 1)) // CHUNK

        def places(c):
            return [codes[s, c * CHUNK + j] for j in range(CHUNK)]

        def scores(c, top):
            found = places(c)
            keys = jnp.concatenate([kv_ref[f & (TILES - 1), :, :HEAD] for f in found], axis=0)
            raw = lax.dot_general(keys, q, (((1,), (1,)), ((), ())), preferred_element_type=jnp.float32)
            for j, f in enumerate(found):
                base = (f // TILES - 1) * TILE
                part = raw[j * TILE:(j + 1) * TILE]
                part = jnp.where((key_at <= q_pos - base) & (key_at >= low - base), part, NEG)
                st[c, j * TILE:(j + 1) * TILE, :] = part
                top = jnp.maximum(top, jnp.max(part.reshape(TILE // 8, 8, ROWS), axis=0))
            return top

        top = lax.fori_loop(0, chunks, scores, jnp.full((8, ROWS), NEG, jnp.float32))
        top = jnp.max(top, axis=0, keepdims=True) * (SCALE * LOG2E)

        def forward(c, held):
            total, out = held
            prob = jnp.exp2(st[c] * (SCALE * LOG2E) - top)
            st[c] = prob
            total = total + jnp.sum(prob.reshape(CHUNK * TILE // 8, 8, ROWS), axis=0)
            vals = jnp.concatenate([kv_ref[f & (TILES - 1), :, HEAD:] for f in places(c)], axis=0)
            out = out + lax.dot_general(
                vals, prob.astype(jnp.bfloat16), (((0,), (0,)), ((), ())),
                preferred_element_type=jnp.float32)
            return total, out

        total, out = lax.fori_loop(
            0, chunks, forward,
            (jnp.zeros((8, ROWS), jnp.float32), jnp.zeros((HEAD, ROWS), jnp.float32)))
        inv = 1.0 / jnp.sum(total, axis=0, keepdims=True)
        out = (out * inv).astype(jnp.bfloat16).astype(jnp.float32)
        delta = jnp.sum(out * g.astype(jnp.float32).T, axis=0, keepdims=True)
        out = out.T.astype(jnp.bfloat16)
        for h in range(REP):
            o_ref[s, :, h * HEAD:(h + 1) * HEAD] = out[h * TILE:(h + 1) * TILE]

        def backward(c, dq):
            found = places(c)
            prob = st[c] * inv
            keys = jnp.concatenate([kv_ref[f & (TILES - 1), :, :HEAD] for f in found], axis=0)
            vals = jnp.concatenate([kv_ref[f & (TILES - 1), :, HEAD:] for f in found], axis=0)
            dprob = lax.dot_general(vals, g, (((1,), (1,)), ((), ())), preferred_element_type=jnp.float32)
            dscore = (prob * (dprob - delta)).astype(jnp.bfloat16)
            dq = dq + lax.dot_general(
                keys, dscore, (((0,), (0,)), ((), ())), preferred_element_type=jnp.float32)
            dk = jnp.dot(dscore, q, preferred_element_type=jnp.float32)
            dv = jnp.dot(prob.astype(jnp.bfloat16), g, preferred_element_type=jnp.float32)
            for j, f in enumerate(found):
                at = f & (TILES - 1)
                acc[at, :, :HEAD] += dk[j * TILE:(j + 1) * TILE]
                acc[at, :, HEAD:] += dv[j * TILE:(j + 1) * TILE]
            return dq

        dq = lax.fori_loop(0, chunks, backward, jnp.zeros((HEAD, ROWS), jnp.float32))
        dq = (dq * SCALE).T.astype(jnp.bfloat16)
        for h in range(REP):
            dq_ref[s, :, h * HEAD:(h + 1) * HEAD] = dq[h * TILE:(h + 1) * TILE]
        return carry

    lax.fori_loop(0, NZ, one_tile, 0)

    def finish(i, carry):
        dkv_ref[i, :, :HEAD] = (acc[i, :, :HEAD] * SCALE).astype(jnp.bfloat16)
        dkv_ref[i, :, HEAD:] = acc[i, :, HEAD:].astype(jnp.bfloat16)
        return carry

    lax.fori_loop(0, TILES, finish, 0, unroll=4)


def attention(codes, counts, own, ends, q, g, kv):
    smem = pl.BlockSpec(memory_space=pltpu.SMEM)
    vmem = pl.BlockSpec(memory_space=pltpu.VMEM)
    wide = jax.ShapeDtypeStruct((NZ, TILE, REP * HEAD), jnp.bfloat16)
    return pl.pallas_call(
        attend,
        out_shape=(wide, wide, jax.ShapeDtypeStruct((TILES, TILE, 2 * HEAD), jnp.bfloat16)),
        in_specs=[smem] * 4 + [vmem] * 3,
        out_specs=(vmem, vmem, vmem),
        scratch_shapes=[
            pltpu.VMEM((TILES, TILE, 2 * HEAD), jnp.float32),
            pltpu.VMEM((MOST_CHUNKS, CHUNK * TILE, ROWS), jnp.float32),
        ],
        compiler_params=pltpu.CompilerParams(vmem_limit_bytes=56 * 1024 * 1024),
        name="attend",
    )(codes, counts, own, ends, q, g, kv)


def exchange(blocks, axes):
    return lax.all_to_all(blocks, axes, split_axis=0, concat_axis=0, tiled=True)


def per_device(queries, keys, values, output_cotangent, tile_order, doc_lengths, read_peer, read_slot):
    order = lax.all_gather(tile_order, ("y", "z", "core"), axis=0, tiled=True)
    codes, counts, own, ends = plan(order, doc_lengths, read_peer[:, 0], read_slot)
    kv = jnp.concatenate(
        [keys.reshape(TILE, KV_HEADS, HEAD), values.reshape(TILE, KV_HEADS, HEAD)], axis=2)
    kv = exchange(kv.transpose(1, 0, 2), "z")
    kv = lax.all_gather(kv, ("x", "y", "core"), axis=0, tiled=True)
    q = exchange(queries.reshape(TILE, KV_HEADS, REP * HEAD).transpose(1, 0, 2), "z")
    g = exchange(output_cotangent.reshape(TILE, KV_HEADS, REP * HEAD).transpose(1, 0, 2), "z")
    out, dq, dkv = attention(codes, counts, own, ends, q, g, kv)
    dkv = exchange(dkv.reshape(NX * NY * NC, NZ * TILE, 2 * HEAD), ("x", "y", "core"))
    dkv = jnp.sum(dkv.astype(jnp.float32), axis=0).astype(jnp.bfloat16)
    dkv = exchange(dkv.reshape(NZ, TILE, 2 * HEAD), "z").transpose(1, 0, 2)
    out = exchange(out, "z").transpose(1, 0, 2).reshape(TILE, KV_HEADS * REP * HEAD)
    dq = exchange(dq, "z").transpose(1, 0, 2).reshape(TILE, KV_HEADS * REP * HEAD)
    return (
        out,
        dq,
        dkv[:, :, :HEAD].reshape(TILE, KV_HEADS * HEAD),
        dkv[:, :, HEAD:].reshape(TILE, KV_HEADS * HEAD),
    )


def solution(mesh):
    fine = Mesh(mesh.devices.reshape(NY, NZ, NC, NX), AXES)
    rows = P(AXES, None)
    return jax.shard_map(
        per_device,
        mesh=fine,
        in_specs=(rows, rows, rows, rows, P(("y", "z", "core")), P(), P(), P()),
        out_specs=(rows, rows, rows, rows),
        check_vma=False,
    )
```

time: 775 us -> 304 us (0.39); the launches traced: 762 us -> 304 us
  waiting for transfers between devices: 365 us -> 32.9 us
  blocking collectives: 0 us -> 180 us
  local copies, waits for them, and re-layouts: 159 us -> 15.8 us
  matrix products: 86 us -> 0 us
  other arithmetic: 83.7 us -> 10.4 us
  starting transfers between devices: 66.7 us -> 15.8 us
  Pallas kernels: 0 us -> 34 us
  between operations: 1.57 us -> 14.9 us
    all_to_all x11 -> x4, waiting for transfers between devices: 365 us -> 32.9 us  [exchange(): return lax.all_to_all(blocks, axes, split_axis=0, concat_axis=0, tiled=True)]
    all_to_all x0 -> x3, blocking collectives: none -> 158 us  [exchange(): return lax.all_to_all(blocks, axes, split_axis=0, concat_axis=0, tiled=True)]
    dot_general x26 -> x0, matrix products: 86 us -> none  [the longest x4 19 us: per_device(): jnp.einsum('qhd,kd->hqk', head_pair(local_q, pair_index), kv_head(all_kv,...]
    gather x7 -> x0, local copies, waits for them, and re-layouts: 67.7 us -> none  [the longest x3 26.8 us: read_table(): first_base = jnp.take_along_axis(base_rows, first_entry, axis=1)]
    all_to_all x11 -> x4, starting transfers between devices: 66.7 us -> 15.8 us  [exchange(): return lax.all_to_all(blocks, axes, split_axis=0, concat_axis=0, tiled=True)]
    pallas_call x0 -> x1, Pallas kernels: none -> 34 us  [attention(): pl.pallas_call(attend, out_shape=(wide, wide, jax.ShapeDtypeStruct((TILES...]
    sub x5 -> x0, other arithmetic: 33.5 us -> none  [the longest x4 33.5 us: per_device(): shifted = jnp.exp(scores - jnp.max(scores, axis=2, keepdims=True))]
    unnamed x63 -> x15, local copies, waits for them, and re-layouts: 36.7 us -> 5.34 us
  transfers between devices with their start and end apart: 11 -> 5, of which waited for: 9 -> 3; matrix products, arithmetic and copies ran while one was open for 12% -> 7% of each run, Pallas kernels for 0% -> 0%
where the time goes in v1:
time: 304 us
  blocking collectives  180 us (59%)
  Pallas kernels  34 us (11%)
  waiting for transfers between devices  32.9 us (11%)
  starting transfers between devices  15.8 us (5%)
  local copies, waits for them, and re-layouts  15.8 us (5%)
  between operations  14.9 us (5%)
  other arithmetic  10.4 us (3%)
    all_to_all x3, blocking collectives, exchange(): return lax.all_to_all(blocks, axes, split_axis=0, concat_axis=0, tiled=True)  158 us
    pallas_call x1, Pallas kernels, attention(): pl.pallas_call(attend, out_shape=(wide, wide, jax.ShapeDtypeStruct((TILES...  34 us
    all_to_all x4, waiting for transfers between devices, exchange(): return lax.all_to_all(blocks, axes, split_axis=0, concat_axis=0, tiled=True)  32.9 us
    unnamed x1, blocking collectives  22.3 us
    all_to_all x4, starting transfers between devices, exchange(): return lax.all_to_all(blocks, axes, split_axis=0, concat_axis=0, tiled=True)  15.8 us
  transfers between devices with their start and end apart: 5, of which 3 were waited for; matrix products, arithmetic and copies ran while one was open for 7% of the time, Pallas kernels for 0%

profile of v1, /device:TPU:6, one launch (start us, length us, event | category | flops | bytes accessed | tf_op | source)
XLA Modules:
  0.0 304.1 jit_solution(7009881304658277391)
XLA Ops:
  7.2 0.0 all-gather.2.cloned.1.call-start
  7.2 0.9 copy.73
  8.1 0.9 copy.74
  9.2 20.2 %all_to_all.35 = bf16[8,64,256]{2,1,0:T(8,128)(2,1)} all-to-all(bf16[8,64,256]{2,1,0:T(8,128)(2,1)S(1)} %copy.61), channel_id=1, replica_groups=mesh['y'=4,'z'=8,'core'=2,'x'=4] {'z'}, dimensions={0} | all-to-all | bytes 524288 | tf_op jit(solution)/shard_map/all_to_all | solution.py:175
  29.4 0.0 all-gather.2.cloned.1.call-update
  29.4 1.9 copy.80
  31.3 3.5 %all-to-all-start = ((bf16[8,64,512]{2,1,0:T(8,128)(2,1)}), bf16[8,64,512]{2,1,0:T(8,128)(2,1)S(1)}, u32[]{:S(2)}, u32[]{:S(2)}) async-start(bf16[8,64,512]{2,1,0:T(8,128)(2,1)} %bitcast.76), calls=%async_computation | async-start | bytes 1048576 | tf_op jit(solution)/shard_map/all_to_all | solution.py:175
  34.8 0.5 broadcast.184
  35.4 1.4 reduce.10
  36.8 0.1 reshape_squeeze.3
  36.8 1.3 dynamic-slice.7
  38.8 0.9 dynamic-update-slice
  39.6 22.3 %all-reduce = s32[256]{0:T(256)S(1)} all-reduce(s32[256]{0:T(256)S(1)} %dynamic-update-slice), channel_id=1, replica_groups=mesh['y'=4,'z'=8,'core'=2,'x'=4] {'y','z','core'}, use_global_device_ids=true, to_apply=%add | all-reduce | flops 256 | bytes 2048
  61.9 0.1 reshape.279
  62.1 0.8 reshape.278
  62.9 0.3 dynamic-slice_reduce_fusion.own
  63.2 0.0 copy-start.2
  63.3 0.2 select_reduce_fusion.1
  63.5 0.8 reduce-window.18
  64.3 0.0 copy-start.3
  64.3 0.1 copy.54
  64.4 0.1 copy.55
  64.5 0.1 sub.56
  64.6 0.1 sub.50
  64.7 0.1 select_reduce_fusion.2
  65.0 0.2 fusion.4
  65.1 0.1 copy.56
  65.2 0.6 reduce-window.19
  65.8 1.9 copy.79
  67.7 0.0 all-to-all-done.q_ref
  67.7 0.0 copy-start
  67.7 5.4 %all-to-all-start.1 = ((bf16[8,64,512]{2,1,0:T(8,128)(2,1)}), bf16[8,64,512]{2,1,0:T(8,128)(2,1)S(1)}, u32[]{:S(2)}, u32[]{:S(2)}) async-start(bf16[8,64,512]{2,1,0:T(8,128)(2,1)} %bitcast.74), calls=%async_computation.1 | async-start | bytes 1048576 | tf_op jit(solution)/shard_map/all_to_all | solution.py:175
  73.1 0.2 slice_reduce_fusion
  73.3 0.1 add_bitcast_fusion
  73.4 0.1 copy.57
  73.5 0.2 fusion.8
  73.7 0.1 copy.58
  73.8 1.3 select_reduce_fusion
  75.1 0.7 copy.62.codes
  75.8 0.7 slice_reduce_fusion.1.counts
  76.5 10.1 %all-to-all-done.1.g_ref = bf16[8,64,512]{2,1,0:T(8,128)(2,1)S(1)} async-done(((bf16[8,64,512]{2,1,0:T(8,128)(2,1)}), bf16[8,64,512]{2,1,0:T(8,128)(2,1)S(1)}, u32[]{:S(2)}, u32[]{:S(2)}) %all-to-all-start.1) | async-done | bytes 524320 | tf_op jit(solution)/shard_map/all_to_all | solution.py:175
  86.5 0.0 copy-start.1
  86.5 0.0 all-gather.2.cloned.1.call-done.kv_ref
  86.5 0.0 copy-done.2
  86.5 0.0 copy-done.3
  86.5 0.0 copy-done
  86.5 0.8 copy-done.1
  87.3 34.0 %attend.1 = (bf16[8,64,512]{2,1,0:T(8,128)(2,1)}, bf16[8,64,512]{2,1,0:T(8,128)(2,1)}, bf16[256,64,256]{2,1,0:T(8,128)(2,1)}) custom-call(s32[8,68]{1,0:T(8,128)} %copy.62.codes, s32[8]{0:T(128)} %slice_reduce_fusion.1.counts, s32[8]{0:T(128)} %copy-done.2, s32[4]{0:T(128)} %bitcast.106, bf16[8,64,512]{2,1,0:T(8,128)(2,1)} %copy-done, ...), custom_call_target="tpu_custom_call" | custom-call | tf_op jit(solution)/shard_map/attend/pallas_call | solution.py:160
  121.3 21.5 %all_to_all.36 = bf16[8,64,512]{2,1,0:T(8,128)(2,1)S(1)} all-to-all(bf16[8,64,512]{2,1,0:T(8,128)(2,1)} %get-tuple-element.7), channel_id=1, replica_groups=mesh['y'=4,'z'=8,'core'=2,'x'=4] {'z'}, dimensions={0} | all-to-all | bytes 1048576 | tf_op jit(solution)/shard_map/all_to_all | solution.py:175
  142.9 116.1 %all_to_all.37 = bf16[32,512,256]{2,1,0:T(8,128)(2,1)} all-to-all(bf16[32,512,256]{2,1,0:T(8,128)(2,1)} %bitcast.82), channel_id=1, replica_groups=mesh['y'=4,'z'=8,'core'=2,'x'=4] {'x','y','core'}, dimensions={0} | all-to-all | bytes 16777216 | tf_op jit(solution)/shard_map/all_to_all | solution.py:175
  258.9 3.5 %all-to-all-start.4 = ((bf16[8,64,512]{2,1,0:T(8,128)(2,1)}), bf16[8,64,512]{2,1,0:T(8,128)(2,1)S(1)}, u32[]{:S(2)}, u32[]{:S(2)}) async-start(bf16[8,64,512]{2,1,0:T(8,128)(2,1)} %get-tuple-element.8), calls=%async_computation.4 | async-start | bytes 1048576 | tf_op jit(solution)/shard_map/all_to_all | solution.py:175
  262.4 5.5 %reduce_sum.32 = bf16[512,256]{1,0:T(8,128)(2,1)} reduce(bf16[32,512,256]{2,1,0:T(8,128)(2,1)} %all_to_all.37, bf16[]{:T(256)} %constant.222.clone.1), dimensions={0}, to_apply=%region_7.8 | reduce | flops 4063232 | bytes 8650754 | tf_op jit(solution)/shard_map/reduce_sum | solution.py:189
  267.9 12.3 %all-to-all-done.4 = bf16[8,64,512]{2,1,0:T(8,128)(2,1)S(1)} async-done(((bf16[8,64,512]{2,1,0:T(8,128)(2,1)}), bf16[8,64,512]{2,1,0:T(8,128)(2,1)S(1)}, u32[]{:S(2)}, u32[]{:S(2)}) %all-to-all-start.4) | async-done | bytes 524320 | tf_op jit(solution)/shard_map/all_to_all | solution.py:175
  280.1 3.4 %all-to-all-start.6 = ((bf16[8,64,256]{2,1,0:T(8,128)(2,1)}), bf16[8,64,256]{2,1,0:T(8,128)(2,1)S(1)}, u32[]{:S(2)}, u32[]{:S(2)}) async-start(bf16[8,64,256]{2,1,0:T(8,128)(2,1)} %bitcast.20), calls=%async_computation.6 | async-start | bytes 524288 | tf_op jit(solution)/shard_map/all_to_all | solution.py:175
  283.6 0.8 copy.69
  284.4 0.8 copy.70
  285.2 10.6 %all-to-all-done.6 = bf16[8,64,256]{2,1,0:T(8,128)(2,1)S(1)} async-done(((bf16[8,64,256]{2,1,0:T(8,128)(2,1)}), bf16[8,64,256]{2,1,0:T(8,128)(2,1)S(1)}, u32[]{:S(2)}, u32[]{:S(2)}) %all-to-all-start.6) | async-done | bytes 262176 | tf_op jit(solution)/shard_map/all_to_all | solution.py:175
  295.8 0.1 slice_bitcast_fusion
  295.9 0.7 copy.81
  296.6 0.7 copy.82
  (18 shorter events, 0.3 us)
Async XLA Ops:
  7.2 79.4 %all-gather.2.cloned.1.call-start = ((), (), s32[]{:S(2)}) async-start(), calls=%async_computation.7 | async-start | bytes 8650752 | tf_op jit(solution)/shard_map/all_gather | solution.py:184
  31.3 36.3 %all-to-all-start = ((bf16[8,64,512]{2,1,0:T(8,128)(2,1)}), bf16[8,64,512]{2,1,0:T(8,128)(2,1)S(1)}, u32[]{:S(2)}, u32[]{:S(2)}) async-start(bf16[8,64,512]{2,1,0:T(8,128)(2,1)} %bitcast.76), calls=%async_computation | async-start | bytes 1048576 | tf_op jit(solution)/shard_map/all_to_all | solution.py:175
  63.2 23.3 %copy-start.2 = (s32[8]{0:T(128)}, s32[8]{0:T(128)S(1)}, u32[]{:S(2)}) copy-start(s32[8]{0:T(128)S(1)} %dynamic-slice_reduce_fusion.own) | copy-start | bytes 100
  64.3 22.2 %copy-start.3 = (s32[4,1]{0,1:T(1,128)}, s32[4,1]{0,1:T(1,128)S(1)}, u32[]{:S(2)}) copy-start(s32[4,1]{0,1:T(1,128)S(1)} %reduce-window.18) | copy-start | bytes 52
  67.7 18.9 %copy-start = (bf16[8,64,512]{2,1,0:T(8,128)(2,1)}, bf16[8,64,512]{2,1,0:T(8,128)(2,1)S(1)}, u32[]{:S(2)}) copy-start(bf16[8,64,512]{2,1,0:T(8,128)(2,1)S(1)} %all-to-all-done.q_ref) | copy-start | bytes 1572868
  67.7 18.9 %all-to-all-start.1 = ((bf16[8,64,512]{2,1,0:T(8,128)(2,1)}), bf16[8,64,512]{2,1,0:T(8,128)(2,1)S(1)}, u32[]{:S(2)}, u32[]{:S(2)}) async-start(bf16[8,64,512]{2,1,0:T(8,128)(2,1)} %bitcast.74), calls=%async_computation.1 | async-start | bytes 1048576 | tf_op jit(solution)/shard_map/all_to_all | solution.py:175
  86.5 0.8 copy-start.1
  258.9 21.2 %all-to-all-start.4 = ((bf16[8,64,512]{2,1,0:T(8,128)(2,1)}), bf16[8,64,512]{2,1,0:T(8,128)(2,1)S(1)}, u32[]{:S(2)}, u32[]{:S(2)}) async-start(bf16[8,64,512]{2,1,0:T(8,128)(2,1)} %get-tuple-element.8), calls=%async_computation.4 | async-start | bytes 1048576 | tf_op jit(solution)/shard_map/all_to_all | solution.py:175
  280.1 15.7 %all-to-all-start.6 = ((bf16[8,64,256]{2,1,0:T(8,128)(2,1)}), bf16[8,64,256]{2,1,0:T(8,128)(2,1)S(1)}, u32[]{:S(2)}, u32[]{:S(2)}) async-start(bf16[8,64,256]{2,1,0:T(8,128)(2,1)} %bitcast.20), calls=%async_computation.6 | async-start | bytes 524288 | tf_op jit(solution)/shard_map/all_to_all | solution.py:175
Sparse Core Ops, SparseCore 0:
  29.6 54.1 all-gather.1

commit v2 on v1

--- a/solution.py
+++ b/solution.py
@@ -58,13 +58,16 @@
     t = jnp.arange(TILES, dtype=jnp.int32)
     tx, tc, tz, ty = t % 4, (t // 4) % 2, (t // 8) % 8, t // 64
     place = ((tx * NY + ty) * NC + tc) * NZ + tz
-    code = place + TILES * (tile_order + 1)
+    dx, dy, half = (tx - x) & 3, (ty - y) & 3, tz // 4
+    hops, hops2 = jnp.where(half == 0, dx, dy), jnp.where(half == 0, dy, dx)
+    goal = ((((tc ^ core) * 2 + half) * 4 + hops) * 2 + (tz // 2) % 2) * 8 + hops2 * 2 + tz % 2
+    code = place + TILES * goal + TILES * TILES * (tile_order + 1)
     wanted = jnp.where(need, rank, 0)[:, :, None] == 1 + jnp.arange(MOST_TILES, dtype=jnp.int32)
     codes = jnp.sum(jnp.where(wanted, code[None, :, None], 0), axis=1)
     return codes, rank[:, -1], own, ends
 
 
-def attend(codes, counts, own, ends, q_ref, g_ref, kv_ref, o_ref, dq_ref, dkv_ref, acc, st):
+def attend(codes, counts, own, ends, q_ref, g_ref, kv_ref, o_ref, dq_ref, near_ref, far_ref, acc, st):
     acc[...] = jnp.zeros_like(acc)
     key_at = lax.broadcasted_iota(jnp.int32, (TILE, ROWS), 0)
     lane = lax.broadcasted_iota(jnp.int32, (1, ROWS), 1) & (TILE - 1)
@@ -89,7 +92,7 @@
             keys = jnp.concatenate([kv_ref[f & (TILES - 1), :, :HEAD] for f in found], axis=0)
             raw = lax.dot_general(keys, q, (((1,), (1,)), ((), ())), preferred_element_type=jnp.float32)
             for j, f in enumerate(found):
-                base = (f // TILES - 1) * TILE
+                base = (f // (TILES * TILES) - 1) * TILE
                 part = raw[j * TILE:(j + 1) * TILE]
                 part = jnp.where((key_at <= q_pos - base) & (key_at >= low - base), part, NEG)
                 st[c, j * TILE:(j + 1) * TILE, :] = part
@@ -132,7 +135,7 @@
             dk = jnp.dot(dscore, q, preferred_element_type=jnp.float32)
             dv = jnp.dot(prob.astype(jnp.bfloat16), g, preferred_element_type=jnp.float32)
             for j, f in enumerate(found):
-                at = f & (TILES - 1)
+                at = (f // TILES) & (TILES - 1)
                 acc[at, :, :HEAD] += dk[j * TILE:(j + 1) * TILE]
                 acc[at, :, HEAD:] += dv[j * TILE:(j + 1) * TILE]
             return dq
@@ -146,22 +149,24 @@
     lax.fori_loop(0, NZ, one_tile, 0)
 
     def finish(i, carry):
-        dkv_ref[i, :, :HEAD] = (acc[i, :, :HEAD] * SCALE).astype(jnp.bfloat16)
-        dkv_ref[i, :, HEAD:] = acc[i, :, HEAD:].astype(jnp.bfloat16)
+        for ref, at in ((near_ref, i), (far_ref, i + TILES // 2)):
+            ref[i, :, :HEAD] = (acc[at, :, :HEAD] * SCALE).astype(jnp.bfloat16)
+            ref[i, :, HEAD:] = acc[at, :, HEAD:].astype(jnp.bfloat16)
         return carry
 
-    lax.fori_loop(0, TILES, finish, 0, unroll=4)
+    lax.fori_loop(0, TILES // 2, finish, 0, unroll=2)
 
 
 def attention(codes, counts, own, ends, q, g, kv):
     smem = pl.BlockSpec(memory_space=pltpu.SMEM)
     vmem = pl.BlockSpec(memory_space=pltpu.VMEM)
     wide = jax.ShapeDtypeStruct((NZ, TILE, REP * HEAD), jnp.bfloat16)
+    part = jax.ShapeDtypeStruct((TILES // 2, TILE, 2 * HEAD), jnp.bfloat16)
     return pl.pallas_call(
         attend,
-        out_shape=(wide, wide, jax.ShapeDtypeStruct((TILES, TILE, 2 * HEAD), jnp.bfloat16)),
+        out_shape=(wide, wide, part, part),
         in_specs=[smem] * 4 + [vmem] * 3,
-        out_specs=(vmem, vmem, vmem),
+        out_specs=(vmem, vmem, vmem, vmem),
         scratch_shapes=[
             pltpu.VMEM((TILES, TILE, 2 * HEAD), jnp.float32),
             pltpu.VMEM((MOST_CHUNKS, CHUNK * TILE, ROWS), jnp.float32),
@@ -173,6 +178,39 @@
 
 def exchange(blocks, axes):
     return lax.all_to_all(blocks, axes, split_axis=0, concat_axis=0, tiled=True)
+
+
+def shift(array, axis, by):
+    size = lax.axis_size(axis)
+    return lax.ppermute(array, axis, [(i, (i + by) % size) for i in range(size)])
+
+
+def added(*arrays):
+    return sum(a.astype(jnp.float32) for a in arrays).astype(jnp.bfloat16)
+
+
+def summed_at_owner(near, far):
+    total = added(near, shift(far, "core", 1))
+    ways = (("x", "y"), ("y", "x"))
+    sent = []
+    for half, (axis, _) in enumerate(ways):
+        t = total[half]
+        up = shift(jnp.stack([t[2, 0], t[1, 1]]), axis, 1)
+        down = shift(jnp.stack([t[2, 1], t[3, 0]]), axis, -1)
+        sent.append((up, down))
+    passed = []
+    for half, (axis, _) in enumerate(ways):
+        t, (up, down) = total[half], sent[half]
+        passed.append((shift(added(t[1, 0], up[0]), axis, 1), shift(added(t[3, 1], down[0]), axis, -1)))
+    rows = []
+    for half in range(2):
+        t, (up, down), (from_low, from_high) = total[half], sent[half], passed[half]
+        rows.append(jnp.stack([added(t[0, 0], from_low, down[1]), added(t[0, 1], from_high, up[1])]))
+    parts = []
+    for (_, axis), row in zip(ways, rows):
+        parts.append(added(
+            row[:, 0], shift(row[:, 1], axis, 1), shift(row[:, 2], axis, 2), shift(row[:, 3], axis, -1)))
+    return jnp.stack(parts).reshape(NZ, TILE, 2 * HEAD)
 
 
 def per_device(queries, keys, values, output_cotangent, tile_order, doc_lengths, read_peer, read_slot):
@@ -184,10 +222,10 @@
     kv = lax.all_gather(kv, ("x", "y", "core"), axis=0, tiled=True)
     q = exchange(queries.reshape(TILE, KV_HEADS, REP * HEAD).transpose(1, 0, 2), "z")
     g = exchange(output_cotangent.reshape(TILE, KV_HEADS, REP * HEAD).transpose(1, 0, 2), "z")
-    out, dq, dkv = attention(codes, counts, own, ends, q, g, kv)
-    dkv = exchange(dkv.reshape(NX * NY * NC, NZ * TILE, 2 * HEAD), ("x", "y", "core"))
-    dkv = jnp.sum(dkv.astype(jnp.float32), axis=0).astype(jnp.bfloat16)
-    dkv = exchange(dkv.reshape(NZ, TILE, 2 * HEAD), "z").transpose(1, 0, 2)
+    out, dq, near, far = attention(codes, counts, own, ends, q, g, kv)
+    pieces = (2, 4, 2, 4, 2, TILE, 2 * HEAD)
+    dkv = summed_at_owner(near.reshape(pieces), far.reshape(pieces))
+    dkv = exchange(dkv, "z").transpose(1, 0, 2)
     out = exchange(out, "z").transpose(1, 0, 2).reshape(TILE, KV_HEADS * REP * HEAD)
     dq = exchange(dq, "z").transpose(1, 0, 2).reshape(TILE, KV_HEADS * REP * HEAD)
     return (

time: 304 us -> 232 us (0.76)
  blocking collectives: 180 us -> 44.5 us
  starting transfers between devices: 15.8 us -> 59.7 us
  waiting for transfers between devices: 32.9 us -> 46.9 us
  other arithmetic: 10.4 us -> 19.7 us
    all_to_all x3 -> x1, blocking collectives: 158 us -> 20.2 us  [exchange(): return lax.all_to_all(blocks, axes, split_axis=0, concat_axis=0, tiled=True)]
    ppermute x0 -> x15, starting transfers between devices: none -> 33.3 us  [shift(): lax.ppermute(array, axis, [(i, (i + by) % size) for i in range(size)])]
    ppermute x0 -> x15, waiting for transfers between devices: none -> 24.9 us  [shift(): lax.ppermute(array, axis, [(i, (i + by) % size) for i in range(size)])]
    all_to_all x4 -> x5, waiting for transfers between devices: 32.9 us -> 21.9 us  [exchange(): return lax.all_to_all(blocks, axes, split_axis=0, concat_axis=0, tiled=True)]
    all_to_all x4 -> x5, starting transfers between devices: 15.8 us -> 26.3 us  [exchange(): return lax.all_to_all(blocks, axes, split_axis=0, concat_axis=0, tiled=True)]
    another operation x4 -> x15, other arithmetic: 1.51 us -> 11 us  [the longest x4 5.41 us: summed_at_owner(): jnp.stack([added(t[0, 0], from_low, down[1]), added(t[0, 1], from_high, u...]
    reduce_sum x1 -> x0, other arithmetic: 5.46 us -> none  [per_device(): dkv = jnp.sum(dkv.astype(jnp.float32), axis=0).astype(jnp.bfloat16)]
    convert_element_type x0 -> x3, other arithmetic: none -> 5.18 us  [added(): return sum((a.astype(jnp.float32) for a in arrays)).astype(jnp.bfloat16)]
  transfers between devices with their start and end apart: 5 -> 21, of which waited for: 3 -> 9; matrix products, arithmetic and copies ran while one was open for 7% -> 11% of each run, Pallas kernels for 0% -> 0%
where the time goes in v2:
time: 232 us; the launch traced here: 234 us
  starting transfers between devices  59.7 us (26%)
  waiting for transfers between devices  46.9 us (20%)
  blocking collectives  44.5 us (19%)
  Pallas kernels  33.1 us (14%)
  other arithmetic  19.7 us (8%)
  local copies, waits for them, and re-layouts  15.3 us (7%)
  between operations  15.2 us (7%)
    ppermute x15, starting transfers between devices, shift(): lax.ppermute(array, axis, [(i, (i + by) % size) for i in range(size)])  33.3 us
    pallas_call x1, Pallas kernels, attention(): pl.pallas_call(attend, out_shape=(wide, wide, part, part), in_specs=[smem...  33.1 us
    all_to_all x5, starting transfers between devices, exchange(): return lax.all_to_all(blocks, axes, split_axis=0, concat_axis=0, tiled=True)  26.3 us
    ppermute x15, waiting for transfers between devices, shift(): lax.ppermute(array, axis, [(i, (i + by) % size) for i in range(size)])  24.9 us
    unnamed x1, blocking collectives  24.3 us
    all_to_all x5, waiting for transfers between devices, exchange(): return lax.all_to_all(blocks, axes, split_axis=0, concat_axis=0, tiled=True)  21.9 us
    all_to_all x1, blocking collectives, exchange(): return lax.all_to_all(blocks, axes, split_axis=0, concat_axis=0, tiled=True)  20.2 us
    another operation x4, other arithmetic, summed_at_owner(): jnp.stack([added(t[0, 0], from_low, down[1]), added(t[0, 1], from_high, u...  5.41 us
  transfers between devices with their start and end apart: 21, of which 9 were waited for; matrix products, arithmetic and copies ran while one was open for 11% of the time, Pallas kernels for 0%

profile of v2, /device:TPU:6, one launch (start us, length us, event | category | flops | bytes accessed | tf_op | source)
XLA Modules:
  0.0 234.5 jit_solution(6898125633158048658)
XLA Ops:
  7.3 1.0 copy.113
  8.3 0.9 copy.114
  9.3 20.2 %all_to_all.30 = bf16[8,64,256]{2,1,0:T(8,128)(2,1)} all-to-all(bf16[8,64,256]{2,1,0:T(8,128)(2,1)S(1)} %copy.94), channel_id=1, replica_groups=mesh['y'=4,'z'=8,'core'=2,'x'=4] {'z'}, dimensions={0} | all-to-all | bytes 524288 | tf_op jit(solution)/shard_map/all_to_all | solution.py:180
  29.6 1.9 copy.120
  31.5 3.5 %all-to-all-start = ((bf16[8,64,512]{2,1,0:T(8,128)(2,1)}), bf16[8,64,512]{2,1,0:T(8,128)(2,1)S(1)}, u32[]{:S(2)}, u32[]{:S(2)}) async-start(bf16[8,64,512]{2,1,0:T(8,128)(2,1)} %bitcast.220), calls=%async_computation | async-start | bytes 1048576 | tf_op jit(solution)/shard_map/all_to_all | solution.py:180
  35.0 0.5 broadcast.213
  35.5 0.7 reduce.9
  36.3 0.6 dynamic-slice.7
  37.6 0.2 dynamic-update-slice
  37.8 24.3 %all-reduce = s32[256]{0:T(256)S(1)} all-reduce(s32[256]{0:T(256)S(1)} %dynamic-update-slice), channel_id=1, replica_groups=mesh['y'=4,'z'=8,'core'=2,'x'=4] {'y','z','core'}, use_global_device_ids=true, to_apply=%add | all-reduce | flops 256 | bytes 2048
  62.4 0.3 dynamic-slice_reduce_fusion.own
  62.7 0.2 select_reduce_fusion.1
  63.0 0.2 reduce-window.18
  64.0 0.6 reduce-window.19
  64.6 0.8 copy.119
  65.5 5.5 %all-to-all-start.1 = ((bf16[8,64,512]{2,1,0:T(8,128)(2,1)}), bf16[8,64,512]{2,1,0:T(8,128)(2,1)S(1)}, u32[]{:S(2)}, u32[]{:S(2)}) async-start(bf16[8,64,512]{2,1,0:T(8,128)(2,1)} %bitcast.218), calls=%async_computation.1 | async-start | bytes 1048576 | tf_op jit(solution)/shard_map/all_to_all | solution.py:180
  71.0 0.2 slice_reduce_fusion
  71.4 0.2 fusion.43
  71.7 1.3 select_reduce_fusion
  73.0 0.7 copy.95.codes
  73.7 0.7 slice_reduce_fusion.1.counts
  74.4 9.9 %all-to-all-done.1.g_ref = bf16[8,64,512]{2,1,0:T(8,128)(2,1)S(1)} async-done(((bf16[8,64,512]{2,1,0:T(8,128)(2,1)}), bf16[8,64,512]{2,1,0:T(8,128)(2,1)S(1)}, u32[]{:S(2)}, u32[]{:S(2)}) %all-to-all-start.1) | async-done | bytes 524320 | tf_op jit(solution)/shard_map/all_to_all | solution.py:180
  84.3 0.8 copy-done.2
  85.0 33.1 %attend.1 = (bf16[8,64,512]{2,1,0:T(8,128)(2,1)}, bf16[8,64,512]{2,1,0:T(8,128)(2,1)}, bf16[128,64,256]{2,1,0:T(8,128)(2,1)}, bf16[128,64,256]{2,1,0:T(8,128)(2,1)}) custom-call(s32[8,68]{1,0:T(8,128)} %copy.95.codes, s32[8]{0:T(128)} %slice_reduce_fusion.1.counts, s32[8]{0:T(128)} %copy-done.8, s32[4]{0:T(128)} %bitcast.249, bf16[8,64,512]{2,1,0:T(8,128)(2,1)} %copy-done.1, ...), custom_call_target="tpu_custom_call" | custom-call | tf_op jit(solution)/shard_map/attend/pallas_call | solution.py:165
  118.2 19.4 %collective-permute-start = (bf16[2,4,2,4,2,64,256]{6,5,4,3,2,1,0:T(8,128)(2,1)}, bf16[2,4,2,4,2,64,256]{6,5,4,3,2,1,0:T(8,128)(2,1)S(1)}, u32[]{:S(2)}, u32[]{:S(2)}) collective-permute-start(bf16[2,4,2,4,2,64,256]{6,5,4,3,2,1,0:T(8,128)(2,1)} %bitcast.250), channel_id=1, source_target_pairs={{0,4},{4,0},{1,5},{5,1},{2,6},{6,2},{3,7},{7,3},{8,12},{12,8},{9,1... | collective-permute-start | bytes 12582920 | tf_op jit(solution)/shard_map/ppermute | solution.py:185
  137.6 7.0 %collective-permute-done = bf16[2,4,2,4,2,64,256]{6,5,4,3,2,1,0:T(8,128)(2,1)S(1)} collective-permute-done((bf16[2,4,2,4,2,64,256]{6,5,4,3,2,1,0:T(8,128)(2,1)}, bf16[2,4,2,4,2,64,256]{6,5,4,3,2,1,0:T(8,128)(2,1)S(1)}, u32[]{:S(2)}, u32[]{:S(2)}) %collective-permute-start) | collective-permute-done | bytes 4194336 | tf_op jit(solution)/shard_map/ppermute | solution.py:185
  144.6 4.0 %fusion = bf16[2,4,2,4,2,64,256]{6,5,4,3,2,1,0:T(8,128)(2,1)S(1)} fusion(bf16[2,4,2,4,2,64,256]{6,5,4,3,2,1,0:T(8,128)(2,1)} %bitcast.226, bf16[2,4,2,4,2,64,256]{6,5,4,3,2,1,0:T(8,128)(2,1)S(1)} %collective-permute-done), kind=kLoop, calls=%fused_computation.1 | loop fusion | flops 8388608 | bytes 12582912 | tf_op jit(solution)/shard_map/convert_element_type | solution.py:189
  148.6 0.4 slice_bitcast_fusion.1
  149.4 1.1 pad_maximum_fusion.2
  150.6 0.9 pad_maximum_fusion.1
  151.4 1.7 collective-permute-start.3
  153.2 0.8 pad_maximum_fusion.3
  154.0 3.2 %collective-permute-start.10 = (bf16[2,4,2,64,256]{4,3,2,1,0:T(8,128)(2,1)}, bf16[2,4,2,64,256]{4,3,2,1,0:T(8,128)(2,1)}, u32[]{:S(2)}, u32[]{:S(2)}) collective-permute-start(bf16[2,4,2,64,256]{4,3,2,1,0:T(8,128)(2,1)} %pad_maximum_fusion.3), channel_id=1, source_target_pairs={{0,192},{64,0},{128,64},{192,128},{1,193},{65,1},{129,65},{193,129... | collective-permute-start | bytes 1572872 | tf_op jit(solution)/shard_map/ppermute | solution.py:185
  157.2 6.3 %collective-permute-done.1 = bf16[2,4,2,64,256]{4,3,2,1,0:T(8,128)(2,1)S(1)} collective-permute-done((bf16[2,4,2,64,256]{4,3,2,1,0:T(8,128)(2,1)S(1)}, bf16[2,4,2,64,256]{4,3,2,1,0:T(8,128)(2,1)S(1)}, u32[]{:S(2)}, u32[]{:S(2)}) %collective-permute-start.1) | collective-permute-done | bytes 524320 | tf_op jit(solution)/shard_map/ppermute | solution.py:185
  163.6 0.7 copy-done.4
  164.3 1.5 collective-permute-start.2
  165.8 7.0 %all-to-all-start.3 = ((bf16[8,64,512]{2,1,0:T(8,128)(2,1)}), bf16[8,64,512]{2,1,0:T(8,128)(2,1)S(1)}, u32[]{:S(2)}, u32[]{:S(2)}) async-start(bf16[8,64,512]{2,1,0:T(8,128)(2,1)} %get-tuple-element.8), calls=%async_computation.3 | async-start | bytes 1048576 | tf_op jit(solution)/shard_map/all_to_all | solution.py:180
  172.9 1.1 fusion.4
  174.0 1.3 fusion.9
  175.4 0.6 collective-permute-start.4
  176.0 6.7 %collective-permute-done.9 = bf16[4,2,64,256]{3,2,1,0:T(8,128)(2,1)S(1)} collective-permute-done((bf16[4,2,64,256]{3,2,1,0:T(8,128)(2,1)S(1)}, bf16[4,2,64,256]{3,2,1,0:T(8,128)(2,1)S(1)}, u32[]{:S(2)}, u32[]{:S(2)}) %collective-permute-start.9) | collective-permute-done | bytes 262176 | tf_op jit(solution)/shard_map/ppermute | solution.py:185
  182.7 1.9 fusion.11
  184.6 1.1 fusion.10
  185.7 0.7 fusion.32
  186.4 2.0 collective-permute-start.5
  188.4 1.2 collective-permute-start.7
  189.6 0.9 collective-permute-start.6
  190.5 6.9 %all-to-all-start.4 = ((bf16[8,64,512]{2,1,0:T(8,128)(2,1)}), bf16[8,64,512]{2,1,0:T(8,128)(2,1)}, u32[]{:S(2)}, u32[]{:S(2)}) async-start(bf16[8,64,512]{2,1,0:T(8,128)(2,1)} %get-tuple-element.9), calls=%async_computation.4 | async-start | bytes 1048576 | tf_op jit(solution)/shard_map/all_to_all | solution.py:180
  197.4 1.1 fusion.12
  198.6 0.4 collective-permute-start.12
  199.0 1.7 collective-permute-start.14
  200.7 0.4 collective-permute-start.13
  201.2 1.1 fusion.19
  202.3 1.4 collective-permute-done.12
  203.6 1.5 collective-permute-done.14
  205.1 2.0 collective-permute-done.13
  207.3 0.7 pad_maximum_fusion.4
  208.0 4.4 %all-to-all-done.4 = bf16[8,64,512]{2,1,0:T(8,128)(2,1)} async-done(((bf16[8,64,512]{2,1,0:T(8,128)(2,1)}), bf16[8,64,512]{2,1,0:T(8,128)(2,1)}, u32[]{:S(2)}, u32[]{:S(2)}) %all-to-all-start.4) | async-done | bytes 524320 | tf_op jit(solution)/shard_map/all_to_all | solution.py:180
  212.4 3.4 %all-to-all-start.5 = ((bf16[8,64,256]{2,1,0:T(8,128)(2,1)}), bf16[8,64,256]{2,1,0:T(8,128)(2,1)S(1)}, u32[]{:S(2)}, u32[]{:S(2)}) async-start(bf16[8,64,256]{2,1,0:T(8,128)(2,1)} %bitcast.62), calls=%async_computation.5 | async-start | bytes 524288 | tf_op jit(solution)/shard_map/all_to_all | solution.py:180
  215.8 0.8 copy.109
  216.6 1.9 copy.110
  218.5 7.7 %all-to-all-done.5 = bf16[8,64,256]{2,1,0:T(8,128)(2,1)S(1)} async-done(((bf16[8,64,256]{2,1,0:T(8,128)(2,1)}), bf16[8,64,256]{2,1,0:T(8,128)(2,1)S(1)}, u32[]{:S(2)}, u32[]{:S(2)}) %all-to-all-start.5) | async-done | bytes 262176 | tf_op jit(solution)/shard_map/all_to_all | solution.py:180
  226.3 0.7 copy.121
  226.9 0.7 copy.122
  (80 shorter events, 2.3 us)
Async XLA Ops:
  7.2 29.2 %copy-start.12 = (u32[256]{0:T(256)S(1)}, u32[256]{0:T(256)}, u32[]{:S(2)}) copy-start(u32[256]{0:T(256)} %constant.256) | copy-start | bytes 3076
  7.2 28.4 %copy-start.7 = (s32[4096,1]{0,1:T(1,128)S(1)}, s32[4096,1]{0,1:T(1,128)}, u32[]{:S(2)}) copy-start(s32[4096,1]{0,1:T(1,128)} %param.14) | copy-start | bytes 49156
  7.2 30.4 %copy-start.10 = (s32[4]{0:T(128)S(1)}, s32[4]{0:T(128)}, u32[]{:S(2)}) copy-start(s32[4]{0:T(128)} %param.12) | copy-start | bytes 52
  7.2 55.1 %copy-start.6 = (s32[4096]{0:T(1024)S(1)}, s32[4096]{0:T(1024)}, u32[]{:S(2)}) copy-start(s32[4096]{0:T(1024)} %param.15) | copy-start | bytes 49156
  7.2 55.8 %copy-start.11 = (s32[4]{0:T(128)S(1)}, s32[4]{0:T(128)}, u32[]{:S(2)}) copy-start(s32[4]{0:T(128)} %param.13) | copy-start | bytes 52
  7.2 57.4 %copy-start.3 = (bf16[64,4096]{1,0:T(8,128)(2,1)S(1)}, bf16[64,4096]{1,0:T(8,128)(2,1)}, u32[]{:S(2)}) copy-start(bf16[64,4096]{1,0:T(8,128)(2,1)} %param.11) | copy-start | bytes 1572868
  7.2 77.0 %all-gather.2.cloned.1.call-start = ((), (), s32[]{:S(2)}) async-start(), calls=%async_computation.6 | async-start | bytes 8650752 | tf_op jit(solution)/shard_map/all_gather | solution.py:222
  31.5 34.0 %all-to-all-start = ((bf16[8,64,512]{2,1,0:T(8,128)(2,1)}), bf16[8,64,512]{2,1,0:T(8,128)(2,1)S(1)}, u32[]{:S(2)}, u32[]{:S(2)}) async-start(bf16[8,64,512]{2,1,0:T(8,128)(2,1)} %bitcast.220), calls=%async_computation | async-start | bytes 1048576 | tf_op jit(solution)/shard_map/all_to_all | solution.py:180
  62.7 21.6 %copy-start.8 = (s32[8]{0:T(128)}, s32[8]{0:T(128)S(1)}, u32[]{:S(2)}) copy-start(s32[8]{0:T(128)S(1)} %dynamic-slice_reduce_fusion.own) | copy-start | bytes 100
  63.2 21.1 %copy-start.9 = (s32[4,1]{0,1:T(1,128)}, s32[4,1]{0,1:T(1,128)S(1)}, u32[]{:S(2)}) copy-start(s32[4,1]{0,1:T(1,128)S(1)} %reduce-window.18) | copy-start | bytes 52
  65.5 18.8 %copy-start.1 = (bf16[8,64,512]{2,1,0:T(8,128)(2,1)}, bf16[8,64,512]{2,1,0:T(8,128)(2,1)S(1)}, u32[]{:S(2)}) copy-start(bf16[8,64,512]{2,1,0:T(8,128)(2,1)S(1)} %all-to-all-done.q_ref) | copy-start | bytes 1572868
  65.5 18.8 %all-to-all-start.1 = ((bf16[8,64,512]{2,1,0:T(8,128)(2,1)}), bf16[8,64,512]{2,1,0:T(8,128)(2,1)S(1)}, u32[]{:S(2)}, u32[]{:S(2)}) async-start(bf16[8,64,512]{2,1,0:T(8,128)(2,1)} %bitcast.218), calls=%async_computation.1 | async-start | bytes 1048576 | tf_op jit(solution)/shard_map/all_to_all | solution.py:180
  84.2 0.8 copy-start.2
  118.2 26.4 %collective-permute-start = (bf16[2,4,2,4,2,64,256]{6,5,4,3,2,1,0:T(8,128)(2,1)}, bf16[2,4,2,4,2,64,256]{6,5,4,3,2,1,0:T(8,128)(2,1)S(1)}, u32[]{:S(2)}, u32[]{:S(2)}) collective-permute-start(bf16[2,4,2,4,2,64,256]{6,5,4,3,2,1,0:T(8,128)(2,1)} %bitcast.250), channel_id=1, source_target_pairs={{0,4},{4,0},{1,5},{5,1},{2,6},{6,2},{3,7},{7,3},{8,12},{12,8},{9,1... | collective-permute-start | bytes 12582920 | tf_op jit(solution)/shard_map/ppermute | solution.py:185
  149.1 14.5 %copy-start = (bf16[4,2,4,2,64,256]{5,4,3,2,1,0:T(8,128)(2,1)}, bf16[4,2,4,2,64,256]{5,4,3,2,1,0:T(8,128)(2,1)S(1)}, u32[]{:S(2)}) copy-start(bf16[4,2,4,2,64,256]{5,4,3,2,1,0:T(8,128)(2,1)S(1)} %get-tuple-element.14) | copy-start | bytes 6291460
  149.2 14.3 %collective-permute-start.1 = (bf16[2,4,2,64,256]{4,3,2,1,0:T(8,128)(2,1)S(1)}, bf16[2,4,2,64,256]{4,3,2,1,0:T(8,128)(2,1)S(1)}, u32[]{:S(2)}, u32[]{:S(2)}) collective-permute-start(bf16[2,4,2,64,256]{4,3,2,1,0:T(8,128)(2,1)S(1)} %pad_maximum_fusion), channel_id=1, source_target_pairs={{0,1},{1,2},{2,3},{3,0},{4,5},{5,6},{6,7},{7,4},{8,9},{9,10},{10,1... | collective-permute-start | bytes 1572872 | tf_op jit(solution)/shard_map/ppermute | solution.py:185
  150.6 22.3 %collective-permute-start.8 = (bf16[2,4,2,64,256]{4,3,2,1,0:T(8,128)(2,1)}, bf16[2,4,2,64,256]{4,3,2,1,0:T(8,128)(2,1)}, u32[]{:S(2)}, u32[]{:S(2)}) collective-permute-start(bf16[2,4,2,64,256]{4,3,2,1,0:T(8,128)(2,1)} %pad_maximum_fusion.2), channel_id=1, source_target_pairs={{0,64},{64,128},{128,192},{192,0},{1,65},{65,129},{129,193},{193,1... | collective-permute-start | bytes 1572872 | tf_op jit(solution)/shard_map/ppermute | solution.py:185
  151.4 22.6 %collective-permute-start.3 = (bf16[2,4,2,64,256]{4,3,2,1,0:T(8,128)(2,1)}, bf16[2,4,2,64,256]{4,3,2,1,0:T(8,128)(2,1)S(1)}, u32[]{:S(2)}, u32[]{:S(2)}) collective-permute-start(bf16[2,4,2,64,256]{4,3,2,1,0:T(8,128)(2,1)} %pad_maximum_fusion.1), channel_id=1, source_target_pairs={{0,3},{1,0},{2,1},{3,2},{4,7},{5,4},{6,5},{7,6},{8,11},{9,8},{10,9... | collective-permute-start | bytes 1572872 | tf_op jit(solution)/shard_map/ppermute | solution.py:185
  154.0 22.0 %collective-permute-start.10 = (bf16[2,4,2,64,256]{4,3,2,1,0:T(8,128)(2,1)}, bf16[2,4,2,64,256]{4,3,2,1,0:T(8,128)(2,1)}, u32[]{:S(2)}, u32[]{:S(2)}) collective-permute-start(bf16[2,4,2,64,256]{4,3,2,1,0:T(8,128)(2,1)} %pad_maximum_fusion.3), channel_id=1, source_target_pairs={{0,192},{64,0},{128,64},{192,128},{1,193},{65,1},{129,65},{193,129... | collective-permute-start | bytes 1572872 | tf_op jit(solution)/shard_map/ppermute | solution.py:185
  163.5 0.8 copy-start.4
  164.3 9.7 %collective-permute-start.2 = (bf16[4,2,64,256]{3,2,1,0:T(8,128)(2,1)S(1)}, bf16[4,2,64,256]{3,2,1,0:T(8,128)(2,1)}, u32[]{:S(2)}, u32[]{:S(2)}) collective-permute-start(bf16[4,2,64,256]{3,2,1,0:T(8,128)(2,1)S(1)} %fusion.8), channel_id=1, source_target_pairs={{0,1},{1,2},{2,3},{3,0},{4,5},{5,6},{6,7},{7,4},{8,9},{9,10},{10,1... | collective-permute-start | bytes 786440 | tf_op jit(solution)/shard_map/ppermute | solution.py:185
  165.8 24.7 %all-to-all-start.3 = ((bf16[8,64,512]{2,1,0:T(8,128)(2,1)}), bf16[8,64,512]{2,1,0:T(8,128)(2,1)S(1)}, u32[]{:S(2)}, u32[]{:S(2)}) async-start(bf16[8,64,512]{2,1,0:T(8,128)(2,1)} %get-tuple-element.8), calls=%async_computation.3 | async-start | bytes 1048576 | tf_op jit(solution)/shard_map/all_to_all | solution.py:180
  172.8 11.8 %copy-start.5 = (bf16[2,4,2,64,256]{4,3,2,1,0:T(8,128)(2,1)S(1)}, bf16[2,4,2,64,256]{4,3,2,1,0:T(8,128)(2,1)}, u32[]{:S(2)}) copy-start(bf16[2,4,2,64,256]{4,3,2,1,0:T(8,128)(2,1)} %copy-done.4) | copy-start | bytes 1572868
  173.9 8.7 %collective-permute-start.9 = (bf16[4,2,64,256]{3,2,1,0:T(8,128)(2,1)S(1)}, bf16[4,2,64,256]{3,2,1,0:T(8,128)(2,1)S(1)}, u32[]{:S(2)}, u32[]{:S(2)}) collective-permute-start(bf16[4,2,64,256]{3,2,1,0:T(8,128)(2,1)S(1)} %fusion.4), channel_id=1, source_target_pairs={{0,64},{64,128},{128,192},{192,0},{1,65},{65,129},{129,193},{193,1... | collective-permute-start | bytes 786440 | tf_op jit(solution)/shard_map/ppermute | solution.py:185
  175.4 9.2 %collective-permute-start.4 = (bf16[4,2,64,256]{3,2,1,0:T(8,128)(2,1)S(1)}, bf16[4,2,64,256]{3,2,1,0:T(8,128)(2,1)S(1)}, u32[]{:S(2)}, u32[]{:S(2)}) collective-permute-start(bf16[4,2,64,256]{3,2,1,0:T(8,128)(2,1)S(1)} %get-tuple-element.17), channel_id=1, source_target_pairs={{0,3},{1,0},{2,1},{3,2},{4,7},{5,4},{6,5},{7,6},{8,11},{9,8},{10,9... | collective-permute-start | bytes 786440 | tf_op jit(solution)/shard_map/ppermute | solution.py:185
  184.6 12.8 %collective-permute-start.11 = (bf16[4,2,64,256]{3,2,1,0:T(8,128)(2,1)}, bf16[4,2,64,256]{3,2,1,0:T(8,128)(2,1)}, u32[]{:S(2)}, u32[]{:S(2)}) collective-permute-start(bf16[4,2,64,256]{3,2,1,0:T(8,128)(2,1)} %get-tuple-element.19), channel_id=1, source_target_pairs={{0,192},{64,0},{128,64},{192,128},{1,193},{65,1},{129,65},{193,129... | collective-permute-start | bytes 786440 | tf_op jit(solution)/shard_map/ppermute | solution.py:185
  186.4 14.3 %collective-permute-start.5 = (bf16[2,2,64,256]{3,2,1,0:T(8,128)(2,1)}, bf16[2,2,64,256]{3,2,1,0:T(8,128)(2,1)}, u32[]{:S(2)}, u32[]{:S(2)}) collective-permute-start(bf16[2,2,64,256]{3,2,1,0:T(8,128)(2,1)} %get-tuple-element.28), channel_id=1, source_target_pairs={{0,64},{64,128},{128,192},{192,0},{1,65},{65,129},{129,193},{193,1... | collective-permute-start | bytes 393224 | tf_op jit(solution)/shard_map/ppermute | solution.py:185
  188.4 12.7 %collective-permute-start.7 = (bf16[2,2,64,256]{3,2,1,0:T(8,128)(2,1)}, bf16[2,2,64,256]{3,2,1,0:T(8,128)(2,1)}, u32[]{:S(2)}, u32[]{:S(2)}) collective-permute-start(bf16[2,2,64,256]{3,2,1,0:T(8,128)(2,1)} %get-tuple-element.29), channel_id=1, source_target_pairs={{0,192},{64,0},{128,64},{192,128},{1,193},{65,1},{129,65},{193,129... | collective-permute-start | bytes 393224 | tf_op jit(solution)/shard_map/ppermute | solution.py:185
  189.6 11.5 %collective-permute-start.6 = (bf16[2,2,64,256]{3,2,1,0:T(8,128)(2,1)S(1)}, bf16[2,2,64,256]{3,2,1,0:T(8,128)(2,1)}, u32[]{:S(2)}, u32[]{:S(2)}) collective-permute-start(bf16[2,2,64,256]{3,2,1,0:T(8,128)(2,1)S(1)} %get-tuple-element.30), channel_id=1, source_target_pairs={{0,128},{64,192},{128,0},{192,64},{1,129},{65,193},{129,1},{193,65... | collective-permute-start | bytes 393224 | tf_op jit(solution)/shard_map/ppermute | solution.py:185
  190.5 21.9 %all-to-all-start.4 = ((bf16[8,64,512]{2,1,0:T(8,128)(2,1)}), bf16[8,64,512]{2,1,0:T(8,128)(2,1)}, u32[]{:S(2)}, u32[]{:S(2)}) async-start(bf16[8,64,512]{2,1,0:T(8,128)(2,1)} %get-tuple-element.9), calls=%async_computation.4 | async-start | bytes 1048576 | tf_op jit(solution)/shard_map/all_to_all | solution.py:180
  198.6 5.0 %collective-permute-start.12 = (bf16[2,2,64,256]{3,2,1,0:T(8,128)(2,1)S(1)}, bf16[2,2,64,256]{3,2,1,0:T(8,128)(2,1)S(1)}, u32[]{:S(2)}, u32[]{:S(2)}) collective-permute-start(bf16[2,2,64,256]{3,2,1,0:T(8,128)(2,1)S(1)} %get-tuple-element.31), channel_id=1, source_target_pairs={{0,1},{1,2},{2,3},{3,0},{4,5},{5,6},{6,7},{7,4},{8,9},{9,10},{10,1... | collective-permute-start | bytes 393224 | tf_op jit(solution)/shard_map/ppermute | solution.py:185
  199.0 6.2 %collective-permute-start.14 = (bf16[2,2,64,256]{3,2,1,0:T(8,128)(2,1)S(1)}, bf16[2,2,64,256]{3,2,1,0:T(8,128)(2,1)S(1)}, u32[]{:S(2)}, u32[]{:S(2)}) collective-permute-start(bf16[2,2,64,256]{3,2,1,0:T(8,128)(2,1)S(1)} %get-tuple-element.32), channel_id=1, source_target_pairs={{0,3},{1,0},{2,1},{3,2},{4,7},{5,4},{6,5},{7,6},{8,11},{9,8},{10,9... | collective-permute-start | bytes 393224 | tf_op jit(solution)/shard_map/ppermute | solution.py:185
  200.7 6.5 %collective-permute-start.13 = (bf16[2,2,64,256]{3,2,1,0:T(8,128)(2,1)S(1)}, bf16[2,2,64,256]{3,2,1,0:T(8,128)(2,1)S(1)}, u32[]{:S(2)}, u32[]{:S(2)}) collective-permute-start(bf16[2,2,64,256]{3,2,1,0:T(8,128)(2,1)S(1)} %get-tuple-element.33), channel_id=1, source_target_pairs={{0,2},{1,3},{2,0},{3,1},{4,6},{5,7},{6,4},{7,5},{8,10},{9,11},{10,... | collective-permute-start | bytes 393224 | tf_op jit(solution)/shard_map/ppermute | solution.py:185
  212.4 13.8 %all-to-all-start.5 = ((bf16[8,64,256]{2,1,0:T(8,128)(2,1)}), bf16[8,64,256]{2,1,0:T(8,128)(2,1)S(1)}, u32[]{:S(2)}, u32[]{:S(2)}) async-start(bf16[8,64,256]{2,1,0:T(8,128)(2,1)} %bitcast.62), calls=%async_computation.5 | async-start | bytes 524288 | tf_op jit(solution)/shard_map/all_to_all | solution.py:180
Sparse Core Ops, SparseCore 0:
  29.7 54.1 all-gather.1

commit v3 on v2

--- a/solution.py
+++ b/solution.py
@@ -14,10 +14,12 @@
 GROUPS = NY * NZ * NC
 TILES = GROUPS * SLOTS
 READS = 64
-CHUNK = 4
-MOST_TILES = 68
+CHUNK = 12
+MOST_TILES = 72
 MOST_CHUNKS = MOST_TILES // CHUNK
 ROWS = REP * TILE
+WIDE = REP * HEAD
+PART = TILES // 4
 SCALE = HEAD ** -0.5
 LOG2E = 1.4426950408889634
 AXES = ("y", "z", "core", "x")
@@ -60,24 +62,32 @@
     place = ((tx * NY + ty) * NC + tc) * NZ + tz
     dx, dy, half = (tx - x) & 3, (ty - y) & 3, tz // 4
     hops, hops2 = jnp.where(half == 0, dx, dy), jnp.where(half == 0, dy, dx)
-    goal = ((((tc ^ core) * 2 + half) * 4 + hops) * 2 + (tz // 2) % 2) * 8 + hops2 * 2 + tz % 2
+    which = hops * 2 + (tz // 2) % 2
+    late, piece = jnp.zeros_like(t), jnp.zeros_like(t)
+    for case, (stage, at) in enumerate(((1, 0), (1, 1), (1, 2), (0, 1), (0, 0), (0, 2), (0, 3), (1, 3))):
+        late, piece = jnp.where(which == case, stage, late), jnp.where(which == case, at, piece)
+    goal = ((1 - (tc ^ core)) * 2 + late) * PART + half * 32 + piece * 8 + hops2 * 2 + tz % 2
     code = place + TILES * goal + TILES * TILES * (tile_order + 1)
     wanted = jnp.where(need, rank, 0)[:, :, None] == 1 + jnp.arange(MOST_TILES, dtype=jnp.int32)
     codes = jnp.sum(jnp.where(wanted, code[None, :, None], 0), axis=1)
     return codes, rank[:, -1], own, ends
 
 
-def attend(codes, counts, own, ends, q_ref, g_ref, kv_ref, o_ref, dq_ref, near_ref, far_ref, acc, st):
+def attend(codes, counts, own, ends, qg_ref, kv_hbm, od_ref, far1, far2, near1, near2, kv_ref, acc, st, sems):
+    load = pltpu.make_async_copy(kv_hbm, kv_ref, sems.at[0])
+    load.start()
     acc[...] = jnp.zeros_like(acc)
+    load.wait()
     key_at = lax.broadcasted_iota(jnp.int32, (TILE, ROWS), 0)
     lane = lax.broadcasted_iota(jnp.int32, (1, ROWS), 1) & (TILE - 1)
 
-    def stacked(ref, s):
-        return jnp.concatenate([ref[s, :, h * HEAD:(h + 1) * HEAD] for h in range(REP)], axis=0)
+    def stacked(s, start):
+        return jnp.concatenate(
+            [qg_ref[s, :, start + h * HEAD:start + (h + 1) * HEAD] for h in range(REP)], axis=0)
 
     def one_tile(s, carry):
-        q = stacked(q_ref, s)
-        g = stacked(g_ref, s)
+        q = stacked(s, 0)
+        g = stacked(s, WIDE)
         q_pos = own[s] * TILE + lane
         low = jnp.zeros_like(q_pos)
         for k in range(4):
@@ -121,7 +131,7 @@
         delta = jnp.sum(out * g.astype(jnp.float32).T, axis=0, keepdims=True)
         out = out.T.astype(jnp.bfloat16)
         for h in range(REP):
-            o_ref[s, :, h * HEAD:(h + 1) * HEAD] = out[h * TILE:(h + 1) * TILE]
+            od_ref[s, :, h * HEAD:(h + 1) * HEAD] = out[h * TILE:(h + 1) * TILE]
 
         def backward(c, dq):
             found = places(c)
@@ -132,48 +142,51 @@
             dscore = (prob * (dprob - delta)).astype(jnp.bfloat16)
             dq = dq + lax.dot_general(
                 keys, dscore, (((0,), (0,)), ((), ())), preferred_element_type=jnp.float32)
-            dk = jnp.dot(dscore, q, preferred_element_type=jnp.float32)
+            dk = jnp.dot(dscore, q, preferred_element_type=jnp.float32) * SCALE
             dv = jnp.dot(prob.astype(jnp.bfloat16), g, preferred_element_type=jnp.float32)
             for j, f in enumerate(found):
                 at = (f // TILES) & (TILES - 1)
-                acc[at, :, :HEAD] += dk[j * TILE:(j + 1) * TILE]
-                acc[at, :, HEAD:] += dv[j * TILE:(j + 1) * TILE]
+                acc[at, :, :HEAD] = added(acc[at, :, :HEAD], dk[j * TILE:(j + 1) * TILE])
+                acc[at, :, HEAD:] = added(acc[at, :, HEAD:], dv[j * TILE:(j + 1) * TILE])
             return dq
 
         dq = lax.fori_loop(0, chunks, backward, jnp.zeros((HEAD, ROWS), jnp.float32))
         dq = (dq * SCALE).T.astype(jnp.bfloat16)
         for h in range(REP):
-            dq_ref[s, :, h * HEAD:(h + 1) * HEAD] = dq[h * TILE:(h + 1) * TILE]
+            od_ref[s, :, WIDE + h * HEAD:WIDE + (h + 1) * HEAD] = dq[h * TILE:(h + 1) * TILE]
         return carry
 
     lax.fori_loop(0, NZ, one_tile, 0)
 
-    def finish(i, carry):
-        for ref, at in ((near_ref, i), (far_ref, i + TILES // 2)):
-            ref[i, :, :HEAD] = (acc[at, :, :HEAD] * SCALE).astype(jnp.bfloat16)
-            ref[i, :, HEAD:] = acc[at, :, HEAD:].astype(jnp.bfloat16)
-        return carry
-
-    lax.fori_loop(0, TILES // 2, finish, 0, unroll=2)
-
-
-def attention(codes, counts, own, ends, q, g, kv):
+    stores = [
+        pltpu.make_async_copy(acc.at[pl.ds(i * PART, PART)], ref, sems.at[1 + i])
+        for i, ref in enumerate((far1, far2, near1, near2))
+    ]
+    for store in stores:
+        store.start()
+    for store in stores:
+        store.wait()
+
+
+def attention(codes, counts, own, ends, qg, kv):
     smem = pl.BlockSpec(memory_space=pltpu.SMEM)
     vmem = pl.BlockSpec(memory_space=pltpu.VMEM)
-    wide = jax.ShapeDtypeStruct((NZ, TILE, REP * HEAD), jnp.bfloat16)
-    part = jax.ShapeDtypeStruct((TILES // 2, TILE, 2 * HEAD), jnp.bfloat16)
+    hbm = pl.BlockSpec(memory_space=pl.ANY)
+    part = jax.ShapeDtypeStruct((PART, TILE, 2 * HEAD), jnp.bfloat16)
     return pl.pallas_call(
         attend,
-        out_shape=(wide, wide, part, part),
-        in_specs=[smem] * 4 + [vmem] * 3,
-        out_specs=(vmem, vmem, vmem, vmem),
+        out_shape=(jax.ShapeDtypeStruct((NZ, TILE, 2 * WIDE), jnp.bfloat16),) + (part,) * 4,
+        in_specs=[smem] * 4 + [vmem, hbm],
+        out_specs=(vmem,) + (hbm,) * 4,
         scratch_shapes=[
-            pltpu.VMEM((TILES, TILE, 2 * HEAD), jnp.float32),
+            pltpu.VMEM((TILES, TILE, 2 * HEAD), jnp.bfloat16),
+            pltpu.VMEM((TILES, TILE, 2 * HEAD), jnp.bfloat16),
             pltpu.VMEM((MOST_CHUNKS, CHUNK * TILE, ROWS), jnp.float32),
+            pltpu.SemaphoreType.DMA((5,)),
         ],
-        compiler_params=pltpu.CompilerParams(vmem_limit_bytes=56 * 1024 * 1024),
+        compiler_params=pltpu.CompilerParams(vmem_limit_bytes=48 * 1024 * 1024),
         name="attend",
-    )(codes, counts, own, ends, q, g, kv)
+    )(codes, counts, own, ends, qg, kv)
 
 
 def exchange(blocks, axes):
@@ -189,25 +202,28 @@
     return sum(a.astype(jnp.float32) for a in arrays).astype(jnp.bfloat16)
 
 
-def summed_at_owner(near, far):
-    total = added(near, shift(far, "core", 1))
+def summed_at_owner(far1, far2, near1, near2):
+    first, second = (2, 2, 2, 4, 2, TILE, 2 * HEAD), (2, 4, 4, 2, TILE, 2 * HEAD)
+    other1, other2 = shift(far1, "core", 1).reshape(first), shift(far2, "core", 1).reshape(second)
+    near1, near2 = near1.reshape(first), near2.reshape(second)
     ways = (("x", "y"), ("y", "x"))
     sent = []
     for half, (axis, _) in enumerate(ways):
-        t = total[half]
-        up = shift(jnp.stack([t[2, 0], t[1, 1]]), axis, 1)
-        down = shift(jnp.stack([t[2, 1], t[3, 0]]), axis, -1)
-        sent.append((up, down))
+        up = added(near1[half, 0], other1[half, 0])
+        down = added(near1[half, 1], other1[half, 1])
+        sent.append((shift(up, axis, 1), shift(down, axis, -1)))
     passed = []
     for half, (axis, _) in enumerate(ways):
-        t, (up, down) = total[half], sent[half]
-        passed.append((shift(added(t[1, 0], up[0]), axis, 1), shift(added(t[3, 1], down[0]), axis, -1)))
-    rows = []
-    for half in range(2):
-        t, (up, down), (from_low, from_high) = total[half], sent[half], passed[half]
-        rows.append(jnp.stack([added(t[0, 0], from_low, down[1]), added(t[0, 1], from_high, up[1])]))
+        up, down = sent[half]
+        passed.append((
+            shift(added(near2[half, 2], other2[half, 2], up[0]), axis, 1),
+            shift(added(near2[half, 3], other2[half, 3], down[0]), axis, -1)))
     parts = []
-    for (_, axis), row in zip(ways, rows):
+    for half, (_, axis) in enumerate(ways):
+        (up, down), (low, high) = sent[half], passed[half]
+        row = jnp.stack([
+            added(near2[half, 0], other2[half, 0], low, down[1]),
+            added(near2[half, 1], other2[half, 1], high, up[1])])
         parts.append(added(
             row[:, 0], shift(row[:, 1], axis, 1), shift(row[:, 2], axis, 2), shift(row[:, 3], axis, -1)))
     return jnp.stack(parts).reshape(NZ, TILE, 2 * HEAD)
@@ -216,24 +232,22 @@
 def per_device(queries, keys, values, output_cotangent, tile_order, doc_lengths, read_peer, read_slot):
     order = lax.all_gather(tile_order, ("y", "z", "core"), axis=0, tiled=True)
     codes, counts, own, ends = plan(order, doc_lengths, read_peer[:, 0], read_slot)
-    kv = jnp.concatenate(
-        [keys.reshape(TILE, KV_HEADS, HEAD), values.reshape(TILE, KV_HEADS, HEAD)], axis=2)
-    kv = exchange(kv.transpose(1, 0, 2), "z")
-    kv = lax.all_gather(kv, ("x", "y", "core"), axis=0, tiled=True)
-    q = exchange(queries.reshape(TILE, KV_HEADS, REP * HEAD).transpose(1, 0, 2), "z")
-    g = exchange(output_cotangent.reshape(TILE, KV_HEADS, REP * HEAD).transpose(1, 0, 2), "z")
-    out, dq, near, far = attention(codes, counts, own, ends, q, g, kv)
-    pieces = (2, 4, 2, 4, 2, TILE, 2 * HEAD)
-    dkv = summed_at_owner(near.reshape(pieces), far.reshape(pieces))
-    dkv = exchange(dkv, "z").transpose(1, 0, 2)
-    out = exchange(out, "z").transpose(1, 0, 2).reshape(TILE, KV_HEADS * REP * HEAD)
-    dq = exchange(dq, "z").transpose(1, 0, 2).reshape(TILE, KV_HEADS * REP * HEAD)
-    return (
-        out,
-        dq,
-        dkv[:, :, :HEAD].reshape(TILE, KV_HEADS * HEAD),
-        dkv[:, :, HEAD:].reshape(TILE, KV_HEADS * HEAD),
-    )
+
+    def by_head(a, b, width):
+        both = [v.reshape(TILE, KV_HEADS, width) for v in (a, b)]
+        return exchange(jnp.concatenate(both, axis=2).transpose(1, 0, 2), "z")
+
+    def by_token(blocks, width):
+        blocks = exchange(blocks, "z").transpose(1, 0, 2)
+        return [blocks[:, :, i * width:(i + 1) * width].reshape(TILE, KV_HEADS * width) for i in range(2)]
+
+    kv = lax.all_gather(by_head(keys, values, HEAD), ("x", "y", "core"), axis=0, tiled=True)
+    kv = kv.reshape(TILES, TILE, 2 * HEAD)
+    qg = by_head(queries, output_cotangent, WIDE)
+    od, *terms = attention(codes, counts, own, ends, qg, kv)
+    out, dq = by_token(od, WIDE)
+    dk, dv = by_token(summed_at_owner(*terms), HEAD)
+    return out, dq, dk, dv
 
 
 def solution(mesh):

time: 232 us -> 211 us (0.909); the launches traced: 234 us -> 210 us
  starting transfers between devices: 59.7 us -> 46.1 us
  blocking collectives: 44.5 us -> 56.4 us
  Pallas kernels: 33.1 us -> 23.8 us
  other arithmetic: 19.7 us -> 12.4 us
  local copies, waits for them, and re-layouts: 15.3 us -> 8.45 us
    all_to_all x5 -> x3, waiting for transfers between devices: 21.9 us -> 8.68 us  [exchange(): return lax.all_to_all(blocks, axes, split_axis=0, concat_axis=0, tiled=True)]
    unnamed x1, blocking collectives: 24.3 us -> 36.2 us
    all_to_all x5 -> x3, starting transfers between devices: 26.3 us -> 16.6 us  [exchange(): return lax.all_to_all(blocks, axes, split_axis=0, concat_axis=0, tiled=True)]
    pallas_call x1, Pallas kernels: 33.1 us -> 23.8 us  [attention(): pl.pallas_call(attend, out_shape=(jax.ShapeDtypeStruct((NZ, TILE, 2 * WID...]
    ppermute x15 -> x16, waiting for transfers between devices: 24.9 us -> 32.2 us  [shift(): lax.ppermute(array, axis, [(i, (i + by) % size) for i in range(size)])]
    all_gather x1, waiting for transfers between devices: 0.01 us -> 6.8 us  [per_device(): lax.all_gather(by_head(keys, values, HEAD), ('x', 'y', 'core'), axis=0, t...]
    another operation x12 -> x7, other arithmetic: 9.14 us -> 4.11 us  [the longest x3 3.25 us: summed_at_owner(): jnp.stack([added(near2[half, 0], other2[half, 0], low, down[1]), added(ne...]
    ppermute x15 -> x16, starting transfers between devices: 33.3 us -> 29.4 us  [shift(): lax.ppermute(array, axis, [(i, (i + by) % size) for i in range(size)])]
  transfers between devices with their start and end apart: 21 -> 20, of which waited for: 9 -> 10; matrix products, arithmetic and copies ran while one was open for 11% -> 8% of each run, Pallas kernels for 0% -> 0%
where the time goes in v3:
time: 211 us; the launch traced here: 210 us
  blocking collectives  56.4 us (27%)
  waiting for transfers between devices  47.6 us (23%)
  starting transfers between devices  46.1 us (22%)
  Pallas kernels  23.8 us (11%)
  between operations  15.1 us (7%)
  other arithmetic  12.4 us (6%)
  local copies, waits for them, and re-layouts  8.45 us (4%)
    unnamed x1, blocking collectives  36.2 us
    ppermute x16, waiting for transfers between devices, shift(): lax.ppermute(array, axis, [(i, (i + by) % size) for i in range(size)])  32.2 us
    ppermute x16, starting transfers between devices, shift(): lax.ppermute(array, axis, [(i, (i + by) % size) for i in range(size)])  29.4 us
    pallas_call x1, Pallas kernels, attention(): pl.pallas_call(attend, out_shape=(jax.ShapeDtypeStruct((NZ, TILE, 2 * WID...  23.8 us
    all_to_all x1, blocking collectives, exchange(): return lax.all_to_all(blocks, axes, split_axis=0, concat_axis=0, tiled=True)  20.2 us
    all_to_all x3, starting transfers between devices, exchange(): return lax.all_to_all(blocks, axes, split_axis=0, concat_axis=0, tiled=True)  16.6 us
    all_to_all x3, waiting for transfers between devices, exchange(): return lax.all_to_all(blocks, axes, split_axis=0, concat_axis=0, tiled=True)  8.68 us
    all_gather x1, waiting for transfers between devices, per_device(): lax.all_gather(by_head(keys, values, HEAD), ('x', 'y', 'core'), axis=0, t...  6.8 us
  transfers between devices with their start and end apart: 20, of which 10 were waited for; matrix products, arithmetic and copies ran while one was open for 8% of the time, Pallas kernels for 0%

profile of v3, /device:TPU:6, one launch (start us, length us, event | category | flops | bytes accessed | tf_op | source)
XLA Modules:
  0.0 209.9 jit_solution(14300375626302986515)
XLA Ops:
  7.2 1.0 copy.112
  8.2 0.9 copy.113
  9.3 20.2 %all_to_all.20 = bf16[8,64,256]{2,1,0:T(8,128)(2,1)} all-to-all(bf16[8,64,256]{2,1,0:T(8,128)(2,1)S(1)} %copy.94), channel_id=1, replica_groups=mesh['y'=4,'z'=8,'core'=2,'x'=4] {'z'}, dimensions={0} | all-to-all | bytes 524288 | tf_op jit(solution)/shard_map/all_to_all | solution.py:193
  29.6 0.1 copy_bitcast_fusion
  29.7 1.2 maximum_bitcast_fusion
  30.9 3.6 %all-to-all-start = ((bf16[8,64,1024]{2,1,0:T(8,128)(2,1)}), bf16[8,64,1024]{2,1,0:T(8,128)(2,1)S(1)}, u32[]{:S(2)}, u32[]{:S(2)}) async-start(bf16[8,64,1024]{2,1,0:T(8,128)(2,1)} %maximum_bitcast_fusion), calls=%async_computation | async-start | bytes 2097152 | tf_op jit(solution)/shard_map/all_to_all | solution.py:193
  34.5 0.2 reduce-window.18
  34.7 0.5 broadcast.221
  35.2 0.7 reduce.9
  35.9 0.1 reshape_squeeze.3
  36.0 0.6 dynamic-slice.7
  37.2 0.2 dynamic-update-slice
  37.5 36.2 %all-reduce = s32[256]{0:T(256)S(1)} all-reduce(s32[256]{0:T(256)S(1)} %dynamic-update-slice), channel_id=1, replica_groups=mesh['y'=4,'z'=8,'core'=2,'x'=4] {'y','z','core'}, use_global_device_ids=true, to_apply=%add | all-reduce | flops 256 | bytes 2048
  73.6 0.1 reshape.348
  73.9 0.2 select_reduce_fusion.1
  74.3 0.1 sub.97
  74.4 0.1 sub.91
  74.5 0.3 dynamic-slice_reduce_fusion.own
  75.1 0.2 fusion.42
  75.4 0.6 reduce-window.19
  75.9 0.2 slice_reduce_fusion
  76.3 0.1 copy.90
  76.4 0.2 fusion.46
  76.7 0.2 slice_reduce_fusion.1.counts
  76.8 0.3 select_reduce_fusion.codes
  77.2 6.8 %all-gather.2.cloned.1.call-done.kv_hbm = bf16[256,64,256]{2,1,0:T(8,128)(2,1)} async-done(((bf16[8,64,256]{2,1,0:T(8,128)(2,1)}), bf16[256,64,256]{2,1,0:T(8,128)(2,1)}) %all-gather.2.cloned.1.call-update) | async-done | bytes 8388624 | tf_op jit(solution)/shard_map/all_gather | solution.py:244
  84.0 23.8 %attend.1 = (bf16[8,64,1024]{2,1,0:T(8,128)(2,1)}, bf16[64,64,256]{2,1,0:T(8,128)(2,1)S(1)}, bf16[64,64,256]{2,1,0:T(8,128)(2,1)}, bf16[64,64,256]{2,1,0:T(8,128)(2,1)}, bf16[64,64,256]{2,1,0:T(8,128)(2,1)}) custom-call(s32[8,72]{1,0:T(8,128)S(1)} %select_reduce_fusion.codes, s32[8]{0:T(128)S(1)} %slice_reduce_fusion.1.counts, ...), custom_call_target="tpu_custom_call" | custom-call | tf_op jit(solution)/shard_map/attend/pallas_call | solution.py:176
  107.8 0.1 collective-permute-start.1
  107.9 0.5 collective-permute-start
  108.4 5.6 %collective-permute-done.1 = bf16[64,64,256]{2,1,0:T(8,128)(2,1)S(1)} collective-permute-done((bf16[64,64,256]{2,1,0:T(8,128)(2,1)S(1)}, bf16[64,64,256]{2,1,0:T(8,128)(2,1)S(1)}, u32[]{:S(2)}, u32[]{:S(2)}) %collective-permute-start.1) | collective-permute-done | bytes 2097184 | tf_op jit(solution)/shard_map/ppermute | solution.py:198
  114.0 3.4 %fusion = (bf16[2,4,2,64,256]{4,3,2,1,0:T(8,128)(2,1)S(1)}, bf16[2,4,2,64,256]{4,3,2,1,0:T(8,128)(2,1)}, bf16[2,4,2,64,256]{4,3,2,1,0:T(8,128)(2,1)S(1)}, bf16[2,4,2,64,256]{4,3,2,1,0:T(8,128)(2,1)}) fusion(bf16[2,2,2,4,2,64,256]{6,5,4,3,2,1,0:T(8,128)(2,1)S(1)} %bitcast.206, bf16[2,2,2,4,2,64,256]{6,5,4,3,2,1,0:T(8,128)(2,1)} %bitcast.205), kind=kLoop, calls=%fused_computation.18 | loop fusion | flops 4194304 | bytes 6291456 | tf_op jit(solution)/shard_map/convert_element_type | solution.py:202
  117.4 0.5 collective-permute-start.2
  117.9 5.1 %collective-permute-start.9 = (bf16[2,4,2,64,256]{4,3,2,1,0:T(8,128)(2,1)S(1)}, bf16[2,4,2,64,256]{4,3,2,1,0:T(8,128)(2,1)S(1)}, u32[]{:S(2)}, u32[]{:S(2)}) collective-permute-start(bf16[2,4,2,64,256]{4,3,2,1,0:T(8,128)(2,1)S(1)} %get-tuple-element.25), channel_id=1, source_target_pairs={{0,64},{64,128},{128,192},{192,0},{1,65},{65,129},{129,193},{193,1... | collective-permute-start | bytes 1572872 | tf_op jit(solution)/shard_map/ppermute | solution.py:198
  123.1 4.2 %collective-permute-start.11 = (bf16[2,4,2,64,256]{4,3,2,1,0:T(8,128)(2,1)}, bf16[2,4,2,64,256]{4,3,2,1,0:T(8,128)(2,1)}, u32[]{:S(2)}, u32[]{:S(2)}) collective-permute-start(bf16[2,4,2,64,256]{4,3,2,1,0:T(8,128)(2,1)} %get-tuple-element.24), channel_id=1, source_target_pairs={{0,192},{64,0},{128,64},{192,128},{1,193},{65,1},{129,65},{193,129... | collective-permute-start | bytes 1572872 | tf_op jit(solution)/shard_map/ppermute | solution.py:198
  127.3 6.1 %collective-permute-done.2 = bf16[2,4,2,64,256]{4,3,2,1,0:T(8,128)(2,1)S(1)} collective-permute-done((bf16[2,4,2,64,256]{4,3,2,1,0:T(8,128)(2,1)S(1)}, bf16[2,4,2,64,256]{4,3,2,1,0:T(8,128)(2,1)S(1)}, u32[]{:S(2)}, u32[]{:S(2)}) %collective-permute-start.2) | collective-permute-done | bytes 524320 | tf_op jit(solution)/shard_map/ppermute | solution.py:198
  133.4 6.0 %collective-permute-done.9 = bf16[2,4,2,64,256]{4,3,2,1,0:T(8,128)(2,1)S(1)} collective-permute-done((bf16[2,4,2,64,256]{4,3,2,1,0:T(8,128)(2,1)S(1)}, bf16[2,4,2,64,256]{4,3,2,1,0:T(8,128)(2,1)S(1)}, u32[]{:S(2)}, u32[]{:S(2)}) %collective-permute-start.9) | collective-permute-done | bytes 524320 | tf_op jit(solution)/shard_map/ppermute | solution.py:198
  139.4 1.0 fusion.11
  140.5 4.6 %collective-permute-start.4 = (bf16[2,4,2,64,256]{4,3,2,1,0:T(8,128)(2,1)}, bf16[2,4,2,64,256]{4,3,2,1,0:T(8,128)(2,1)}, u32[]{:S(2)}, u32[]{:S(2)}) collective-permute-start(bf16[2,4,2,64,256]{4,3,2,1,0:T(8,128)(2,1)} %get-tuple-element.26), channel_id=1, source_target_pairs={{0,3},{1,0},{2,1},{3,2},{4,7},{5,4},{6,5},{7,6},{8,11},{9,8},{10,9... | collective-permute-start | bytes 1572872 | tf_op jit(solution)/shard_map/ppermute | solution.py:198
  145.1 6.9 %all-to-all-start.2 = ((bf16[8,64,1024]{2,1,0:T(8,128)(2,1)}), bf16[8,64,1024]{2,1,0:T(8,128)(2,1)S(1)}, u32[]{:S(2)}, u32[]{:S(2)}) async-start(bf16[8,64,1024]{2,1,0:T(8,128)(2,1)} %get-tuple-element.9), calls=%async_computation.2 | async-start | bytes 2097152 | tf_op jit(solution)/shard_map/all_to_all | solution.py:193
  152.0 0.6 collective-permute-start.3
  152.6 1.5 fusion.14
  154.2 3.2 %collective-permute-start.12 = (bf16[4,2,64,256]{3,2,1,0:T(8,128)(2,1)S(1)}, bf16[4,2,64,256]{3,2,1,0:T(8,128)(2,1)S(1)}, u32[]{:S(2)}, u32[]{:S(2)}) collective-permute-start(bf16[4,2,64,256]{3,2,1,0:T(8,128)(2,1)S(1)} %get-tuple-element.19), channel_id=1, source_target_pairs={{0,192},{64,0},{128,64},{192,128},{1,193},{65,1},{129,65},{193,129... | collective-permute-start | bytes 786440 | tf_op jit(solution)/shard_map/ppermute | solution.py:198
  157.4 2.4 %collective-permute-done.3 = bf16[4,2,64,256]{3,2,1,0:T(8,128)(2,1)S(1)} collective-permute-done((bf16[4,2,64,256]{3,2,1,0:T(8,128)(2,1)}, bf16[4,2,64,256]{3,2,1,0:T(8,128)(2,1)S(1)}, u32[]{:S(2)}, u32[]{:S(2)}) %collective-permute-start.3) | collective-permute-done | bytes 262176 | tf_op jit(solution)/shard_map/ppermute | solution.py:198
  159.8 2.1 %collective-permute-done.12 = bf16[4,2,64,256]{3,2,1,0:T(8,128)(2,1)S(1)} collective-permute-done((bf16[4,2,64,256]{3,2,1,0:T(8,128)(2,1)S(1)}, bf16[4,2,64,256]{3,2,1,0:T(8,128)(2,1)S(1)}, u32[]{:S(2)}, u32[]{:S(2)}) %collective-permute-start.12) | collective-permute-done | bytes 262176 | tf_op jit(solution)/shard_map/ppermute | solution.py:198
  161.9 1.6 fusion.12
  163.5 1.5 collective-permute-start.5
  165.0 1.9 collective-permute-start.13
  166.9 0.2 collective-permute-start.15
  167.1 1.7 collective-permute-start.14
  168.8 4.8 %collective-permute-done.5 = bf16[4,2,64,256]{3,2,1,0:T(8,128)(2,1)S(1)} collective-permute-done((bf16[4,2,64,256]{3,2,1,0:T(8,128)(2,1)S(1)}, bf16[4,2,64,256]{3,2,1,0:T(8,128)(2,1)S(1)}, u32[]{:S(2)}, u32[]{:S(2)}) %collective-permute-start.5) | collective-permute-done | bytes 262176 | tf_op jit(solution)/shard_map/ppermute | solution.py:198
  173.7 0.2 fusion.13
  173.9 1.7 collective-permute-start.6
  175.6 2.2 %collective-permute-start.8 = (bf16[2,2,64,256]{3,2,1,0:T(8,128)(2,1)S(1)}, bf16[2,2,64,256]{3,2,1,0:T(8,128)(2,1)S(1)}, u32[]{:S(2)}, u32[]{:S(2)}) collective-permute-start(bf16[2,2,64,256]{3,2,1,0:T(8,128)(2,1)S(1)} %get-tuple-element.30), channel_id=1, source_target_pairs={{0,192},{64,0},{128,64},{192,128},{1,193},{65,1},{129,65},{193,129... | collective-permute-start | bytes 393224 | tf_op jit(solution)/shard_map/ppermute | solution.py:198
  177.7 1.4 collective-permute-start.7
  179.2 1.4 collective-permute-done.6
  180.6 3.6 %collective-permute-done.7 = bf16[2,2,64,256]{3,2,1,0:T(8,128)(2,1)S(1)} collective-permute-done((bf16[2,2,64,256]{3,2,1,0:T(8,128)(2,1)S(1)}, bf16[2,2,64,256]{3,2,1,0:T(8,128)(2,1)S(1)}, u32[]{:S(2)}, u32[]{:S(2)}) %collective-permute-start.7) | collective-permute-done | bytes 131104 | tf_op jit(solution)/shard_map/ppermute | solution.py:198
  184.3 0.7 pad_maximum_fusion
  185.0 6.1 %all-to-all-start.3 = ((bf16[8,64,256]{2,1,0:T(8,128)(2,1)}), bf16[8,64,256]{2,1,0:T(8,128)(2,1)S(1)}, u32[]{:S(2)}, u32[]{:S(2)}) async-start(bf16[8,64,256]{2,1,0:T(8,128)(2,1)} %bitcast.56), calls=%async_computation.3 | async-start | bytes 524288 | tf_op jit(solution)/shard_map/all_to_all | solution.py:193
  191.1 0.1 slice_bitcast_fusion
  191.3 0.8 copy.109
  192.1 0.8 copy.108
  192.9 8.7 %all-to-all-done.3 = bf16[8,64,256]{2,1,0:T(8,128)(2,1)S(1)} async-done(((bf16[8,64,256]{2,1,0:T(8,128)(2,1)}), bf16[8,64,256]{2,1,0:T(8,128)(2,1)S(1)}, u32[]{:S(2)}, u32[]{:S(2)}) %all-to-all-start.3) | async-done | bytes 262176 | tf_op jit(solution)/shard_map/all_to_all | solution.py:193
  201.7 0.7 copy.118
  202.4 0.7 copy.119
  (69 shorter events, 1.3 us)
Async XLA Ops:
  7.2 22.4 %copy-start.4 = (bf16[64,4096]{1,0:T(8,128)(2,1)S(1)}, bf16[64,4096]{1,0:T(8,128)(2,1)}, u32[]{:S(2)}) copy-start(bf16[64,4096]{1,0:T(8,128)(2,1)} %param.11) | copy-start | bytes 1572868
  7.2 22.4 %copy-start.5 = (bf16[64,4096]{1,0:T(8,128)(2,1)S(1)}, bf16[64,4096]{1,0:T(8,128)(2,1)}, u32[]{:S(2)}) copy-start(bf16[64,4096]{1,0:T(8,128)(2,1)} %param.8) | copy-start | bytes 1572868
  7.2 76.8 %all-gather.2.cloned.1.call-start = ((), (), s32[]{:S(2)}) async-start(), calls=%async_computation.4 | async-start | bytes 8650752 | tf_op jit(solution)/shard_map/all_gather | solution.py:244
  29.7 4.8 %copy-start.10 = (s32[4]{0:T(128)S(1)}, s32[4]{0:T(128)}, u32[]{:S(2)}) copy-start(s32[4]{0:T(128)} %param.13) | copy-start | bytes 52
  29.7 5.5 %copy-start.9 = (s32[4096,1]{0,1:T(1,128)S(1)}, s32[4096,1]{0,1:T(1,128)}, u32[]{:S(2)}) copy-start(s32[4096,1]{0,1:T(1,128)} %param.14) | copy-start | bytes 49156
  29.7 6.3 %copy-start.12 = (u32[256]{0:T(256)S(1)}, u32[256]{0:T(256)}, u32[]{:S(2)}) copy-start(u32[256]{0:T(256)} %constant.265) | copy-start | bytes 3076
  29.7 7.5 %copy-start.11 = (s32[4]{0:T(128)S(1)}, s32[4]{0:T(128)}, u32[]{:S(2)}) copy-start(s32[4]{0:T(128)} %param.12) | copy-start | bytes 52
  29.7 44.1 %copy-start.8 = (s32[4096]{0:T(1024)S(1)}, s32[4096]{0:T(1024)}, u32[]{:S(2)}) copy-start(s32[4096]{0:T(1024)} %param.15) | copy-start | bytes 49156
  30.9 46.2 %all-to-all-start = ((bf16[8,64,1024]{2,1,0:T(8,128)(2,1)}), bf16[8,64,1024]{2,1,0:T(8,128)(2,1)S(1)}, u32[]{:S(2)}, u32[]{:S(2)}) async-start(bf16[8,64,1024]{2,1,0:T(8,128)(2,1)} %maximum_bitcast_fusion), calls=%async_computation | async-start | bytes 2097152 | tf_op jit(solution)/shard_map/all_to_all | solution.py:193
  107.8 6.2 %collective-permute-start.1 = (bf16[64,64,256]{2,1,0:T(8,128)(2,1)S(1)}, bf16[64,64,256]{2,1,0:T(8,128)(2,1)S(1)}, u32[]{:S(2)}, u32[]{:S(2)}) collective-permute-start(bf16[64,64,256]{2,1,0:T(8,128)(2,1)S(1)} %get-tuple-element.13), channel_id=1, source_target_pairs={{0,4},{4,0},{1,5},{5,1},{2,6},{6,2},{3,7},{7,3},{8,12},{12,8},{9,1... | collective-permute-start | bytes 6291464 | tf_op jit(solution)/shard_map/ppermute | solution.py:198
  107.9 19.4 %collective-permute-start = (bf16[64,64,256]{2,1,0:T(8,128)(2,1)}, bf16[64,64,256]{2,1,0:T(8,128)(2,1)S(1)}, u32[]{:S(2)}, u32[]{:S(2)}) collective-permute-start(bf16[64,64,256]{2,1,0:T(8,128)(2,1)} %get-tuple-element.11), channel_id=1, source_target_pairs={{0,4},{4,0},{1,5},{5,1},{2,6},{6,2},{3,7},{7,3},{8,12},{12,8},{9,1... | collective-permute-start | bytes 6291464 | tf_op jit(solution)/shard_map/ppermute | solution.py:198
  114.0 25.4 %copy-start = (bf16[64,64,256]{2,1,0:T(8,128)(2,1)S(1)}, bf16[64,64,256]{2,1,0:T(8,128)(2,1)}, u32[]{:S(2)}) copy-start(bf16[64,64,256]{2,1,0:T(8,128)(2,1)} %get-tuple-element.10) | copy-start | bytes 6291460
  117.4 16.0 %collective-permute-start.2 = (bf16[2,4,2,64,256]{4,3,2,1,0:T(8,128)(2,1)S(1)}, bf16[2,4,2,64,256]{4,3,2,1,0:T(8,128)(2,1)S(1)}, u32[]{:S(2)}, u32[]{:S(2)}) collective-permute-start(bf16[2,4,2,64,256]{4,3,2,1,0:T(8,128)(2,1)S(1)} %get-tuple-element.23), channel_id=1, source_target_pairs={{0,1},{1,2},{2,3},{3,0},{4,5},{5,6},{6,7},{7,4},{8,9},{9,10},{10,1... | collective-permute-start | bytes 1572872 | tf_op jit(solution)/shard_map/ppermute | solution.py:198
  117.9 21.5 %collective-permute-start.9 = (bf16[2,4,2,64,256]{4,3,2,1,0:T(8,128)(2,1)S(1)}, bf16[2,4,2,64,256]{4,3,2,1,0:T(8,128)(2,1)S(1)}, u32[]{:S(2)}, u32[]{:S(2)}) collective-permute-start(bf16[2,4,2,64,256]{4,3,2,1,0:T(8,128)(2,1)S(1)} %get-tuple-element.25), channel_id=1, source_target_pairs={{0,64},{64,128},{128,192},{192,0},{1,65},{65,129},{129,193},{193,1... | collective-permute-start | bytes 1572872 | tf_op jit(solution)/shard_map/ppermute | solution.py:198
  123.1 29.6 %collective-permute-start.11 = (bf16[2,4,2,64,256]{4,3,2,1,0:T(8,128)(2,1)}, bf16[2,4,2,64,256]{4,3,2,1,0:T(8,128)(2,1)}, u32[]{:S(2)}, u32[]{:S(2)}) collective-permute-start(bf16[2,4,2,64,256]{4,3,2,1,0:T(8,128)(2,1)} %get-tuple-element.24), channel_id=1, source_target_pairs={{0,192},{64,0},{128,64},{192,128},{1,193},{65,1},{129,65},{193,129... | collective-permute-start | bytes 1572872 | tf_op jit(solution)/shard_map/ppermute | solution.py:198
  127.3 12.2 %copy-start.1 = (bf16[64,64,256]{2,1,0:T(8,128)(2,1)}, bf16[64,64,256]{2,1,0:T(8,128)(2,1)S(1)}, u32[]{:S(2)}) copy-start(bf16[64,64,256]{2,1,0:T(8,128)(2,1)S(1)} %collective-permute-done) | copy-start | bytes 6291460
  133.4 7.1 %copy-start.6 = (bf16[2,4,2,64,256]{4,3,2,1,0:T(8,128)(2,1)}, bf16[2,4,2,64,256]{4,3,2,1,0:T(8,128)(2,1)S(1)}, u32[]{:S(2)}) copy-start(bf16[2,4,2,64,256]{4,3,2,1,0:T(8,128)(2,1)S(1)} %collective-permute-done.2) | copy-start | bytes 1572868
  139.4 1.0 copy-start.3
  140.5 12.2 %collective-permute-start.10 = (bf16[4,2,64,256]{3,2,1,0:T(8,128)(2,1)}, bf16[4,2,64,256]{3,2,1,0:T(8,128)(2,1)S(1)}, u32[]{:S(2)}, u32[]{:S(2)}) collective-permute-start(bf16[4,2,64,256]{3,2,1,0:T(8,128)(2,1)} %get-tuple-element.22), channel_id=1, source_target_pairs={{0,64},{64,128},{128,192},{192,0},{1,65},{65,129},{129,193},{193,1... | collective-permute-start | bytes 786440 | tf_op jit(solution)/shard_map/ppermute | solution.py:198
  140.5 16.9 %collective-permute-start.4 = (bf16[2,4,2,64,256]{4,3,2,1,0:T(8,128)(2,1)}, bf16[2,4,2,64,256]{4,3,2,1,0:T(8,128)(2,1)}, u32[]{:S(2)}, u32[]{:S(2)}) collective-permute-start(bf16[2,4,2,64,256]{4,3,2,1,0:T(8,128)(2,1)} %get-tuple-element.26), channel_id=1, source_target_pairs={{0,3},{1,0},{2,1},{3,2},{4,7},{5,4},{6,5},{7,6},{8,11},{9,8},{10,9... | collective-permute-start | bytes 1572872 | tf_op jit(solution)/shard_map/ppermute | solution.py:198
  145.1 39.9 %all-to-all-start.2 = ((bf16[8,64,1024]{2,1,0:T(8,128)(2,1)}), bf16[8,64,1024]{2,1,0:T(8,128)(2,1)S(1)}, u32[]{:S(2)}, u32[]{:S(2)}) async-start(bf16[8,64,1024]{2,1,0:T(8,128)(2,1)} %get-tuple-element.9), calls=%async_computation.2 | async-start | bytes 2097152 | tf_op jit(solution)/shard_map/all_to_all | solution.py:193
  152.0 9.9 %copy-start.2 = (bf16[64,64,256]{2,1,0:T(8,128)(2,1)S(1)}, bf16[64,64,256]{2,1,0:T(8,128)(2,1)}, u32[]{:S(2)}) copy-start(bf16[64,64,256]{2,1,0:T(8,128)(2,1)} %copy-done.1) | copy-start | bytes 6291460
  152.0 7.7 %collective-permute-start.3 = (bf16[4,2,64,256]{3,2,1,0:T(8,128)(2,1)}, bf16[4,2,64,256]{3,2,1,0:T(8,128)(2,1)S(1)}, u32[]{:S(2)}, u32[]{:S(2)}) collective-permute-start(bf16[4,2,64,256]{3,2,1,0:T(8,128)(2,1)} %get-tuple-element.21), channel_id=1, source_target_pairs={{0,1},{1,2},{2,3},{3,0},{4,5},{5,6},{6,7},{7,4},{8,9},{9,10},{10,1... | collective-permute-start | bytes 786440 | tf_op jit(solution)/shard_map/ppermute | solution.py:198
  154.1 19.5 %copy-start.7 = (bf16[2,4,2,64,256]{4,3,2,1,0:T(8,128)(2,1)S(1)}, bf16[2,4,2,64,256]{4,3,2,1,0:T(8,128)(2,1)}, u32[]{:S(2)}) copy-start(bf16[2,4,2,64,256]{4,3,2,1,0:T(8,128)(2,1)} %copy-done.6) | copy-start | bytes 1572868
  154.2 7.7 %collective-permute-start.12 = (bf16[4,2,64,256]{3,2,1,0:T(8,128)(2,1)S(1)}, bf16[4,2,64,256]{3,2,1,0:T(8,128)(2,1)S(1)}, u32[]{:S(2)}, u32[]{:S(2)}) collective-permute-start(bf16[4,2,64,256]{3,2,1,0:T(8,128)(2,1)S(1)} %get-tuple-element.19), channel_id=1, source_target_pairs={{0,192},{64,0},{128,64},{192,128},{1,193},{65,1},{129,65},{193,129... | collective-permute-start | bytes 786440 | tf_op jit(solution)/shard_map/ppermute | solution.py:198
  163.5 10.2 %collective-permute-start.5 = (bf16[4,2,64,256]{3,2,1,0:T(8,128)(2,1)S(1)}, bf16[4,2,64,256]{3,2,1,0:T(8,128)(2,1)S(1)}, u32[]{:S(2)}, u32[]{:S(2)}) collective-permute-start(bf16[4,2,64,256]{3,2,1,0:T(8,128)(2,1)S(1)} %get-tuple-element.17), channel_id=1, source_target_pairs={{0,3},{1,0},{2,1},{3,2},{4,7},{5,4},{6,5},{7,6},{8,11},{9,8},{10,9... | collective-permute-start | bytes 786440 | tf_op jit(solution)/shard_map/ppermute | solution.py:198
  165.0 12.7 %collective-permute-start.13 = (bf16[2,2,64,256]{3,2,1,0:T(8,128)(2,1)S(1)}, bf16[2,2,64,256]{3,2,1,0:T(8,128)(2,1)S(1)}, u32[]{:S(2)}, u32[]{:S(2)}) collective-permute-start(bf16[2,2,64,256]{3,2,1,0:T(8,128)(2,1)S(1)} %get-tuple-element.32), channel_id=1, source_target_pairs={{0,1},{1,2},{2,3},{3,0},{4,5},{5,6},{6,7},{7,4},{8,9},{9,10},{10,1... | collective-permute-start | bytes 393224 | tf_op jit(solution)/shard_map/ppermute | solution.py:198
  166.9 12.2 %collective-permute-start.15 = (bf16[2,2,64,256]{3,2,1,0:T(8,128)(2,1)S(1)}, bf16[2,2,64,256]{3,2,1,0:T(8,128)(2,1)S(1)}, u32[]{:S(2)}, u32[]{:S(2)}) collective-permute-start(bf16[2,2,64,256]{3,2,1,0:T(8,128)(2,1)S(1)} %get-tuple-element.33), channel_id=1, source_target_pairs={{0,3},{1,0},{2,1},{3,2},{4,7},{5,4},{6,5},{7,6},{8,11},{9,8},{10,9... | collective-permute-start | bytes 393224 | tf_op jit(solution)/shard_map/ppermute | solution.py:198
  167.1 12.0 %collective-permute-start.14 = (bf16[2,2,64,256]{3,2,1,0:T(8,128)(2,1)S(1)}, bf16[2,2,64,256]{3,2,1,0:T(8,128)(2,1)S(1)}, u32[]{:S(2)}, u32[]{:S(2)}) collective-permute-start(bf16[2,2,64,256]{3,2,1,0:T(8,128)(2,1)S(1)} %get-tuple-element.34), channel_id=1, source_target_pairs={{0,2},{1,3},{2,0},{3,1},{4,6},{5,7},{6,4},{7,5},{8,10},{9,11},{10,... | collective-permute-start | bytes 393224 | tf_op jit(solution)/shard_map/ppermute | solution.py:198
  173.9 6.7 %collective-permute-start.6 = (bf16[2,2,64,256]{3,2,1,0:T(8,128)(2,1)S(1)}, bf16[2,2,64,256]{3,2,1,0:T(8,128)(2,1)S(1)}, u32[]{:S(2)}, u32[]{:S(2)}) collective-permute-start(bf16[2,2,64,256]{3,2,1,0:T(8,128)(2,1)S(1)} %get-tuple-element.29), channel_id=1, source_target_pairs={{0,64},{64,128},{128,192},{192,0},{1,65},{65,129},{129,193},{193,1... | collective-permute-start | bytes 393224 | tf_op jit(solution)/shard_map/ppermute | solution.py:198
  175.6 5.0 %collective-permute-start.8 = (bf16[2,2,64,256]{3,2,1,0:T(8,128)(2,1)S(1)}, bf16[2,2,64,256]{3,2,1,0:T(8,128)(2,1)S(1)}, u32[]{:S(2)}, u32[]{:S(2)}) collective-permute-start(bf16[2,2,64,256]{3,2,1,0:T(8,128)(2,1)S(1)} %get-tuple-element.30), channel_id=1, source_target_pairs={{0,192},{64,0},{128,64},{192,128},{1,193},{65,1},{129,65},{193,129... | collective-permute-start | bytes 393224 | tf_op jit(solution)/shard_map/ppermute | solution.py:198
  177.7 6.5 %collective-permute-start.7 = (bf16[2,2,64,256]{3,2,1,0:T(8,128)(2,1)S(1)}, bf16[2,2,64,256]{3,2,1,0:T(8,128)(2,1)S(1)}, u32[]{:S(2)}, u32[]{:S(2)}) collective-permute-start(bf16[2,2,64,256]{3,2,1,0:T(8,128)(2,1)S(1)} %get-tuple-element.31), channel_id=1, source_target_pairs={{0,128},{64,192},{128,0},{192,64},{1,129},{65,193},{129,1},{193,65... | collective-permute-start | bytes 393224 | tf_op jit(solution)/shard_map/ppermute | solution.py:198
  185.0 16.6 %all-to-all-start.3 = ((bf16[8,64,256]{2,1,0:T(8,128)(2,1)}), bf16[8,64,256]{2,1,0:T(8,128)(2,1)S(1)}, u32[]{:S(2)}, u32[]{:S(2)}) async-start(bf16[8,64,256]{2,1,0:T(8,128)(2,1)} %bitcast.56), calls=%async_computation.3 | async-start | bytes 524288 | tf_op jit(solution)/shard_map/all_to_all | solution.py:193
Sparse Core Ops, SparseCore 0:
  29.7 54.2 all-gather.1

commit v4 on v3

v4 whole, which is shorter than its diff:
```python
import jax
import jax.numpy as jnp
from jax import lax
from jax.experimental import pallas as pl
from jax.experimental.pallas import tpu as pltpu
from jax.sharding import Mesh, PartitionSpec as P

HEAD = 128
TILE = 64
SLOTS = 4
KV_HEADS = 8
REP = 4
NX, NY, NZ, NC = 4, 4, 8, 2
GROUPS = NY * NZ * NC
TILES = GROUPS * SLOTS
READS = 64
CHUNK = 12
MOST_TILES = 72
MOST_CHUNKS = MOST_TILES // CHUNK
ROWS = REP * TILE
WIDE = REP * HEAD
PART = TILES // 8
TOGETHER = 2
SCALE = HEAD ** -0.5
LOG2E = 1.4426950408889634
AXES = ("y", "z", "core", "x")
NEG = -1e30


def plan(tile_order, doc_lengths, read_peer, read_slot):
    x, y, core = lax.axis_index("x"), lax.axis_index("y"), lax.axis_index("core")
    ends = jnp.cumsum(doc_lengths, dtype=jnp.int32)

    def mine(table):
        table = table.reshape(NY, NZ, NC, READS)
        table = lax.dynamic_index_in_dim(table, y, 0, keepdims=False)
        return lax.dynamic_index_in_dim(table, core, 1, keepdims=False)

    peers, bases = mine(read_peer), mine(read_slot)
    group = (y * NZ + jnp.arange(NZ, dtype=jnp.int32)) * NC + core
    all_groups = jnp.arange(GROUPS, dtype=jnp.int32)
    same = peers[:, :, None] == all_groups[None, None, :]
    count = jnp.sum(same.astype(jnp.int32), axis=1)
    entry = jnp.arange(READS, dtype=jnp.int32)
    first = jnp.min(jnp.where(same, (entry[None, :] * SLOTS + bases)[:, :, None], READS * SLOTS), axis=1)
    slot = jnp.arange(SLOTS, dtype=jnp.int32)
    listed = ((slot[None, None, :] - first[:, :, None]) & (SLOTS - 1)) < count[:, :, None]
    listed = listed | (all_groups[None, :] == group[:, None])[:, :, None]
    listed = listed.reshape(NZ, TILES)
    order = tile_order.reshape(NY, NZ, NC, SLOTS)
    own = lax.dynamic_index_in_dim(order, y, 0, keepdims=False)
    own = lax.dynamic_index_in_dim(own, core, 1, keepdims=False)
    own = lax.dynamic_index_in_dim(own, x, 1, keepdims=False)
    start = jnp.max(jnp.where(ends[None, :] <= own[:, None] * TILE, ends[None, :], 0), axis=1)
    need = (
        listed
        & (tile_order[None, :] <= own[:, None])
        & (tile_order[None, :] * TILE + (TILE - 1) >= start[:, None])
    )
    rank = jnp.cumsum(need.astype(jnp.int32), axis=1)
    t = jnp.arange(TILES, dtype=jnp.int32)
    tx, tc, tz, ty = t % 4, (t // 4) % 2, (t // 8) % 8, t // 64
    place = ((tx * NY + ty) * NC + tc) * NZ + tz
    dx, dy, half = (tx - x) & 3, (ty - y) & 3, tz // 4
    hops, hops2 = jnp.where(half == 0, dx, dy), jnp.where(half == 0, dy, dx)
    goal = ((1 - (tc ^ core)) * 4 + hops) * PART + half * 16 + hops2 * 4 + tz % 4
    code = place + TILES * goal + TILES * TILES * (tile_order + 1)
    wanted = jnp.where(need, rank, 0)[:, :, None] == 1 + jnp.arange(MOST_TILES, dtype=jnp.int32)
    codes = jnp.sum(jnp.where(wanted, code[None, :, None], 0), axis=1)
    counts = rank[:, -1]
    s = jnp.arange(NZ, dtype=jnp.int32)
    ahead = (counts[None, :] > counts[:, None]) | ((counts[None, :] == counts[:, None]) & (s[None, :] < s[:, None]))
    turn = jnp.sum(ahead.astype(jnp.int32), axis=1)
    turns = jnp.sum(jnp.where(turn[None, :] == s[:, None], s[None, :], 0), axis=1)
    return codes, counts, own, ends, turns


def attend(codes, counts, own, ends, turns, qg_ref, kv_hbm, od_ref, *refs):
    parts, (kv_ref, acc, st, sems) = refs[:8], refs[8:]
    load = pltpu.make_async_copy(kv_hbm, kv_ref, sems.at[0])
    load.start()
    acc[...] = jnp.zeros_like(acc)
    load.wait()
    key_at = lax.broadcasted_iota(jnp.int32, (TILE, ROWS), 0)
    lane = lax.broadcasted_iota(jnp.int32, (1, ROWS), 1) & (TILE - 1)

    def stacked(s, start):
        return jnp.concatenate(
            [qg_ref[s, :, start + h * HEAD:start + (h + 1) * HEAD] for h in range(REP)], axis=0)

    def bounds(s):
        q_pos = own[s] * TILE + lane
        low = jnp.zeros_like(q_pos)
        for k in range(4):
            low = jnp.where(q_pos >= ends[k], ends[k], low)
        return q_pos, low

    def rows(c, s, part):
        found = [codes[s, c * CHUNK + j] for j in range(CHUNK)]
        return [kv_ref[f & (TILES - 1), :, part * HEAD:(part + 1) * HEAD] for f in found], found

    def some_tiles(n, carry):
        tiles = [turns[n * TOGETHER + i] for i in range(TOGETHER)]
        q = [stacked(s, 0) for s in tiles]
        g = [stacked(s, WIDE) for s in tiles]
        limits = [bounds(s) for s in tiles]
        chunks = (counts[tiles[0]] + (CHUNK - 1)) // CHUNK

        def scores(c, tops):
            new = []
            for i, s in enumerate(tiles):
                q_pos, low = limits[i]
                keys, found = rows(c, s, 0)
                raw = lax.dot_general(
                    jnp.concatenate(keys, axis=0), q[i], (((1,), (1,)), ((), ())),
                    preferred_element_type=jnp.float32)
                top = tops[i]
                for j, f in enumerate(found):
                    base = (f // (TILES * TILES) - 1) * TILE
                    part = raw[j * TILE:(j + 1) * TILE]
                    part = jnp.where((key_at <= q_pos - base) & (key_at >= low - base), part, NEG)
                    st[i, c, j * TILE:(j + 1) * TILE, :] = part
                    top = jnp.maximum(top, jnp.max(part.reshape(TILE // 8, 8, ROWS), axis=0))
                new.append(top)
            return tuple(new)

        tops = lax.fori_loop(0, chunks, scores, (jnp.full((8, ROWS), NEG, jnp.float32),) * TOGETHER)
        tops = [jnp.max(top, axis=0, keepdims=True) * (SCALE * LOG2E) for top in tops]

        def forward(c, held):
            new = []
            for i, s in enumerate(tiles):
                total, out = held[i]
                prob = jnp.exp2(st[i, c] * (SCALE * LOG2E) - tops[i])
                st[i, c] = prob
                total = total + jnp.sum(prob.reshape(CHUNK * TILE // 8, 8, ROWS), axis=0)
                vals, _ = rows(c, s, 1)
                out = out + lax.dot_general(
                    jnp.concatenate(vals, axis=0), prob.astype(jnp.bfloat16), (((0,), (0,)), ((), ())),
                    preferred_element_type=jnp.float32)
                new.append((total, out))
            return tuple(new)

        start = (jnp.zeros((8, ROWS), jnp.float32), jnp.zeros((HEAD, ROWS), jnp.float32))
        held = lax.fori_loop(0, chunks, forward, (start,) * TOGETHER)
        invs, deltas = [], []
        for i, s in enumerate(tiles):
            total, out = held[i]
            inv = 1.0 / jnp.sum(total, axis=0, keepdims=True)
            out = (out * inv).astype(jnp.bfloat16).astype(jnp.float32)
            invs.append(inv)
            deltas.append(jnp.sum(out * g[i].astype(jnp.float32).T, axis=0, keepdims=True))
            out = out.T.astype(jnp.bfloat16)
            for h in range(REP):
                od_ref[s, :, h * HEAD:(h + 1) * HEAD] = out[h * TILE:(h + 1) * TILE]

        def backward(c, dqs):
            new = []
            for i, s in enumerate(tiles):
                prob = st[i, c] * invs[i]
                keys, found = rows(c, s, 0)
                vals, _ = rows(c, s, 1)
                dprob = lax.dot_general(
                    jnp.concatenate(vals, axis=0), g[i], (((1,), (1,)), ((), ())),
                    preferred_element_type=jnp.float32)
                dscore = (prob * (dprob - deltas[i])).astype(jnp.bfloat16)
                new.append(dqs[i] + lax.dot_general(
                    jnp.concatenate(keys, axis=0), dscore, (((0,), (0,)), ((), ())),
                    preferred_element_type=jnp.float32))
                dk = jnp.dot(dscore, q[i], preferred_element_type=jnp.float32) * SCALE
                dv = jnp.dot(prob.astype(jnp.bfloat16), g[i], preferred_element_type=jnp.float32)
                for j, f in enumerate(found):
                    at = (f // TILES) & (TILES - 1)
                    acc[at, :, :HEAD] = added(acc[at, :, :HEAD], dk[j * TILE:(j + 1) * TILE])
                    acc[at, :, HEAD:] = added(acc[at, :, HEAD:], dv[j * TILE:(j + 1) * TILE])
            return tuple(new)

        dqs = lax.fori_loop(0, chunks, backward, (jnp.zeros((HEAD, ROWS), jnp.float32),) * TOGETHER)
        for s, dq in zip(tiles, dqs):
            dq = (dq * SCALE).T.astype(jnp.bfloat16)
            for h in range(REP):
                od_ref[s, :, WIDE + h * HEAD:WIDE + (h + 1) * HEAD] = dq[h * TILE:(h + 1) * TILE]
        return carry

    lax.fori_loop(0, NZ // TOGETHER, some_tiles, 0)

    stores = [
        pltpu.make_async_copy(acc.at[pl.ds(i * PART, PART)], ref, sems.at[1 + i])
        for i, ref in enumerate(parts)
    ]
    for store in stores:
        store.start()
    for store in stores:
        store.wait()


def attention(codes, counts, own, ends, turns, qg, kv):
    smem = pl.BlockSpec(memory_space=pltpu.SMEM)
    vmem = pl.BlockSpec(memory_space=pltpu.VMEM)
    hbm = pl.BlockSpec(memory_space=pl.ANY)
    part = jax.ShapeDtypeStruct((PART, TILE, 2 * HEAD), jnp.bfloat16)
    return pl.pallas_call(
        attend,
        out_shape=(jax.ShapeDtypeStruct((NZ, TILE, 2 * WIDE), jnp.bfloat16),) + (part,) * 8,
        in_specs=[smem] * 5 + [vmem, hbm],
        out_specs=(vmem,) + (hbm,) * 8,
        scratch_shapes=[
            pltpu.VMEM((TILES, TILE, 2 * HEAD), jnp.bfloat16),
            pltpu.VMEM((TILES, TILE, 2 * HEAD), jnp.bfloat16),
            pltpu.VMEM((TOGETHER, MOST_CHUNKS, CHUNK * TILE, ROWS), jnp.float32),
            pltpu.SemaphoreType.DMA((9,)),
        ],
        compiler_params=pltpu.CompilerParams(vmem_limit_bytes=48 * 1024 * 1024),
        name="attend",
    )(codes, counts, own, ends, turns, qg, kv)


def exchange(blocks, axes):
    return lax.all_to_all(blocks, axes, split_axis=0, concat_axis=0, tiled=True)


def shift(array, axis, by):
    size = lax.axis_size(axis)
    return lax.ppermute(array, axis, [(i, (i + by) % size) for i in range(size)])


def added(*arrays):
    return sum(a.astype(jnp.float32) for a in arrays).astype(jnp.bfloat16)


def summed_at_owner(far, near, beside):
    shape = (2, 4, 4, TILE, 2 * HEAD)
    near = [part.reshape(shape) for part in near]
    other = {hops: shift(far[hops], "core", 1).reshape(shape) for hops in (2, 1, 3, 0)}
    ways = (("x", "y"), ("y", "x"))
    got = ([], [])
    for hops in (2, 1, 3):
        for half, (axis, _) in enumerate(ways):
            got[half].append(shift(added(near[hops][half], other[hops][half]), axis, hops))
    beside, got = lax.optimization_barrier((beside, got))
    parts = []
    for half, (_, axis) in enumerate(ways):
        row = added(near[0][half], other[0][half], *got[half])
        parts.append(added(row[0], *[shift(row[hops], axis, hops) for hops in (2, 1, 3)]))
    return jnp.concatenate(parts), beside


def per_device(queries, keys, values, output_cotangent, tile_order, doc_lengths, read_peer, read_slot):
    order = lax.all_gather(tile_order, ("y", "z", "core"), axis=0, tiled=True)
    lists = plan(order, doc_lengths, read_peer[:, 0], read_slot)

    def by_head(a, b, width):
        both = [v.reshape(TILE, KV_HEADS, width) for v in (a, b)]
        return exchange(jnp.concatenate(both, axis=2).transpose(1, 0, 2), "z")

    def by_token(blocks, width):
        blocks = blocks.transpose(1, 0, 2)
        return [blocks[:, :, i * width:(i + 1) * width].reshape(TILE, KV_HEADS * width) for i in range(2)]

    kv = lax.all_gather(by_head(keys, values, HEAD), ("x", "y", "core"), axis=0, tiled=True)
    kv = kv.reshape(TILES, TILE, 2 * HEAD)
    qg = by_head(queries, output_cotangent, WIDE)
    od, *terms = attention(*lists, qg, kv)
    dkv, od = summed_at_owner(terms[:4], terms[4:], exchange(od, "z"))
    out, dq = by_token(od, WIDE)
    dk, dv = by_token(exchange(dkv, "z"), HEAD)
    return out, dq, dk, dv


def solution(mesh):
    fine = Mesh(mesh.devices.reshape(NY, NZ, NC, NX), AXES)
    rows = P(AXES, None)
    return jax.shard_map(
        per_device,
        mesh=fine,
        in_specs=(rows, rows, rows, rows, P(("y", "z", "core")), P(), P(), P()),
        out_specs=(rows, rows, rows, rows),
        check_vma=False,
    )
```

time: 211 us -> 198 us (0.938)
  waiting for transfers between devices: 47.6 us -> 38.3 us
  starting transfers between devices: 46.1 us -> 38.2 us
  local copies, waits for them, and re-layouts: 8.45 us -> 10.7 us
    ppermute x16, starting transfers between devices: 29.4 us -> 20.4 us  [shift(): lax.ppermute(array, axis, [(i, (i + by) % size) for i in range(size)])]
    ppermute x16, waiting for transfers between devices: 32.2 us -> 25.3 us  [shift(): lax.ppermute(array, axis, [(i, (i + by) % size) for i in range(size)])]
    another operation x10 -> x4, other arithmetic: 4.98 us -> 0.86 us  [the longest x3 3.25 us: summed_at_owner(): jnp.stack([added(near2[half, 0], other2[half, 0], low, down[1]), added(ne...]
    convert_element_type x2 -> x7, other arithmetic: 4.42 us -> 8.28 us  [added(): return sum((a.astype(jnp.float32) for a in arrays)).astype(jnp.bfloat16)]
    unnamed x34, local copies, waits for them, and re-layouts: 3.5 us -> 5.66 us
  transfers between devices with their start and end apart: 20 -> 20, of which waited for: 10 -> 9; matrix products, arithmetic and copies ran while one was open for 8% -> 9% of each run, Pallas kernels for 0% -> 0%
where the time goes in v4:
time: 198 us; the launch traced here: 196 us
  blocking collectives  56.4 us (28%)
  waiting for transfers between devices  38.3 us (19%)
  starting transfers between devices  38.2 us (19%)
  Pallas kernels  23.9 us (12%)
  between operations  15.2 us (8%)
  other arithmetic  13.4 us (7%)
  local copies, waits for them, and re-layouts  10.7 us (5%)
    unnamed x1, blocking collectives  36.2 us
    ppermute x16, waiting for transfers between devices, shift(): lax.ppermute(array, axis, [(i, (i + by) % size) for i in range(size)])  25.3 us
    pallas_call x1, Pallas kernels, attention(): pl.pallas_call(attend, out_shape=(jax.ShapeDtypeStruct((NZ, TILE, 2 * WID...  23.9 us
    ppermute x16, starting transfers between devices, shift(): lax.ppermute(array, axis, [(i, (i + by) % size) for i in range(size)])  20.4 us
    all_to_all x1, blocking collectives, exchange(): return lax.all_to_all(blocks, axes, split_axis=0, concat_axis=0, tiled=True)  20.2 us
    all_to_all x3, starting transfers between devices, exchange(): return lax.all_to_all(blocks, axes, split_axis=0, concat_axis=0, tiled=True)  17.7 us
    convert_element_type x7, other arithmetic, added(): return sum((a.astype(jnp.float32) for a in arrays)).astype(jnp.bfloat16)  8.28 us
    all_to_all x3, waiting for transfers between devices, exchange(): return lax.all_to_all(blocks, axes, split_axis=0, concat_axis=0, tiled=True)  7.51 us
  transfers between devices with their start and end apart: 20, of which 9 were waited for; matrix products, arithmetic and copies ran while one was open for 9% of the time, Pallas kernels for 0%

profile of v4, /device:TPU:6, one launch (start us, length us, event | category | flops | bytes accessed | tf_op | source)
XLA Modules:
  0.0 196.1 jit_solution(193122552422669874)
XLA Ops:
  7.2 1.0 copy.76
  8.2 0.9 copy.77
  9.3 20.2 %all_to_all.20 = bf16[8,64,256]{2,1,0:T(8,128)(2,1)} all-to-all(bf16[8,64,256]{2,1,0:T(8,128)(2,1)S(1)} %copy.65), channel_id=1, replica_groups=mesh['y'=4,'z'=8,'core'=2,'x'=4] {'z'}, dimensions={0} | all-to-all | bytes 524288 | tf_op jit(solution)/shard_map/all_to_all | solution.py:219
  29.6 0.1 copy_bitcast_fusion
  29.7 1.2 maximum_bitcast_fusion
  30.9 3.6 %all-to-all-start = ((bf16[8,64,1024]{2,1,0:T(8,128)(2,1)}), bf16[8,64,1024]{2,1,0:T(8,128)(2,1)S(1)}, u32[]{:S(2)}, u32[]{:S(2)}) async-start(bf16[8,64,1024]{2,1,0:T(8,128)(2,1)} %maximum_bitcast_fusion), calls=%async_computation | async-start | bytes 2097152 | tf_op jit(solution)/shard_map/all_to_all | solution.py:219
  34.5 0.2 reduce-window.18
  34.7 0.5 broadcast.197
  35.2 0.7 reduce.9
  36.0 0.6 dynamic-slice.7
  37.2 0.2 dynamic-update-slice
  37.5 36.2 %all-reduce = s32[256]{0:T(256)S(1)} all-reduce(s32[256]{0:T(256)S(1)} %dynamic-update-slice), channel_id=1, replica_groups=mesh['y'=4,'z'=8,'core'=2,'x'=4] {'y','z','core'}, use_global_device_ids=true, to_apply=%add | all-reduce | flops 256 | bytes 2048
  73.6 0.1 reshape.349
  73.9 0.2 select_reduce_fusion.1
  74.3 0.1 sub.91
  74.4 0.1 sub.85
  74.5 0.3 dynamic-slice_reduce_fusion.own
  75.1 0.2 fusion.10
  75.3 0.6 reduce-window.19
  75.9 0.2 slice_reduce_fusion
  76.3 0.1 copy.61
  76.4 0.2 fusion.14
  76.6 0.2 slice_reduce_fusion.1.counts
  76.8 0.2 convert_reduce_fusion.1
  77.0 0.1 select_reduce_fusion.2.turns
  77.1 0.3 select_reduce_fusion.codes
  77.5 1.0 copy-done
  78.4 5.5 %all-gather.2.cloned.1.call-done.kv_hbm = bf16[256,64,256]{2,1,0:T(8,128)(2,1)} async-done(((bf16[8,64,256]{2,1,0:T(8,128)(2,1)}), bf16[256,64,256]{2,1,0:T(8,128)(2,1)}) %all-gather.2.cloned.1.call-update) | async-done | bytes 8388624 | tf_op jit(solution)/shard_map/all_gather | solution.py:260
  84.0 23.9 %attend.1 = (bf16[8,64,1024]{2,1,0:T(8,128)(2,1)}, bf16[32,64,256]{2,1,0:T(8,128)(2,1)S(1)}, bf16[32,64,256]{2,1,0:T(8,128)(2,1)S(1)}, bf16[32,64,256]{2,1,0:T(8...) custom-call(s32[8,72]{1,0:T(8,128)S(1)} %select_reduce_fusion.codes,, ...), custom_call_target="tpu_custom_call" | custom-call | tf_op jit(solution)/shard_map/attend/pallas_call | solution.py:202
  107.9 5.1 %collective-permute-start = (bf16[32,64,256]{2,1,0:T(8,128)(2,1)}, bf16[32,64,256]{2,1,0:T(8,128)(2,1)}, u32[]{:S(2)}, u32[]{:S(2)}) collective-permute-start(bf16[32,64,256]{2,1,0:T(8,128)(2,1)} %get-tuple-element.22), channel_id=1, source_target_pairs={{0,4},{4,0},{1,5},{5,1},{2,6},{6,2},{3,7},{7,3},{8,12},{12,8},{9,1... | collective-permute-start | bytes 3145736 | tf_op jit(solution)/shard_map/ppermute | solution.py:224
  113.0 0.1 collective-permute-start.2
  113.1 0.4 collective-permute-start.4
  113.5 7.0 %all-to-all-start.2 = ((bf16[8,64,1024]{2,1,0:T(8,128)(2,1)}), bf16[8,64,1024]{2,1,0:T(8,128)(2,1)}, u32[]{:S(2)}, u32[]{:S(2)}) async-start(bf16[8,64,1024]{2,1,0:T(8,128)(2,1)} %get-tuple-element.20), calls=%async_computation.2 | async-start | bytes 2097152 | tf_op jit(solution)/shard_map/all_to_all | solution.py:219
  120.6 2.0 add_convert_fusion.4
  122.7 2.8 %collective-permute-start.6 = (bf16[4,4,64,256]{3,2,1,0:T(8,128)(2,1)S(1)}, bf16[4,4,64,256]{3,2,1,0:T(8,128)(2,1)}, u32[]{:S(2)}, u32[]{:S(2)}) collective-permute-start(bf16[4,4,64,256]{3,2,1,0:T(8,128)(2,1)S(1)} %bitcast.120), channel_id=1, source_target_pairs={{0,128},{64,192},{128,0},{192,64},{1,129},{65,193},{129,1},{193,65... | collective-permute-start | bytes 1572872 | tf_op jit(solution)/shard_map/ppermute | solution.py:224
  125.6 1.6 add_convert_fusion.3
  127.2 2.2 %collective-permute-start.3 = (bf16[4,4,64,256]{3,2,1,0:T(8,128)(2,1)S(1)}, bf16[4,4,64,256]{3,2,1,0:T(8,128)(2,1)S(1)}, u32[]{:S(2)}, u32[]{:S(2)}) collective-permute-start(bf16[4,4,64,256]{3,2,1,0:T(8,128)(2,1)S(1)} %bitcast.122), channel_id=1, source_target_pairs={{0,1},{1,2},{2,3},{3,0},{4,5},{5,6},{6,7},{7,4},{8,9},{9,10},{10,1... | collective-permute-start | bytes 1572872 | tf_op jit(solution)/shard_map/ppermute | solution.py:224
  129.3 1.6 add_convert_fusion.2
  130.9 0.6 collective-permute-start.5
  131.6 7.4 %collective-permute-done.1 = bf16[4,4,64,256]{3,2,1,0:T(8,128)(2,1)S(1)} collective-permute-done((bf16[4,4,64,256]{3,2,1,0:T(8,128)(2,1)S(1)}, bf16[4,4,64,256]{3,2,1,0:T(8,128)(2,1)S(1)}, u32[]{:S(2)}, u32[]{:S(2)}) %collective-permute-start.1) | collective-permute-done | bytes 524320 | tf_op jit(solution)/shard_map/ppermute | solution.py:224
  139.0 0.8 collective-permute-start.8
  139.8 0.4 convert_add_fusion.1
  140.2 7.2 %collective-permute-done.3 = bf16[4,4,64,256]{3,2,1,0:T(8,128)(2,1)S(1)} collective-permute-done((bf16[4,4,64,256]{3,2,1,0:T(8,128)(2,1)S(1)}, bf16[4,4,64,256]{3,2,1,0:T(8,128)(2,1)S(1)}, u32[]{:S(2)}, u32[]{:S(2)}) %collective-permute-start.3) | collective-permute-done | bytes 524320 | tf_op jit(solution)/shard_map/ppermute | solution.py:224
  147.4 2.5 %collective-permute-done.7 = bf16[4,4,64,256]{3,2,1,0:T(8,128)(2,1)} collective-permute-done((bf16[4,4,64,256]{3,2,1,0:T(8,128)(2,1)S(1)}, bf16[4,4,64,256]{3,2,1,0:T(8,128)(2,1)}, u32[]{:S(2)}, u32[]{:S(2)}) %collective-permute-start.7) | collective-permute-done | bytes 524320 | tf_op jit(solution)/shard_map/ppermute | solution.py:224
  149.9 2.3 %collective-permute-done.8 = bf16[4,4,64,256]{3,2,1,0:T(8,128)(2,1)} collective-permute-done((bf16[4,4,64,256]{3,2,1,0:T(8,128)(2,1)S(1)}, bf16[4,4,64,256]{3,2,1,0:T(8,128)(2,1)}, u32[]{:S(2)}, u32[]{:S(2)}) %collective-permute-start.8) | collective-permute-done | bytes 524320 | tf_op jit(solution)/shard_map/ppermute | solution.py:224
  152.2 1.7 add_convert_fusion
  153.9 1.0 collective-permute-start.13
  154.9 2.4 %collective-permute-start.15 = (bf16[4,64,256]{2,1,0:T(8,128)(2,1)S(1)}, bf16[4,64,256]{2,1,0:T(8,128)(2,1)S(1)}, u32[]{:S(2)}, u32[]{:S(2)}) collective-permute-start(bf16[4,64,256]{2,1,0:T(8,128)(2,1)S(1)} %get-tuple-element.52), channel_id=1, source_target_pairs={{0,3},{1,0},{2,1},{3,2},{4,7},{5,4},{6,5},{7,6},{8,11},{9,8},{10,9... | collective-permute-start | bytes 393224 | tf_op jit(solution)/shard_map/ppermute | solution.py:224
  157.2 0.9 collective-permute-start.14
  158.1 1.3 add_convert_fusion.1
  159.5 2.0 %collective-permute-start.10 = (bf16[4,64,256]{2,1,0:T(8,128)(2,1)S(1)}, bf16[4,64,256]{2,1,0:T(8,128)(2,1)S(1)}, u32[]{:S(2)}, u32[]{:S(2)}) collective-permute-start(bf16[4,64,256]{2,1,0:T(8,128)(2,1)S(1)} %get-tuple-element.48), channel_id=1, source_target_pairs={{0,128},{64,192},{128,0},{192,64},{1,129},{65,193},{129,1},{193,65... | collective-permute-start | bytes 393224 | tf_op jit(solution)/shard_map/ppermute | solution.py:224
  161.5 1.7 collective-permute-start.12
  163.2 0.3 collective-permute-start.11
  163.6 3.6 %collective-permute-done.10 = bf16[4,64,256]{2,1,0:T(8,128)(2,1)S(1)} collective-permute-done((bf16[4,64,256]{2,1,0:T(8,128)(2,1)S(1)}, bf16[4,64,256]{2,1,0:T(8,128)(2,1)S(1)}, u32[]{:S(2)}, u32[]{:S(2)}) %collective-permute-start.10) | collective-permute-done | bytes 131104 | tf_op jit(solution)/shard_map/ppermute | solution.py:224
  167.2 0.2 collective-permute-done.12
  167.4 2.0 %collective-permute-done.11 = bf16[4,64,256]{2,1,0:T(8,128)(2,1)S(1)} collective-permute-done((bf16[4,64,256]{2,1,0:T(8,128)(2,1)S(1)}, bf16[4,64,256]{2,1,0:T(8,128)(2,1)S(1)}, u32[]{:S(2)}, u32[]{:S(2)}) %collective-permute-start.11) | collective-permute-done | bytes 131104 | tf_op jit(solution)/shard_map/ppermute | solution.py:224
  169.5 0.7 pad_maximum_fusion
  170.2 7.1 %all-to-all-start.3 = ((bf16[8,64,256]{2,1,0:T(8,128)(2,1)}), bf16[8,64,256]{2,1,0:T(8,128)(2,1)S(1)}, u32[]{:S(2)}, u32[]{:S(2)}) async-start(bf16[8,64,256]{2,1,0:T(8,128)(2,1)} %pad_maximum_fusion), calls=%async_computation.3 | async-start | bytes 524288 | tf_op jit(solution)/shard_map/all_to_all | solution.py:219
  177.3 1.3 slice_bitcast_fusion
  178.6 0.8 copy.73
  179.5 0.8 copy.72
  180.3 7.5 %all-to-all-done.3 = bf16[8,64,256]{2,1,0:T(8,128)(2,1)S(1)} async-done(((bf16[8,64,256]{2,1,0:T(8,128)(2,1)}), bf16[8,64,256]{2,1,0:T(8,128)(2,1)S(1)}, u32[]{:S(2)}, u32[]{:S(2)}) %all-to-all-start.3) | async-done | bytes 262176 | tf_op jit(solution)/shard_map/all_to_all | solution.py:219
  187.9 0.7 copy.82
  188.6 0.7 copy.83
  (72 shorter events, 1.5 us)
Async XLA Ops:
  7.2 22.4 %copy-start.4 = (bf16[64,4096]{1,0:T(8,128)(2,1)S(1)}, bf16[64,4096]{1,0:T(8,128)(2,1)}, u32[]{:S(2)}) copy-start(bf16[64,4096]{1,0:T(8,128)(2,1)} %param.11) | copy-start | bytes 1572868
  7.2 22.4 %copy-start.5 = (bf16[64,4096]{1,0:T(8,128)(2,1)S(1)}, bf16[64,4096]{1,0:T(8,128)(2,1)}, u32[]{:S(2)}) copy-start(bf16[64,4096]{1,0:T(8,128)(2,1)} %param.8) | copy-start | bytes 1572868
  7.2 76.8 %all-gather.2.cloned.1.call-start = ((), (), s32[]{:S(2)}) async-start(), calls=%async_computation.4 | async-start | bytes 8650752 | tf_op jit(solution)/shard_map/all_gather | solution.py:260
  29.7 4.8 %copy-start.10 = (s32[4]{0:T(128)S(1)}, s32[4]{0:T(128)}, u32[]{:S(2)}) copy-start(s32[4]{0:T(128)} %param.13) | copy-start | bytes 52
  29.7 5.5 %copy-start.9 = (s32[4096,1]{0,1:T(1,128)S(1)}, s32[4096,1]{0,1:T(1,128)}, u32[]{:S(2)}) copy-start(s32[4096,1]{0,1:T(1,128)} %param.14) | copy-start | bytes 49156
  29.7 6.3 %copy-start.12 = (u32[256]{0:T(256)S(1)}, u32[256]{0:T(256)}, u32[]{:S(2)}) copy-start(u32[256]{0:T(256)} %constant.247) | copy-start | bytes 3076
  29.7 7.5 %copy-start.11 = (s32[4]{0:T(128)S(1)}, s32[4]{0:T(128)}, u32[]{:S(2)}) copy-start(s32[4]{0:T(128)} %param.12) | copy-start | bytes 52
  29.7 44.1 %copy-start.8 = (s32[4096]{0:T(1024)S(1)}, s32[4096]{0:T(1024)}, u32[]{:S(2)}) copy-start(s32[4096]{0:T(1024)} %param.15) | copy-start | bytes 49156
  30.9 46.5 %all-to-all-start = ((bf16[8,64,1024]{2,1,0:T(8,128)(2,1)}), bf16[8,64,1024]{2,1,0:T(8,128)(2,1)S(1)}, u32[]{:S(2)}, u32[]{:S(2)}) async-start(bf16[8,64,1024]{2,1,0:T(8,128)(2,1)} %maximum_bitcast_fusion), calls=%async_computation | async-start | bytes 2097152 | tf_op jit(solution)/shard_map/all_to_all | solution.py:219
  77.4 1.0 copy-start
  107.9 12.8 %collective-permute-start = (bf16[32,64,256]{2,1,0:T(8,128)(2,1)}, bf16[32,64,256]{2,1,0:T(8,128)(2,1)}, u32[]{:S(2)}, u32[]{:S(2)}) collective-permute-start(bf16[32,64,256]{2,1,0:T(8,128)(2,1)} %get-tuple-element.22), channel_id=1, source_target_pairs={{0,4},{4,0},{1,5},{5,1},{2,6},{6,2},{3,7},{7,3},{8,12},{12,8},{9,1... | collective-permute-start | bytes 3145736 | tf_op jit(solution)/shard_map/ppermute | solution.py:224
  113.0 12.6 %collective-permute-start.2 = (bf16[32,64,256]{2,1,0:T(8,128)(2,1)S(1)}, bf16[32,64,256]{2,1,0:T(8,128)(2,1)}, u32[]{:S(2)}, u32[]{:S(2)}) collective-permute-start(bf16[32,64,256]{2,1,0:T(8,128)(2,1)S(1)} %get-tuple-element.24), channel_id=1, source_target_pairs={{0,4},{4,0},{1,5},{5,1},{2,6},{6,2},{3,7},{7,3},{8,12},{12,8},{9,1... | collective-permute-start | bytes 3145736 | tf_op jit(solution)/shard_map/ppermute | solution.py:224
  113.1 16.2 %collective-permute-start.4 = (bf16[32,64,256]{2,1,0:T(8,128)(2,1)S(1)}, bf16[32,64,256]{2,1,0:T(8,128)(2,1)}, u32[]{:S(2)}, u32[]{:S(2)}) collective-permute-start(bf16[32,64,256]{2,1,0:T(8,128)(2,1)S(1)} %get-tuple-element.26), channel_id=1, source_target_pairs={{0,4},{4,0},{1,5},{5,1},{2,6},{6,2},{3,7},{7,3},{8,12},{12,8},{9,1... | collective-permute-start | bytes 3145736 | tf_op jit(solution)/shard_map/ppermute | solution.py:224
  113.5 38.7 %all-to-all-start.2 = ((bf16[8,64,1024]{2,1,0:T(8,128)(2,1)}), bf16[8,64,1024]{2,1,0:T(8,128)(2,1)}, u32[]{:S(2)}, u32[]{:S(2)}) async-start(bf16[8,64,1024]{2,1,0:T(8,128)(2,1)} %get-tuple-element.20), calls=%async_computation.2 | async-start | bytes 2097152 | tf_op jit(solution)/shard_map/all_to_all | solution.py:219
  120.5 5.0 %copy-start.2 = (bf16[32,64,256]{2,1,0:T(8,128)(2,1)S(1)}, bf16[32,64,256]{2,1,0:T(8,128)(2,1)}, u32[]{:S(2)}) copy-start(bf16[32,64,256]{2,1,0:T(8,128)(2,1)} %get-tuple-element.23) | copy-start | bytes 3145732
  120.5 10.4 %collective-permute-start.9 = (bf16[32,64,256]{2,1,0:T(8,128)(2,1)S(1)}, bf16[32,64,256]{2,1,0:T(8,128)(2,1)S(1)}, u32[]{:S(2)}, u32[]{:S(2)}) collective-permute-start(bf16[32,64,256]{2,1,0:T(8,128)(2,1)S(1)} %get-tuple-element.29), channel_id=1, source_target_pairs={{0,4},{4,0},{1,5},{5,1},{2,6},{6,2},{3,7},{7,3},{8,12},{12,8},{9,1... | collective-permute-start | bytes 3145736 | tf_op jit(solution)/shard_map/ppermute | solution.py:224
  122.6 6.7 %copy-start.1 = (bf16[32,64,256]{2,1,0:T(8,128)(2,1)S(1)}, bf16[32,64,256]{2,1,0:T(8,128)(2,1)}, u32[]{:S(2)}) copy-start(bf16[32,64,256]{2,1,0:T(8,128)(2,1)} %get-tuple-element.25) | copy-start | bytes 3145732
  122.6 16.4 %collective-permute-start.1 = (bf16[4,4,64,256]{3,2,1,0:T(8,128)(2,1)S(1)}, bf16[4,4,64,256]{3,2,1,0:T(8,128)(2,1)S(1)}, u32[]{:S(2)}, u32[]{:S(2)}) collective-permute-start(bf16[4,4,64,256]{3,2,1,0:T(8,128)(2,1)S(1)} %bitcast.123), channel_id=1, source_target_pairs={{0,2},{1,3},{2,0},{3,1},{4,6},{5,7},{6,4},{7,5},{8,10},{9,11},{10,... | collective-permute-start | bytes 1572872 | tf_op jit(solution)/shard_map/ppermute | solution.py:224
  122.7 17.4 %collective-permute-start.6 = (bf16[4,4,64,256]{3,2,1,0:T(8,128)(2,1)S(1)}, bf16[4,4,64,256]{3,2,1,0:T(8,128)(2,1)}, u32[]{:S(2)}, u32[]{:S(2)}) collective-permute-start(bf16[4,4,64,256]{3,2,1,0:T(8,128)(2,1)S(1)} %bitcast.120), channel_id=1, source_target_pairs={{0,128},{64,192},{128,0},{192,64},{1,129},{65,193},{129,1},{193,65... | collective-permute-start | bytes 1572872 | tf_op jit(solution)/shard_map/ppermute | solution.py:224
  127.2 12.6 %copy-start.3 = (bf16[32,64,256]{2,1,0:T(8,128)(2,1)S(1)}, bf16[32,64,256]{2,1,0:T(8,128)(2,1)}, u32[]{:S(2)}) copy-start(bf16[32,64,256]{2,1,0:T(8,128)(2,1)} %get-tuple-element.28) | copy-start | bytes 3145732
  127.2 20.2 %collective-permute-start.3 = (bf16[4,4,64,256]{3,2,1,0:T(8,128)(2,1)S(1)}, bf16[4,4,64,256]{3,2,1,0:T(8,128)(2,1)S(1)}, u32[]{:S(2)}, u32[]{:S(2)}) collective-permute-start(bf16[4,4,64,256]{3,2,1,0:T(8,128)(2,1)S(1)} %bitcast.122), channel_id=1, source_target_pairs={{0,1},{1,2},{2,3},{3,0},{4,5},{5,6},{6,7},{7,4},{8,9},{9,10},{10,1... | collective-permute-start | bytes 1572872 | tf_op jit(solution)/shard_map/ppermute | solution.py:224
  129.3 20.6 %collective-permute-start.7 = (bf16[4,4,64,256]{3,2,1,0:T(8,128)(2,1)S(1)}, bf16[4,4,64,256]{3,2,1,0:T(8,128)(2,1)}, u32[]{:S(2)}, u32[]{:S(2)}) collective-permute-start(bf16[4,4,64,256]{3,2,1,0:T(8,128)(2,1)S(1)} %bitcast.121), channel_id=1, source_target_pairs={{0,64},{64,128},{128,192},{192,0},{1,65},{65,129},{129,193},{193,1... | collective-permute-start | bytes 1572872 | tf_op jit(solution)/shard_map/ppermute | solution.py:224
  130.9 19.0 %collective-permute-start.5 = (bf16[4,4,64,256]{3,2,1,0:T(8,128)(2,1)S(1)}, bf16[4,4,64,256]{3,2,1,0:T(8,128)(2,1)}, u32[]{:S(2)}, u32[]{:S(2)}) collective-permute-start(bf16[4,4,64,256]{3,2,1,0:T(8,128)(2,1)S(1)} %bitcast.125), channel_id=1, source_target_pairs={{0,3},{1,0},{2,1},{3,2},{4,7},{5,4},{6,5},{7,6},{8,11},{9,8},{10,9... | collective-permute-start | bytes 1572872 | tf_op jit(solution)/shard_map/ppermute | solution.py:224
  139.0 1.2 copy-start.6
  139.0 13.2 %collective-permute-start.8 = (bf16[4,4,64,256]{3,2,1,0:T(8,128)(2,1)S(1)}, bf16[4,4,64,256]{3,2,1,0:T(8,128)(2,1)}, u32[]{:S(2)}, u32[]{:S(2)}) collective-permute-start(bf16[4,4,64,256]{3,2,1,0:T(8,128)(2,1)S(1)} %bitcast.124), channel_id=1, source_target_pairs={{0,192},{64,0},{128,64},{192,128},{1,193},{65,1},{129,65},{193,129... | collective-permute-start | bytes 1572872 | tf_op jit(solution)/shard_map/ppermute | solution.py:224
  140.2 18.0 %copy-start.7 = (bf16[4,4,64,256]{3,2,1,0:T(8,128)(2,1)S(1)}, bf16[4,4,64,256]{3,2,1,0:T(8,128)(2,1)}, u32[]{:S(2)}) copy-start(bf16[4,4,64,256]{3,2,1,0:T(8,128)(2,1)} %copy-done.6) | copy-start | bytes 1572868
  153.9 9.3 %collective-permute-start.13 = (bf16[4,64,256]{2,1,0:T(8,128)(2,1)S(1)}, bf16[4,64,256]{2,1,0:T(8,128)(2,1)S(1)}, u32[]{:S(2)}, u32[]{:S(2)}) collective-permute-start(bf16[4,64,256]{2,1,0:T(8,128)(2,1)S(1)} %get-tuple-element.51), channel_id=1, source_target_pairs={{0,2},{1,3},{2,0},{3,1},{4,6},{5,7},{6,4},{7,5},{8,10},{9,11},{10,... | collective-permute-start | bytes 393224 | tf_op jit(solution)/shard_map/ppermute | solution.py:224
  154.9 8.7 %collective-permute-start.15 = (bf16[4,64,256]{2,1,0:T(8,128)(2,1)S(1)}, bf16[4,64,256]{2,1,0:T(8,128)(2,1)S(1)}, u32[]{:S(2)}, u32[]{:S(2)}) collective-permute-start(bf16[4,64,256]{2,1,0:T(8,128)(2,1)S(1)} %get-tuple-element.52), channel_id=1, source_target_pairs={{0,3},{1,0},{2,1},{3,2},{4,7},{5,4},{6,5},{7,6},{8,11},{9,8},{10,9... | collective-permute-start | bytes 393224 | tf_op jit(solution)/shard_map/ppermute | solution.py:224
  157.2 6.3 %collective-permute-start.14 = (bf16[4,64,256]{2,1,0:T(8,128)(2,1)S(1)}, bf16[4,64,256]{2,1,0:T(8,128)(2,1)S(1)}, u32[]{:S(2)}, u32[]{:S(2)}) collective-permute-start(bf16[4,64,256]{2,1,0:T(8,128)(2,1)S(1)} %get-tuple-element.53), channel_id=1, source_target_pairs={{0,1},{1,2},{2,3},{3,0},{4,5},{5,6},{6,7},{7,4},{8,9},{9,10},{10,1... | collective-permute-start | bytes 393224 | tf_op jit(solution)/shard_map/ppermute | solution.py:224
  159.5 7.7 %collective-permute-start.10 = (bf16[4,64,256]{2,1,0:T(8,128)(2,1)S(1)}, bf16[4,64,256]{2,1,0:T(8,128)(2,1)S(1)}, u32[]{:S(2)}, u32[]{:S(2)}) collective-permute-start(bf16[4,64,256]{2,1,0:T(8,128)(2,1)S(1)} %get-tuple-element.48), channel_id=1, source_target_pairs={{0,128},{64,192},{128,0},{192,64},{1,129},{65,193},{129,1},{193,65... | collective-permute-start | bytes 393224 | tf_op jit(solution)/shard_map/ppermute | solution.py:224
  161.5 5.9 %collective-permute-start.12 = (bf16[4,64,256]{2,1,0:T(8,128)(2,1)S(1)}, bf16[4,64,256]{2,1,0:T(8,128)(2,1)S(1)}, u32[]{:S(2)}, u32[]{:S(2)}) collective-permute-start(bf16[4,64,256]{2,1,0:T(8,128)(2,1)S(1)} %get-tuple-element.49), channel_id=1, source_target_pairs={{0,192},{64,0},{128,64},{192,128},{1,193},{65,1},{129,65},{193,129... | collective-permute-start | bytes 393224 | tf_op jit(solution)/shard_map/ppermute | solution.py:224
  163.2 6.2 %collective-permute-start.11 = (bf16[4,64,256]{2,1,0:T(8,128)(2,1)S(1)}, bf16[4,64,256]{2,1,0:T(8,128)(2,1)S(1)}, u32[]{:S(2)}, u32[]{:S(2)}) collective-permute-start(bf16[4,64,256]{2,1,0:T(8,128)(2,1)S(1)} %get-tuple-element.50), channel_id=1, source_target_pairs={{0,64},{64,128},{128,192},{192,0},{1,65},{65,129},{129,193},{193,1... | collective-permute-start | bytes 393224 | tf_op jit(solution)/shard_map/ppermute | solution.py:224
  170.2 17.6 %all-to-all-start.3 = ((bf16[8,64,256]{2,1,0:T(8,128)(2,1)}), bf16[8,64,256]{2,1,0:T(8,128)(2,1)S(1)}, u32[]{:S(2)}, u32[]{:S(2)}) async-start(bf16[8,64,256]{2,1,0:T(8,128)(2,1)} %pad_maximum_fusion), calls=%async_computation.3 | async-start | bytes 524288 | tf_op jit(solution)/shard_map/all_to_all | solution.py:219
Sparse Core Ops, SparseCore 0:
  29.7 54.2 all-gather.1

commit v5 on v4

--- a/solution.py
+++ b/solution.py
@@ -81,7 +81,7 @@
     load.start()
     acc[...] = jnp.zeros_like(acc)
     load.wait()
-    key_at = lax.broadcasted_iota(jnp.int32, (TILE, ROWS), 0)
+    key_at = lax.broadcasted_iota(jnp.int32, (TILE, ROWS), 0).astype(jnp.float32)
     lane = lax.broadcasted_iota(jnp.int32, (1, ROWS), 1) & (TILE - 1)
 
     def stacked(s, start):
@@ -118,7 +118,7 @@
                 for j, f in enumerate(found):
                     base = (f // (TILES * TILES) - 1) * TILE
                     part = raw[j * TILE:(j + 1) * TILE]
-                    part = jnp.where((key_at <= q_pos - base) & (key_at >= low - base), part, NEG)
+                    part = jnp.where((key_at <= (q_pos - base).astype(jnp.float32)) & (key_at >= (low - base).astype(jnp.float32)), part, NEG)
                     st[i, c, j * TILE:(j + 1) * TILE, :] = part
                     top = jnp.maximum(top, jnp.max(part.reshape(TILE // 8, 8, ROWS), axis=0))
                 new.append(top)
@@ -257,7 +257,9 @@
         blocks = blocks.transpose(1, 0, 2)
         return [blocks[:, :, i * width:(i + 1) * width].reshape(TILE, KV_HEADS * width) for i in range(2)]
 
-    kv = lax.all_gather(by_head(keys, values, HEAD), ("x", "y", "core"), axis=0, tiled=True)
+    cuts = [slice(h * HEAD, (h + 1) * HEAD) for h in range(KV_HEADS)]
+    block = jnp.stack([jnp.concatenate([keys[:, cut], values[:, cut]], axis=1) for cut in cuts])
+    kv = lax.all_gather(exchange(block, "z"), ("x", "y", "core"), axis=0, tiled=True)
     kv = kv.reshape(TILES, TILE, 2 * HEAD)
     qg = by_head(queries, output_cotangent, WIDE)
     od, *terms = attention(*lists, qg, kv)

time: 198 us -> 196 us (0.990)
  starting transfers between devices: 38.2 us -> 44.9 us
  waiting for transfers between devices: 38.3 us -> 33.7 us
  Pallas kernels: 23.9 us -> 20.9 us
    ppermute x16, starting transfers between devices: 20.4 us -> 27.2 us  [shift(): lax.ppermute(array, axis, [(i, (i + by) % size) for i in range(size)])]
    ppermute x16, waiting for transfers between devices: 25.3 us -> 20.7 us  [shift(): lax.ppermute(array, axis, [(i, (i + by) % size) for i in range(size)])]
    pallas_call x1, Pallas kernels: 23.9 us -> 20.9 us  [attention(): pl.pallas_call(attend, out_shape=(jax.ShapeDtypeStruct((NZ, TILE, 2 * WID...]
    unnamed x34 -> x32, local copies, waits for them, and re-layouts: 5.66 us -> 3.72 us
  transfers between devices with their start and end apart: 20 -> 20, of which waited for: 9 -> 10; matrix products, arithmetic and copies ran while one was open for 9% -> 9% of each run, Pallas kernels for 0% -> 0%
where the time goes in v5:
time: 196 us; the launch traced here: 194 us
  blocking collectives  56.4 us (29%)
  starting transfers between devices  44.9 us (23%)
  waiting for transfers between devices  33.7 us (17%)
  Pallas kernels  20.9 us (11%)
  between operations  15.3 us (8%)
  other arithmetic  13.5 us (7%)
  local copies, waits for them, and re-layouts  9.64 us (5%)
    unnamed x1, blocking collectives  36.2 us
    ppermute x16, starting transfers between devices, shift(): lax.ppermute(array, axis, [(i, (i + by) % size) for i in range(size)])  27.2 us
    pallas_call x1, Pallas kernels, attention(): pl.pallas_call(attend, out_shape=(jax.ShapeDtypeStruct((NZ, TILE, 2 * WID...  20.9 us
    ppermute x16, waiting for transfers between devices, shift(): lax.ppermute(array, axis, [(i, (i + by) % size) for i in range(size)])  20.7 us
    all_to_all x1, blocking collectives, exchange(): return lax.all_to_all(blocks, axes, split_axis=0, concat_axis=0, tiled=True)  20.2 us
    all_to_all x3, starting transfers between devices, exchange(): return lax.all_to_all(blocks, axes, split_axis=0, concat_axis=0, tiled=True)  17.6 us
    convert_element_type x7, other arithmetic, added(): return sum((a.astype(jnp.float32) for a in arrays)).astype(jnp.bfloat16)  8.28 us
    all_to_all x3, waiting for transfers between devices, exchange(): return lax.all_to_all(blocks, axes, split_axis=0, concat_axis=0, tiled=True)  7.51 us
  transfers between devices with their start and end apart: 20, of which 10 were waited for; matrix products, arithmetic and copies ran while one was open for 9% of the time, Pallas kernels for 0%

profile of v5, /device:TPU:6, one launch (start us, length us, event | category | flops | bytes accessed | tf_op | source)
XLA Modules:
  0.0 194.3 jit_solution(14172329310016228358)
XLA Ops:
  7.2 1.0 fusion.32
  8.3 20.2 %all_to_all.20 = bf16[8,64,256]{2,1,0:T(8,128)(2,1)} all-to-all(bf16[8,64,256]{2,1,0:T(8,128)(2,1)S(1)} %fusion.22), channel_id=1, replica_groups=mesh['y'=4,'z'=8,'core'=2,'x'=4] {'z'}, dimensions={0} | all-to-all | bytes 524288 | tf_op jit(solution)/shard_map/all_to_all | solution.py:219
  28.8 1.2 maximum_bitcast_fusion
  30.0 3.6 %all-to-all-start = ((bf16[8,64,1024]{2,1,0:T(8,128)(2,1)}), bf16[8,64,1024]{2,1,0:T(8,128)(2,1)S(1)}, u32[]{:S(2)}, u32[]{:S(2)}) async-start(bf16[8,64,1024]{2,1,0:T(8,128)(2,1)} %maximum_bitcast_fusion), calls=%async_computation | async-start | bytes 2097152 | tf_op jit(solution)/shard_map/all_to_all | solution.py:219
  33.6 0.2 reduce-window.18
  33.7 0.5 broadcast.197
  34.3 0.7 reduce.9
  35.1 0.6 dynamic-slice.7
  36.3 0.2 dynamic-update-slice
  36.6 36.2 %all-reduce = s32[256]{0:T(256)S(1)} all-reduce(s32[256]{0:T(256)S(1)} %dynamic-update-slice), channel_id=1, replica_groups=mesh['y'=4,'z'=8,'core'=2,'x'=4] {'y','z','core'}, use_global_device_ids=true, to_apply=%add | all-reduce | flops 256 | bytes 2048
  72.7 0.1 reshape.343
  73.0 0.2 select_reduce_fusion.1
  73.4 0.1 sub.91
  73.5 0.1 sub.85
  73.6 0.3 dynamic-slice_reduce_fusion.own
  74.2 0.2 fusion.10
  74.4 0.6 reduce-window.19
  75.0 0.2 slice_reduce_fusion
  75.3 0.1 copy.46
  75.5 0.2 fusion.14
  75.7 0.2 slice_reduce_fusion.1.counts
  75.9 0.2 convert_reduce_fusion.1
  76.1 0.1 select_reduce_fusion.2.turns
  76.2 0.3 select_reduce_fusion.codes
  76.5 1.0 copy-done
  77.5 5.5 %all-gather.2.cloned.1.call-done.kv_hbm = bf16[256,64,256]{2,1,0:T(8,128)(2,1)} async-done(((bf16[8,64,256]{2,1,0:T(8,128)(2,1)}), bf16[256,64,256]{2,1,0:T(8,128)(2,1)}) %all-gather.2.cloned.1.call-update) | async-done | bytes 8388624 | tf_op jit(solution)/shard_map/all_gather | solution.py:262
  83.0 20.9 %attend.1 = (bf16[8,64,1024]{2,1,0:T(8,128)(2,1)}, bf16[32,64,256]{2,1,0:T(8,128)(2,1)S(1)}, bf16[32,64,256]{2,1,0:T(8,128)(2,1)S(1)}, bf16[32,64,256]{2,1,0:T(8...) custom-call(s32[8,72]{1,0:T(8,128)S(1)} %select_reduce_fusion.codes,, ...), custom_call_target="tpu_custom_call" | custom-call | tf_op jit(solution)/shard_map/attend/pallas_call | solution.py:202
  103.9 4.8 %collective-permute-start = (bf16[32,64,256]{2,1,0:T(8,128)(2,1)}, bf16[32,64,256]{2,1,0:T(8,128)(2,1)}, u32[]{:S(2)}, u32[]{:S(2)}) collective-permute-start(bf16[32,64,256]{2,1,0:T(8,128)(2,1)} %get-tuple-element.22), channel_id=1, source_target_pairs={{0,4},{4,0},{1,5},{5,1},{2,6},{6,2},{3,7},{7,3},{8,12},{12,8},{9,1... | collective-permute-start | bytes 3145736 | tf_op jit(solution)/shard_map/ppermute | solution.py:224
  108.8 0.1 collective-permute-start.2
  108.9 0.4 collective-permute-start.4
  109.3 7.0 %all-to-all-start.2 = ((bf16[8,64,1024]{2,1,0:T(8,128)(2,1)}), bf16[8,64,1024]{2,1,0:T(8,128)(2,1)}, u32[]{:S(2)}, u32[]{:S(2)}) async-start(bf16[8,64,1024]{2,1,0:T(8,128)(2,1)} %get-tuple-element.20), calls=%async_computation.2 | async-start | bytes 2097152 | tf_op jit(solution)/shard_map/all_to_all | solution.py:219
  116.4 2.0 %add_convert_fusion.4 = (bf16[16,64,256]{2,1,0:T(8,128)(2,1)S(1)}, bf16[16,64,256]{2,1,0:T(8,128)(2,1)S(1)}) fusion(bf16[32,64,256]{2,1,0:T(8,128)(2,1)} %collective-permute-done, bf16[32,64,256]{2,1,0:T(8,128)(2,1)} %get-tuple-element.21), kind=kLoop, calls=%fused_computation.7 | loop fusion | flops 2097152 | bytes 3145728 | tf_op jit(solution)/shard_map/convert_element_type | solution.py:228
  118.3 1.5 collective-permute-start.1
  119.9 3.7 %collective-permute-start.6 = (bf16[4,4,64,256]{3,2,1,0:T(8,128)(2,1)S(1)}, bf16[4,4,64,256]{3,2,1,0:T(8,128)(2,1)}, u32[]{:S(2)}, u32[]{:S(2)}) collective-permute-start(bf16[4,4,64,256]{3,2,1,0:T(8,128)(2,1)S(1)} %bitcast.144), channel_id=1, source_target_pairs={{0,128},{64,192},{128,0},{192,64},{1,129},{65,193},{129,1},{193,65... | collective-permute-start | bytes 1572872 | tf_op jit(solution)/shard_map/ppermute | solution.py:224
  123.6 1.6 add_convert_fusion.3
  125.2 0.6 collective-permute-start.3
  125.8 4.1 %collective-permute-start.7 = (bf16[4,4,64,256]{3,2,1,0:T(8,128)(2,1)S(1)}, bf16[4,4,64,256]{3,2,1,0:T(8,128)(2,1)}, u32[]{:S(2)}, u32[]{:S(2)}) collective-permute-start(bf16[4,4,64,256]{3,2,1,0:T(8,128)(2,1)S(1)} %bitcast.145), channel_id=1, source_target_pairs={{0,64},{64,128},{128,192},{192,0},{1,65},{65,129},{129,193},{193,1... | collective-permute-start | bytes 1572872 | tf_op jit(solution)/shard_map/ppermute | solution.py:224
  129.9 1.6 add_convert_fusion.2
  131.6 3.1 %collective-permute-done.1 = bf16[4,4,64,256]{3,2,1,0:T(8,128)(2,1)S(1)} collective-permute-done((bf16[4,4,64,256]{3,2,1,0:T(8,128)(2,1)S(1)}, bf16[4,4,64,256]{3,2,1,0:T(8,128)(2,1)S(1)}, u32[]{:S(2)}, u32[]{:S(2)}) %collective-permute-start.1) | collective-permute-done | bytes 524320 | tf_op jit(solution)/shard_map/ppermute | solution.py:224
  134.7 0.9 collective-permute-start.8
  135.6 0.4 convert_add_fusion.1
  135.9 0.5 collective-permute-done.6
  136.4 6.9 %collective-permute-done.3 = bf16[4,4,64,256]{3,2,1,0:T(8,128)(2,1)S(1)} collective-permute-done((bf16[4,4,64,256]{3,2,1,0:T(8,128)(2,1)S(1)}, bf16[4,4,64,256]{3,2,1,0:T(8,128)(2,1)S(1)}, u32[]{:S(2)}, u32[]{:S(2)}) %collective-permute-start.3) | collective-permute-done | bytes 524320 | tf_op jit(solution)/shard_map/ppermute | solution.py:224
  143.4 3.8 %collective-permute-done.7 = bf16[4,4,64,256]{3,2,1,0:T(8,128)(2,1)} collective-permute-done((bf16[4,4,64,256]{3,2,1,0:T(8,128)(2,1)S(1)}, bf16[4,4,64,256]{3,2,1,0:T(8,128)(2,1)}, u32[]{:S(2)}, u32[]{:S(2)}) %collective-permute-start.7) | collective-permute-done | bytes 524320 | tf_op jit(solution)/shard_map/ppermute | solution.py:224
  147.2 1.0 collective-permute-done.8
  148.2 1.7 add_convert_fusion
  149.9 0.9 collective-permute-start.13
  150.8 4.0 %collective-permute-start.15 = (bf16[4,64,256]{2,1,0:T(8,128)(2,1)S(1)}, bf16[4,64,256]{2,1,0:T(8,128)(2,1)S(1)}, u32[]{:S(2)}, u32[]{:S(2)}) collective-permute-start(bf16[4,64,256]{2,1,0:T(8,128)(2,1)S(1)} %get-tuple-element.52), channel_id=1, source_target_pairs={{0,3},{1,0},{2,1},{3,2},{4,7},{5,4},{6,5},{7,6},{8,11},{9,8},{10,9... | collective-permute-start | bytes 393224 | tf_op jit(solution)/shard_map/ppermute | solution.py:224
  154.8 1.2 collective-permute-start.14
  156.0 1.3 add_convert_fusion.1
  157.4 2.4 %collective-permute-start.10 = (bf16[4,64,256]{2,1,0:T(8,128)(2,1)S(1)}, bf16[4,64,256]{2,1,0:T(8,128)(2,1)S(1)}, u32[]{:S(2)}, u32[]{:S(2)}) collective-permute-start(bf16[4,64,256]{2,1,0:T(8,128)(2,1)S(1)} %get-tuple-element.48), channel_id=1, source_target_pairs={{0,128},{64,192},{128,0},{192,64},{1,129},{65,193},{129,1},{193,65... | collective-permute-start | bytes 393224 | tf_op jit(solution)/shard_map/ppermute | solution.py:224
  159.8 1.6 collective-permute-start.12
  161.4 0.8 collective-permute-start.11
  162.2 3.0 %collective-permute-done.10 = bf16[4,64,256]{2,1,0:T(8,128)(2,1)S(1)} collective-permute-done((bf16[4,64,256]{2,1,0:T(8,128)(2,1)S(1)}, bf16[4,64,256]{2,1,0:T(8,128)(2,1)S(1)}, u32[]{:S(2)}, u32[]{:S(2)}) %collective-permute-start.10) | collective-permute-done | bytes 131104 | tf_op jit(solution)/shard_map/ppermute | solution.py:224
  165.2 1.3 collective-permute-done.12
  166.5 1.0 collective-permute-done.11
  167.7 0.7 pad_maximum_fusion
  168.4 7.1 %all-to-all-start.3 = ((bf16[8,64,256]{2,1,0:T(8,128)(2,1)}), bf16[8,64,256]{2,1,0:T(8,128)(2,1)S(1)}, u32[]{:S(2)}, u32[]{:S(2)}) async-start(bf16[8,64,256]{2,1,0:T(8,128)(2,1)} %pad_maximum_fusion), calls=%async_computation.3 | async-start | bytes 524288 | tf_op jit(solution)/shard_map/all_to_all | solution.py:219
  175.5 1.3 slice_bitcast_fusion
  176.8 0.8 copy.57
  177.6 0.8 copy.56
  178.5 7.5 %all-to-all-done.3 = bf16[8,64,256]{2,1,0:T(8,128)(2,1)S(1)} async-done(((bf16[8,64,256]{2,1,0:T(8,128)(2,1)}), bf16[8,64,256]{2,1,0:T(8,128)(2,1)S(1)}, u32[]{:S(2)}, u32[]{:S(2)}) %all-to-all-start.3) | async-done | bytes 262176 | tf_op jit(solution)/shard_map/all_to_all | solution.py:219
  186.1 0.7 copy.64
  186.7 0.7 copy.65
  (77 shorter events, 1.6 us)
Async XLA Ops:
  7.2 21.4 %copy-start.4 = (bf16[64,4096]{1,0:T(8,128)(2,1)S(1)}, bf16[64,4096]{1,0:T(8,128)(2,1)}, u32[]{:S(2)}) copy-start(bf16[64,4096]{1,0:T(8,128)(2,1)} %param.11) | copy-start | bytes 1572868
  7.2 21.4 %copy-start.5 = (bf16[64,4096]{1,0:T(8,128)(2,1)S(1)}, bf16[64,4096]{1,0:T(8,128)(2,1)}, u32[]{:S(2)}) copy-start(bf16[64,4096]{1,0:T(8,128)(2,1)} %param.8) | copy-start | bytes 1572868
  7.2 75.8 %all-gather.2.cloned.1.call-start = ((), (), s32[]{:S(2)}) async-start(), calls=%async_computation.4 | async-start | bytes 8650752 | tf_op jit(solution)/shard_map/all_gather | solution.py:262
  28.7 4.8 %copy-start.10 = (s32[4]{0:T(128)S(1)}, s32[4]{0:T(128)}, u32[]{:S(2)}) copy-start(s32[4]{0:T(128)} %param.13) | copy-start | bytes 52
  28.7 5.5 %copy-start.9 = (s32[4096,1]{0,1:T(1,128)S(1)}, s32[4096,1]{0,1:T(1,128)}, u32[]{:S(2)}) copy-start(s32[4096,1]{0,1:T(1,128)} %param.14) | copy-start | bytes 49156
  28.7 6.3 %copy-start.12 = (u32[256]{0:T(256)S(1)}, u32[256]{0:T(256)}, u32[]{:S(2)}) copy-start(u32[256]{0:T(256)} %constant.247) | copy-start | bytes 3076
  28.8 7.6 %copy-start.11 = (s32[4]{0:T(128)S(1)}, s32[4]{0:T(128)}, u32[]{:S(2)}) copy-start(s32[4]{0:T(128)} %param.12) | copy-start | bytes 52
  28.8 44.1 %copy-start.8 = (s32[4096]{0:T(1024)S(1)}, s32[4096]{0:T(1024)}, u32[]{:S(2)}) copy-start(s32[4096]{0:T(1024)} %param.15) | copy-start | bytes 49156
  30.0 46.5 %all-to-all-start = ((bf16[8,64,1024]{2,1,0:T(8,128)(2,1)}), bf16[8,64,1024]{2,1,0:T(8,128)(2,1)S(1)}, u32[]{:S(2)}, u32[]{:S(2)}) async-start(bf16[8,64,1024]{2,1,0:T(8,128)(2,1)} %maximum_bitcast_fusion), calls=%async_computation | async-start | bytes 2097152 | tf_op jit(solution)/shard_map/all_to_all | solution.py:219
  76.5 1.0 copy-start
  103.9 12.4 %collective-permute-start = (bf16[32,64,256]{2,1,0:T(8,128)(2,1)}, bf16[32,64,256]{2,1,0:T(8,128)(2,1)}, u32[]{:S(2)}, u32[]{:S(2)}) collective-permute-start(bf16[32,64,256]{2,1,0:T(8,128)(2,1)} %get-tuple-element.22), channel_id=1, source_target_pairs={{0,4},{4,0},{1,5},{5,1},{2,6},{6,2},{3,7},{7,3},{8,12},{12,8},{9,1... | collective-permute-start | bytes 3145736 | tf_op jit(solution)/shard_map/ppermute | solution.py:224
  108.8 14.8 %collective-permute-start.2 = (bf16[32,64,256]{2,1,0:T(8,128)(2,1)S(1)}, bf16[32,64,256]{2,1,0:T(8,128)(2,1)}, u32[]{:S(2)}, u32[]{:S(2)}) collective-permute-start(bf16[32,64,256]{2,1,0:T(8,128)(2,1)S(1)} %get-tuple-element.24), channel_id=1, source_target_pairs={{0,4},{4,0},{1,5},{5,1},{2,6},{6,2},{3,7},{7,3},{8,12},{12,8},{9,1... | collective-permute-start | bytes 3145736 | tf_op jit(solution)/shard_map/ppermute | solution.py:224
  108.9 16.9 %collective-permute-start.4 = (bf16[32,64,256]{2,1,0:T(8,128)(2,1)S(1)}, bf16[32,64,256]{2,1,0:T(8,128)(2,1)}, u32[]{:S(2)}, u32[]{:S(2)}) collective-permute-start(bf16[32,64,256]{2,1,0:T(8,128)(2,1)S(1)} %get-tuple-element.26), channel_id=1, source_target_pairs={{0,4},{4,0},{1,5},{5,1},{2,6},{6,2},{3,7},{7,3},{8,12},{12,8},{9,1... | collective-permute-start | bytes 3145736 | tf_op jit(solution)/shard_map/ppermute | solution.py:224
  109.3 38.9 %all-to-all-start.2 = ((bf16[8,64,1024]{2,1,0:T(8,128)(2,1)}), bf16[8,64,1024]{2,1,0:T(8,128)(2,1)}, u32[]{:S(2)}, u32[]{:S(2)}) async-start(bf16[8,64,1024]{2,1,0:T(8,128)(2,1)} %get-tuple-element.20), calls=%async_computation.2 | async-start | bytes 2097152 | tf_op jit(solution)/shard_map/all_to_all | solution.py:219
  116.3 7.3 %copy-start.2 = (bf16[32,64,256]{2,1,0:T(8,128)(2,1)S(1)}, bf16[32,64,256]{2,1,0:T(8,128)(2,1)}, u32[]{:S(2)}) copy-start(bf16[32,64,256]{2,1,0:T(8,128)(2,1)} %get-tuple-element.23) | copy-start | bytes 3145732
  116.3 15.2 %collective-permute-start.9 = (bf16[32,64,256]{2,1,0:T(8,128)(2,1)S(1)}, bf16[32,64,256]{2,1,0:T(8,128)(2,1)S(1)}, u32[]{:S(2)}, u32[]{:S(2)}) collective-permute-start(bf16[32,64,256]{2,1,0:T(8,128)(2,1)S(1)} %get-tuple-element.29), channel_id=1, source_target_pairs={{0,4},{4,0},{1,5},{5,1},{2,6},{6,2},{3,7},{7,3},{8,12},{12,8},{9,1... | collective-permute-start | bytes 3145736 | tf_op jit(solution)/shard_map/ppermute | solution.py:224
  118.3 11.5 %copy-start.1 = (bf16[32,64,256]{2,1,0:T(8,128)(2,1)S(1)}, bf16[32,64,256]{2,1,0:T(8,128)(2,1)}, u32[]{:S(2)}) copy-start(bf16[32,64,256]{2,1,0:T(8,128)(2,1)} %get-tuple-element.25) | copy-start | bytes 3145732
  118.3 16.3 %collective-permute-start.1 = (bf16[4,4,64,256]{3,2,1,0:T(8,128)(2,1)S(1)}, bf16[4,4,64,256]{3,2,1,0:T(8,128)(2,1)S(1)}, u32[]{:S(2)}, u32[]{:S(2)}) collective-permute-start(bf16[4,4,64,256]{3,2,1,0:T(8,128)(2,1)S(1)} %bitcast.147), channel_id=1, source_target_pairs={{0,2},{1,3},{2,0},{3,1},{4,6},{5,7},{6,4},{7,5},{8,10},{9,11},{10,... | collective-permute-start | bytes 1572872 | tf_op jit(solution)/shard_map/ppermute | solution.py:224
  119.9 16.6 %collective-permute-start.6 = (bf16[4,4,64,256]{3,2,1,0:T(8,128)(2,1)S(1)}, bf16[4,4,64,256]{3,2,1,0:T(8,128)(2,1)}, u32[]{:S(2)}, u32[]{:S(2)}) collective-permute-start(bf16[4,4,64,256]{3,2,1,0:T(8,128)(2,1)S(1)} %bitcast.144), channel_id=1, source_target_pairs={{0,128},{64,192},{128,0},{192,64},{1,129},{65,193},{129,1},{193,65... | collective-permute-start | bytes 1572872 | tf_op jit(solution)/shard_map/ppermute | solution.py:224
  125.2 10.4 %copy-start.3 = (bf16[32,64,256]{2,1,0:T(8,128)(2,1)S(1)}, bf16[32,64,256]{2,1,0:T(8,128)(2,1)}, u32[]{:S(2)}) copy-start(bf16[32,64,256]{2,1,0:T(8,128)(2,1)} %get-tuple-element.28) | copy-start | bytes 3145732
  125.2 18.2 %collective-permute-start.3 = (bf16[4,4,64,256]{3,2,1,0:T(8,128)(2,1)S(1)}, bf16[4,4,64,256]{3,2,1,0:T(8,128)(2,1)S(1)}, u32[]{:S(2)}, u32[]{:S(2)}) collective-permute-start(bf16[4,4,64,256]{3,2,1,0:T(8,128)(2,1)S(1)} %bitcast.146), channel_id=1, source_target_pairs={{0,1},{1,2},{2,3},{3,0},{4,5},{5,6},{6,7},{7,4},{8,9},{9,10},{10,1... | collective-permute-start | bytes 1572872 | tf_op jit(solution)/shard_map/ppermute | solution.py:224
  125.8 21.4 %collective-permute-start.7 = (bf16[4,4,64,256]{3,2,1,0:T(8,128)(2,1)S(1)}, bf16[4,4,64,256]{3,2,1,0:T(8,128)(2,1)}, u32[]{:S(2)}, u32[]{:S(2)}) collective-permute-start(bf16[4,4,64,256]{3,2,1,0:T(8,128)(2,1)S(1)} %bitcast.145), channel_id=1, source_target_pairs={{0,64},{64,128},{128,192},{192,0},{1,65},{65,129},{129,193},{193,1... | collective-permute-start | bytes 1572872 | tf_op jit(solution)/shard_map/ppermute | solution.py:224
  131.5 15.7 %collective-permute-start.5 = (bf16[4,4,64,256]{3,2,1,0:T(8,128)(2,1)S(1)}, bf16[4,4,64,256]{3,2,1,0:T(8,128)(2,1)}, u32[]{:S(2)}, u32[]{:S(2)}) collective-permute-start(bf16[4,4,64,256]{3,2,1,0:T(8,128)(2,1)S(1)} %bitcast.149), channel_id=1, source_target_pairs={{0,3},{1,0},{2,1},{3,2},{4,7},{5,4},{6,5},{7,6},{8,11},{9,8},{10,9... | collective-permute-start | bytes 1572872 | tf_op jit(solution)/shard_map/ppermute | solution.py:224
  134.7 1.3 copy-start.6
  134.7 13.5 %collective-permute-start.8 = (bf16[4,4,64,256]{3,2,1,0:T(8,128)(2,1)S(1)}, bf16[4,4,64,256]{3,2,1,0:T(8,128)(2,1)}, u32[]{:S(2)}, u32[]{:S(2)}) collective-permute-start(bf16[4,4,64,256]{3,2,1,0:T(8,128)(2,1)S(1)} %bitcast.148), channel_id=1, source_target_pairs={{0,192},{64,0},{128,64},{192,128},{1,193},{65,1},{129,65},{193,129... | collective-permute-start | bytes 1572872 | tf_op jit(solution)/shard_map/ppermute | solution.py:224
  136.4 19.6 %copy-start.7 = (bf16[4,4,64,256]{3,2,1,0:T(8,128)(2,1)S(1)}, bf16[4,4,64,256]{3,2,1,0:T(8,128)(2,1)}, u32[]{:S(2)}) copy-start(bf16[4,4,64,256]{3,2,1,0:T(8,128)(2,1)} %copy-done.6) | copy-start | bytes 1572868
  149.9 11.5 %collective-permute-start.13 = (bf16[4,64,256]{2,1,0:T(8,128)(2,1)S(1)}, bf16[4,64,256]{2,1,0:T(8,128)(2,1)S(1)}, u32[]{:S(2)}, u32[]{:S(2)}) collective-permute-start(bf16[4,64,256]{2,1,0:T(8,128)(2,1)S(1)} %get-tuple-element.51), channel_id=1, source_target_pairs={{0,2},{1,3},{2,0},{3,1},{4,6},{5,7},{6,4},{7,5},{8,10},{9,11},{10,... | collective-permute-start | bytes 393224 | tf_op jit(solution)/shard_map/ppermute | solution.py:224
  150.8 11.3 %collective-permute-start.15 = (bf16[4,64,256]{2,1,0:T(8,128)(2,1)S(1)}, bf16[4,64,256]{2,1,0:T(8,128)(2,1)S(1)}, u32[]{:S(2)}, u32[]{:S(2)}) collective-permute-start(bf16[4,64,256]{2,1,0:T(8,128)(2,1)S(1)} %get-tuple-element.52), channel_id=1, source_target_pairs={{0,3},{1,0},{2,1},{3,2},{4,7},{5,4},{6,5},{7,6},{8,11},{9,8},{10,9... | collective-permute-start | bytes 393224 | tf_op jit(solution)/shard_map/ppermute | solution.py:224
  154.8 7.4 %collective-permute-start.14 = (bf16[4,64,256]{2,1,0:T(8,128)(2,1)S(1)}, bf16[4,64,256]{2,1,0:T(8,128)(2,1)S(1)}, u32[]{:S(2)}, u32[]{:S(2)}) collective-permute-start(bf16[4,64,256]{2,1,0:T(8,128)(2,1)S(1)} %get-tuple-element.53), channel_id=1, source_target_pairs={{0,1},{1,2},{2,3},{3,0},{4,5},{5,6},{6,7},{7,4},{8,9},{9,10},{10,1... | collective-permute-start | bytes 393224 | tf_op jit(solution)/shard_map/ppermute | solution.py:224
  157.4 7.8 %collective-permute-start.10 = (bf16[4,64,256]{2,1,0:T(8,128)(2,1)S(1)}, bf16[4,64,256]{2,1,0:T(8,128)(2,1)S(1)}, u32[]{:S(2)}, u32[]{:S(2)}) collective-permute-start(bf16[4,64,256]{2,1,0:T(8,128)(2,1)S(1)} %get-tuple-element.48), channel_id=1, source_target_pairs={{0,128},{64,192},{128,0},{192,64},{1,129},{65,193},{129,1},{193,65... | collective-permute-start | bytes 393224 | tf_op jit(solution)/shard_map/ppermute | solution.py:224
  159.8 6.7 %collective-permute-start.12 = (bf16[4,64,256]{2,1,0:T(8,128)(2,1)S(1)}, bf16[4,64,256]{2,1,0:T(8,128)(2,1)S(1)}, u32[]{:S(2)}, u32[]{:S(2)}) collective-permute-start(bf16[4,64,256]{2,1,0:T(8,128)(2,1)S(1)} %get-tuple-element.49), channel_id=1, source_target_pairs={{0,192},{64,0},{128,64},{192,128},{1,193},{65,1},{129,65},{193,129... | collective-permute-start | bytes 393224 | tf_op jit(solution)/shard_map/ppermute | solution.py:224
  161.4 6.2 %collective-permute-start.11 = (bf16[4,64,256]{2,1,0:T(8,128)(2,1)S(1)}, bf16[4,64,256]{2,1,0:T(8,128)(2,1)S(1)}, u32[]{:S(2)}, u32[]{:S(2)}) collective-permute-start(bf16[4,64,256]{2,1,0:T(8,128)(2,1)S(1)} %get-tuple-element.50), channel_id=1, source_target_pairs={{0,64},{64,128},{128,192},{192,0},{1,65},{65,129},{129,193},{193,1... | collective-permute-start | bytes 393224 | tf_op jit(solution)/shard_map/ppermute | solution.py:224
  168.4 17.6 %all-to-all-start.3 = ((bf16[8,64,256]{2,1,0:T(8,128)(2,1)}), bf16[8,64,256]{2,1,0:T(8,128)(2,1)S(1)}, u32[]{:S(2)}, u32[]{:S(2)}) async-start(bf16[8,64,256]{2,1,0:T(8,128)(2,1)} %pad_maximum_fusion), calls=%async_computation.3 | async-start | bytes 524288 | tf_op jit(solution)/shard_map/all_to_all | solution.py:219
Sparse Core Ops, SparseCore 0:
  28.7 54.2 all-gather.1

commit v6 on v5

--- a/solution.py
+++ b/solution.py
@@ -77,10 +77,13 @@
 
 def attend(codes, counts, own, ends, turns, qg_ref, kv_hbm, od_ref, *refs):
     parts, (kv_ref, acc, st, sems) = refs[:8], refs[8:]
-    load = pltpu.make_async_copy(kv_hbm, kv_ref, sems.at[0])
-    load.start()
+    loads = [
+        pltpu.make_async_copy(kv_hbm.at[:, :, cut], kv_ref.at[:, :, cut], sems.at[i])
+        for i, cut in ((0, pl.ds(0, HEAD)), (9, pl.ds(HEAD, HEAD)))]
+    for load in loads:
+        load.start()
     acc[...] = jnp.zeros_like(acc)
-    load.wait()
+    loads[0].wait()
     key_at = lax.broadcasted_iota(jnp.int32, (TILE, ROWS), 0).astype(jnp.float32)
     lane = lax.broadcasted_iota(jnp.int32, (1, ROWS), 1) & (TILE - 1)
 
@@ -125,6 +128,11 @@
             return tuple(new)
 
         tops = lax.fori_loop(0, chunks, scores, (jnp.full((8, ROWS), NEG, jnp.float32),) * TOGETHER)
+
+        @pl.when(n == 0)
+        def _():
+            loads[1].wait()
+
         tops = [jnp.max(top, axis=0, keepdims=True) * (SCALE * LOG2E) for top in tops]
 
         def forward(c, held):
@@ -208,7 +216,7 @@
             pltpu.VMEM((TILES, TILE, 2 * HEAD), jnp.bfloat16),
             pltpu.VMEM((TILES, TILE, 2 * HEAD), jnp.bfloat16),
             pltpu.VMEM((TOGETHER, MOST_CHUNKS, CHUNK * TILE, ROWS), jnp.float32),
-            pltpu.SemaphoreType.DMA((9,)),
+            pltpu.SemaphoreType.DMA((10,)),
         ],
         compiler_params=pltpu.CompilerParams(vmem_limit_bytes=48 * 1024 * 1024),
         name="attend",

time: 196 us -> 196 us (level)
  starting transfers between devices: 44.9 us -> 39.3 us
  Pallas kernels: 20.9 us -> 26.4 us
    pallas_call x1, Pallas kernels: 20.9 us -> 26.4 us  [attention(): pl.pallas_call(attend, out_shape=(jax.ShapeDtypeStruct((NZ, TILE, 2 * WID...]
    ppermute x16, starting transfers between devices: 27.2 us -> 21.7 us  [shift(): lax.ppermute(array, axis, [(i, (i + by) % size) for i in range(size)])]
  transfers between devices with their start and end apart: 20 -> 20, of which waited for: 10 -> 9; matrix products, arithmetic and copies ran while one was open for 9% -> 9% of each run, Pallas kernels for 0% -> 0%
where the time goes in v6:
time: 196 us; the launch traced here: 195 us
  blocking collectives  56.4 us (29%)
  starting transfers between devices  39.3 us (20%)
  waiting for transfers between devices  33.8 us (17%)
  Pallas kernels  26.4 us (13%)
  between operations  15.2 us (8%)
  other arithmetic  13.5 us (7%)
  local copies, waits for them, and re-layouts  10 us (5%)
    unnamed x1, blocking collectives  36.2 us
    pallas_call x1, Pallas kernels, attention(): pl.pallas_call(attend, out_shape=(jax.ShapeDtypeStruct((NZ, TILE, 2 * WID...  26.4 us
    ppermute x16, starting transfers between devices, shift(): lax.ppermute(array, axis, [(i, (i + by) % size) for i in range(size)])  21.7 us
    ppermute x16, waiting for transfers between devices, shift(): lax.ppermute(array, axis, [(i, (i + by) % size) for i in range(size)])  20.8 us
    all_to_all x1, blocking collectives, exchange(): return lax.all_to_all(blocks, axes, split_axis=0, concat_axis=0, tiled=True)  20.2 us
    all_to_all x3, starting transfers between devices, exchange(): return lax.all_to_all(blocks, axes, split_axis=0, concat_axis=0, tiled=True)  17.6 us
    convert_element_type x7, other arithmetic, added(): return sum((a.astype(jnp.float32) for a in arrays)).astype(jnp.bfloat16)  8.28 us
    all_to_all x3, waiting for transfers between devices, exchange(): return lax.all_to_all(blocks, axes, split_axis=0, concat_axis=0, tiled=True)  7.51 us
  transfers between devices with their start and end apart: 20, of which 9 were waited for; matrix products, arithmetic and copies ran while one was open for 9% of the time, Pallas kernels for 0%

profile of v6, /device:TPU:6, one launch (start us, length us, event | category | flops | bytes accessed | tf_op | source)
XLA Modules:
  0.0 194.8 jit_solution(8907167573007341312)
XLA Ops:
  7.2 1.0 fusion.32
  8.3 20.2 %all_to_all.20 = bf16[8,64,256]{2,1,0:T(8,128)(2,1)} all-to-all(bf16[8,64,256]{2,1,0:T(8,128)(2,1)S(1)} %fusion.22), channel_id=1, replica_groups=mesh['y'=4,'z'=8,'core'=2,'x'=4] {'z'}, dimensions={0} | all-to-all | bytes 524288 | tf_op jit(solution)/shard_map/all_to_all | solution.py:227
  28.6 0.1 copy_bitcast_fusion
  28.8 1.2 maximum_bitcast_fusion
  30.0 3.6 %all-to-all-start = ((bf16[8,64,1024]{2,1,0:T(8,128)(2,1)}), bf16[8,64,1024]{2,1,0:T(8,128)(2,1)S(1)}, u32[]{:S(2)}, u32[]{:S(2)}) async-start(bf16[8,64,1024]{2,1,0:T(8,128)(2,1)} %maximum_bitcast_fusion), calls=%async_computation | async-start | bytes 2097152 | tf_op jit(solution)/shard_map/all_to_all | solution.py:227
  33.6 0.2 reduce-window.18
  33.7 0.5 broadcast.197
  34.3 0.7 reduce.9
  35.1 0.6 dynamic-slice.7
  36.3 0.2 dynamic-update-slice
  36.6 36.2 %all-reduce = s32[256]{0:T(256)S(1)} all-reduce(s32[256]{0:T(256)S(1)} %dynamic-update-slice), channel_id=1, replica_groups=mesh['y'=4,'z'=8,'core'=2,'x'=4] {'y','z','core'}, use_global_device_ids=true, to_apply=%add | all-reduce | flops 256 | bytes 2048
  72.7 0.1 reshape.343
  73.0 0.2 select_reduce_fusion.1
  73.4 0.1 sub.91
  73.5 0.1 sub.85
  73.6 0.3 dynamic-slice_reduce_fusion.own
  74.2 0.2 fusion.10
  74.4 0.6 reduce-window.19
  75.0 0.2 slice_reduce_fusion
  75.3 0.1 copy.46
  75.5 0.2 fusion.14
  75.7 0.2 slice_reduce_fusion.1.counts
  75.9 0.2 convert_reduce_fusion.1
  76.1 0.1 select_reduce_fusion.2.turns
  76.2 0.3 select_reduce_fusion.codes
  76.5 1.0 copy-done
  77.5 5.5 %all-gather.2.cloned.1.call-done.kv_hbm = bf16[256,64,256]{2,1,0:T(8,128)(2,1)} async-done(((bf16[8,64,256]{2,1,0:T(8,128)(2,1)}), bf16[256,64,256]{2,1,0:T(8,128)(2,1)}) %all-gather.2.cloned.1.call-update) | async-done | bytes 8388624 | tf_op jit(solution)/shard_map/all_gather | solution.py:270
  83.0 26.4 %attend.1 = (bf16[8,64,1024]{2,1,0:T(8,128)(2,1)}, bf16[32,64,256]{2,1,0:T(8,128)(2,1)S(1)}, bf16[32,64,256]{2,1,0:T(8,128)(2,1)S(1)}, bf16[32,64,256]{2,1,0:T(8...) custom-call(s32[8,72]{1,0:T(8,128)S(1)} %select_reduce_fusion.codes,, ...), custom_call_target="tpu_custom_call" | custom-call | tf_op jit(solution)/shard_map/attend/pallas_call | solution.py:210
  109.5 0.1 collective-permute-start
  109.6 0.5 collective-permute-start.2
  110.1 0.1 collective-permute-start.4
  110.2 7.0 %all-to-all-start.2 = ((bf16[8,64,1024]{2,1,0:T(8,128)(2,1)}), bf16[8,64,1024]{2,1,0:T(8,128)(2,1)}, u32[]{:S(2)}, u32[]{:S(2)}) async-start(bf16[8,64,1024]{2,1,0:T(8,128)(2,1)} %get-tuple-element.20), calls=%async_computation.2 | async-start | bytes 2097152 | tf_op jit(solution)/shard_map/all_to_all | solution.py:227
  117.1 0.2 collective-permute-start.9
  117.4 2.0 %add_convert_fusion.4 = (bf16[16,64,256]{2,1,0:T(8,128)(2,1)S(1)}, bf16[16,64,256]{2,1,0:T(8,128)(2,1)S(1)}) fusion(bf16[32,64,256]{2,1,0:T(8,128)(2,1)} %collective-permute-done, bf16[32,64,256]{2,1,0:T(8,128)(2,1)} %get-tuple-element.21), kind=kLoop, calls=%fused_computation.7 | loop fusion | flops 2097152 | bytes 3145728 | tf_op jit(solution)/shard_map/convert_element_type | solution.py:236
  119.5 1.5 collective-permute-start.6
  121.0 1.6 add_convert_fusion.3
  122.6 4.4 %collective-permute-start.3 = (bf16[4,4,64,256]{3,2,1,0:T(8,128)(2,1)S(1)}, bf16[4,4,64,256]{3,2,1,0:T(8,128)(2,1)S(1)}, u32[]{:S(2)}, u32[]{:S(2)}) collective-permute-start(bf16[4,4,64,256]{3,2,1,0:T(8,128)(2,1)S(1)} %bitcast.146), channel_id=1, source_target_pairs={{0,1},{1,2},{2,3},{3,0},{4,5},{5,6},{6,7},{7,4},{8,9},{9,10},{10,1... | collective-permute-start | bytes 1572872 | tf_op jit(solution)/shard_map/ppermute | solution.py:232
  127.0 2.6 %collective-permute-start.7 = (bf16[4,4,64,256]{3,2,1,0:T(8,128)(2,1)S(1)}, bf16[4,4,64,256]{3,2,1,0:T(8,128)(2,1)}, u32[]{:S(2)}, u32[]{:S(2)}) collective-permute-start(bf16[4,4,64,256]{3,2,1,0:T(8,128)(2,1)S(1)} %bitcast.145), channel_id=1, source_target_pairs={{0,64},{64,128},{128,192},{192,0},{1,65},{65,129},{129,193},{193,1... | collective-permute-start | bytes 1572872 | tf_op jit(solution)/shard_map/ppermute | solution.py:232
  129.6 1.6 add_convert_fusion.2
  131.2 1.1 collective-permute-start.5
  132.3 3.4 %collective-permute-done.1 = bf16[4,4,64,256]{3,2,1,0:T(8,128)(2,1)S(1)} collective-permute-done((bf16[4,4,64,256]{3,2,1,0:T(8,128)(2,1)S(1)}, bf16[4,4,64,256]{3,2,1,0:T(8,128)(2,1)S(1)}, u32[]{:S(2)}, u32[]{:S(2)}) %collective-permute-start.1) | collective-permute-done | bytes 524320 | tf_op jit(solution)/shard_map/ppermute | solution.py:232
  135.7 0.4 convert_add_fusion.1
  136.1 0.4 copy-done.6
  136.5 9.9 %collective-permute-done.3 = bf16[4,4,64,256]{3,2,1,0:T(8,128)(2,1)S(1)} collective-permute-done((bf16[4,4,64,256]{3,2,1,0:T(8,128)(2,1)S(1)}, bf16[4,4,64,256]{3,2,1,0:T(8,128)(2,1)S(1)}, u32[]{:S(2)}, u32[]{:S(2)}) %collective-permute-start.3) | collective-permute-done | bytes 524320 | tf_op jit(solution)/shard_map/ppermute | solution.py:232
  146.4 0.1 collective-permute-done.7
  146.5 2.1 %collective-permute-done.8 = bf16[4,4,64,256]{3,2,1,0:T(8,128)(2,1)} collective-permute-done((bf16[4,4,64,256]{3,2,1,0:T(8,128)(2,1)S(1)}, bf16[4,4,64,256]{3,2,1,0:T(8,128)(2,1)}, u32[]{:S(2)}, u32[]{:S(2)}) %collective-permute-start.8) | collective-permute-done | bytes 524320 | tf_op jit(solution)/shard_map/ppermute | solution.py:232
  148.6 1.7 add_convert_fusion
  150.3 1.8 collective-permute-start.13
  152.1 4.5 %collective-permute-start.15 = (bf16[4,64,256]{2,1,0:T(8,128)(2,1)S(1)}, bf16[4,64,256]{2,1,0:T(8,128)(2,1)S(1)}, u32[]{:S(2)}, u32[]{:S(2)}) collective-permute-start(bf16[4,64,256]{2,1,0:T(8,128)(2,1)S(1)} %get-tuple-element.52), channel_id=1, source_target_pairs={{0,3},{1,0},{2,1},{3,2},{4,7},{5,4},{6,5},{7,6},{8,11},{9,8},{10,9... | collective-permute-start | bytes 393224 | tf_op jit(solution)/shard_map/ppermute | solution.py:232
  156.6 1.3 add_convert_fusion.1
  158.0 2.4 %collective-permute-start.10 = (bf16[4,64,256]{2,1,0:T(8,128)(2,1)S(1)}, bf16[4,64,256]{2,1,0:T(8,128)(2,1)S(1)}, u32[]{:S(2)}, u32[]{:S(2)}) collective-permute-start(bf16[4,64,256]{2,1,0:T(8,128)(2,1)S(1)} %get-tuple-element.48), channel_id=1, source_target_pairs={{0,128},{64,192},{128,0},{192,64},{1,129},{65,193},{129,1},{193,65... | collective-permute-start | bytes 393224 | tf_op jit(solution)/shard_map/ppermute | solution.py:232
  160.3 1.6 collective-permute-start.12
  161.9 0.8 collective-permute-start.11
  162.8 3.0 %collective-permute-done.10 = bf16[4,64,256]{2,1,0:T(8,128)(2,1)S(1)} collective-permute-done((bf16[4,64,256]{2,1,0:T(8,128)(2,1)S(1)}, bf16[4,64,256]{2,1,0:T(8,128)(2,1)S(1)}, u32[]{:S(2)}, u32[]{:S(2)}) %collective-permute-start.10) | collective-permute-done | bytes 131104 | tf_op jit(solution)/shard_map/ppermute | solution.py:232
  165.8 1.3 collective-permute-done.12
  167.1 1.0 collective-permute-done.11
  168.2 0.7 pad_maximum_fusion
  168.9 7.1 %all-to-all-start.3 = ((bf16[8,64,256]{2,1,0:T(8,128)(2,1)}), bf16[8,64,256]{2,1,0:T(8,128)(2,1)S(1)}, u32[]{:S(2)}, u32[]{:S(2)}) async-start(bf16[8,64,256]{2,1,0:T(8,128)(2,1)} %pad_maximum_fusion), calls=%async_computation.3 | async-start | bytes 524288 | tf_op jit(solution)/shard_map/all_to_all | solution.py:227
  176.0 1.3 slice_bitcast_fusion
  177.3 0.8 copy.57
  178.2 0.8 copy.56
  179.0 7.5 %all-to-all-done.3 = bf16[8,64,256]{2,1,0:T(8,128)(2,1)S(1)} async-done(((bf16[8,64,256]{2,1,0:T(8,128)(2,1)}), bf16[8,64,256]{2,1,0:T(8,128)(2,1)S(1)}, u32[]{:S(2)}, u32[]{:S(2)}) %all-to-all-start.3) | async-done | bytes 262176 | tf_op jit(solution)/shard_map/all_to_all | solution.py:227
  186.6 0.7 copy.64
  187.2 0.7 copy.65
  (77 shorter events, 1.4 us)
Async XLA Ops:
  7.2 21.4 %copy-start.4 = (bf16[64,4096]{1,0:T(8,128)(2,1)S(1)}, bf16[64,4096]{1,0:T(8,128)(2,1)}, u32[]{:S(2)}) copy-start(bf16[64,4096]{1,0:T(8,128)(2,1)} %param.11) | copy-start | bytes 1572868
  7.2 21.4 %copy-start.5 = (bf16[64,4096]{1,0:T(8,128)(2,1)S(1)}, bf16[64,4096]{1,0:T(8,128)(2,1)}, u32[]{:S(2)}) copy-start(bf16[64,4096]{1,0:T(8,128)(2,1)} %param.8) | copy-start | bytes 1572868
  7.2 75.8 %all-gather.2.cloned.1.call-start = ((), (), s32[]{:S(2)}) async-start(), calls=%async_computation.4 | async-start | bytes 8650752 | tf_op jit(solution)/shard_map/all_gather | solution.py:270
  28.7 4.8 %copy-start.10 = (s32[4]{0:T(128)S(1)}, s32[4]{0:T(128)}, u32[]{:S(2)}) copy-start(s32[4]{0:T(128)} %param.13) | copy-start | bytes 52
  28.7 5.5 %copy-start.9 = (s32[4096,1]{0,1:T(1,128)S(1)}, s32[4096,1]{0,1:T(1,128)}, u32[]{:S(2)}) copy-start(s32[4096,1]{0,1:T(1,128)} %param.14) | copy-start | bytes 49156
  28.7 6.3 %copy-start.12 = (u32[256]{0:T(256)S(1)}, u32[256]{0:T(256)}, u32[]{:S(2)}) copy-start(u32[256]{0:T(256)} %constant.247) | copy-start | bytes 3076
  28.8 7.6 %copy-start.11 = (s32[4]{0:T(128)S(1)}, s32[4]{0:T(128)}, u32[]{:S(2)}) copy-start(s32[4]{0:T(128)} %param.12) | copy-start | bytes 52
  28.8 44.1 %copy-start.8 = (s32[4096]{0:T(1024)S(1)}, s32[4096]{0:T(1024)}, u32[]{:S(2)}) copy-start(s32[4096]{0:T(1024)} %param.15) | copy-start | bytes 49156
  30.0 46.5 %all-to-all-start = ((bf16[8,64,1024]{2,1,0:T(8,128)(2,1)}), bf16[8,64,1024]{2,1,0:T(8,128)(2,1)S(1)}, u32[]{:S(2)}, u32[]{:S(2)}) async-start(bf16[8,64,1024]{2,1,0:T(8,128)(2,1)} %maximum_bitcast_fusion), calls=%async_computation | async-start | bytes 2097152 | tf_op jit(solution)/shard_map/all_to_all | solution.py:227
  76.5 1.0 copy-start
  109.5 7.9 %collective-permute-start = (bf16[32,64,256]{2,1,0:T(8,128)(2,1)}, bf16[32,64,256]{2,1,0:T(8,128)(2,1)}, u32[]{:S(2)}, u32[]{:S(2)}) collective-permute-start(bf16[32,64,256]{2,1,0:T(8,128)(2,1)} %get-tuple-element.22), channel_id=1, source_target_pairs={{0,4},{4,0},{1,5},{5,1},{2,6},{6,2},{3,7},{7,3},{8,12},{12,8},{9,1... | collective-permute-start | bytes 3145736 | tf_op jit(solution)/shard_map/ppermute | solution.py:232
  109.6 11.4 %collective-permute-start.2 = (bf16[32,64,256]{2,1,0:T(8,128)(2,1)S(1)}, bf16[32,64,256]{2,1,0:T(8,128)(2,1)}, u32[]{:S(2)}, u32[]{:S(2)}) collective-permute-start(bf16[32,64,256]{2,1,0:T(8,128)(2,1)S(1)} %get-tuple-element.24), channel_id=1, source_target_pairs={{0,4},{4,0},{1,5},{5,1},{2,6},{6,2},{3,7},{7,3},{8,12},{12,8},{9,1... | collective-permute-start | bytes 3145736 | tf_op jit(solution)/shard_map/ppermute | solution.py:232
  110.1 16.9 %collective-permute-start.4 = (bf16[32,64,256]{2,1,0:T(8,128)(2,1)S(1)}, bf16[32,64,256]{2,1,0:T(8,128)(2,1)}, u32[]{:S(2)}, u32[]{:S(2)}) collective-permute-start(bf16[32,64,256]{2,1,0:T(8,128)(2,1)S(1)} %get-tuple-element.26), channel_id=1, source_target_pairs={{0,4},{4,0},{1,5},{5,1},{2,6},{6,2},{3,7},{7,3},{8,12},{12,8},{9,1... | collective-permute-start | bytes 3145736 | tf_op jit(solution)/shard_map/ppermute | solution.py:232
  110.2 38.4 %all-to-all-start.2 = ((bf16[8,64,1024]{2,1,0:T(8,128)(2,1)}), bf16[8,64,1024]{2,1,0:T(8,128)(2,1)}, u32[]{:S(2)}, u32[]{:S(2)}) async-start(bf16[8,64,1024]{2,1,0:T(8,128)(2,1)} %get-tuple-element.20), calls=%async_computation.2 | async-start | bytes 2097152 | tf_op jit(solution)/shard_map/all_to_all | solution.py:227
  117.1 3.8 %copy-start.2 = (bf16[32,64,256]{2,1,0:T(8,128)(2,1)S(1)}, bf16[32,64,256]{2,1,0:T(8,128)(2,1)}, u32[]{:S(2)}) copy-start(bf16[32,64,256]{2,1,0:T(8,128)(2,1)} %get-tuple-element.23) | copy-start | bytes 3145732
  117.1 14.1 %collective-permute-start.9 = (bf16[32,64,256]{2,1,0:T(8,128)(2,1)S(1)}, bf16[32,64,256]{2,1,0:T(8,128)(2,1)S(1)}, u32[]{:S(2)}, u32[]{:S(2)}) collective-permute-start(bf16[32,64,256]{2,1,0:T(8,128)(2,1)S(1)} %get-tuple-element.29), channel_id=1, source_target_pairs={{0,4},{4,0},{1,5},{5,1},{2,6},{6,2},{3,7},{7,3},{8,12},{12,8},{9,1... | collective-permute-start | bytes 3145736 | tf_op jit(solution)/shard_map/ppermute | solution.py:232
  119.4 10.3 %copy-start.1 = (bf16[32,64,256]{2,1,0:T(8,128)(2,1)S(1)}, bf16[32,64,256]{2,1,0:T(8,128)(2,1)}, u32[]{:S(2)}) copy-start(bf16[32,64,256]{2,1,0:T(8,128)(2,1)} %get-tuple-element.25) | copy-start | bytes 3145732
  119.4 16.3 %collective-permute-start.1 = (bf16[4,4,64,256]{3,2,1,0:T(8,128)(2,1)S(1)}, bf16[4,4,64,256]{3,2,1,0:T(8,128)(2,1)S(1)}, u32[]{:S(2)}, u32[]{:S(2)}) collective-permute-start(bf16[4,4,64,256]{3,2,1,0:T(8,128)(2,1)S(1)} %bitcast.147), channel_id=1, source_target_pairs={{0,2},{1,3},{2,0},{3,1},{4,6},{5,7},{6,4},{7,5},{8,10},{9,11},{10,... | collective-permute-start | bytes 1572872 | tf_op jit(solution)/shard_map/ppermute | solution.py:232
  119.5 17.0 %collective-permute-start.6 = (bf16[4,4,64,256]{3,2,1,0:T(8,128)(2,1)S(1)}, bf16[4,4,64,256]{3,2,1,0:T(8,128)(2,1)}, u32[]{:S(2)}, u32[]{:S(2)}) collective-permute-start(bf16[4,4,64,256]{3,2,1,0:T(8,128)(2,1)S(1)} %bitcast.144), channel_id=1, source_target_pairs={{0,128},{64,192},{128,0},{192,64},{1,129},{65,193},{129,1},{193,65... | collective-permute-start | bytes 1572872 | tf_op jit(solution)/shard_map/ppermute | solution.py:232
  122.6 13.1 %copy-start.3 = (bf16[32,64,256]{2,1,0:T(8,128)(2,1)S(1)}, bf16[32,64,256]{2,1,0:T(8,128)(2,1)}, u32[]{:S(2)}) copy-start(bf16[32,64,256]{2,1,0:T(8,128)(2,1)} %get-tuple-element.28) | copy-start | bytes 3145732
  122.6 23.8 %collective-permute-start.3 = (bf16[4,4,64,256]{3,2,1,0:T(8,128)(2,1)S(1)}, bf16[4,4,64,256]{3,2,1,0:T(8,128)(2,1)S(1)}, u32[]{:S(2)}, u32[]{:S(2)}) collective-permute-start(bf16[4,4,64,256]{3,2,1,0:T(8,128)(2,1)S(1)} %bitcast.146), channel_id=1, source_target_pairs={{0,1},{1,2},{2,3},{3,0},{4,5},{5,6},{6,7},{7,4},{8,9},{9,10},{10,1... | collective-permute-start | bytes 1572872 | tf_op jit(solution)/shard_map/ppermute | solution.py:232
  127.0 19.5 %collective-permute-start.7 = (bf16[4,4,64,256]{3,2,1,0:T(8,128)(2,1)S(1)}, bf16[4,4,64,256]{3,2,1,0:T(8,128)(2,1)}, u32[]{:S(2)}, u32[]{:S(2)}) collective-permute-start(bf16[4,4,64,256]{3,2,1,0:T(8,128)(2,1)S(1)} %bitcast.145), channel_id=1, source_target_pairs={{0,64},{64,128},{128,192},{192,0},{1,65},{65,129},{129,193},{193,1... | collective-permute-start | bytes 1572872 | tf_op jit(solution)/shard_map/ppermute | solution.py:232
  131.2 15.3 %collective-permute-start.5 = (bf16[4,4,64,256]{3,2,1,0:T(8,128)(2,1)S(1)}, bf16[4,4,64,256]{3,2,1,0:T(8,128)(2,1)}, u32[]{:S(2)}, u32[]{:S(2)}) collective-permute-start(bf16[4,4,64,256]{3,2,1,0:T(8,128)(2,1)S(1)} %bitcast.149), channel_id=1, source_target_pairs={{0,3},{1,0},{2,1},{3,2},{4,7},{5,4},{6,5},{7,6},{8,11},{9,8},{10,9... | collective-permute-start | bytes 1572872 | tf_op jit(solution)/shard_map/ppermute | solution.py:232
  135.7 0.8 copy-start.6
  135.7 12.9 %collective-permute-start.8 = (bf16[4,4,64,256]{3,2,1,0:T(8,128)(2,1)S(1)}, bf16[4,4,64,256]{3,2,1,0:T(8,128)(2,1)}, u32[]{:S(2)}, u32[]{:S(2)}) collective-permute-start(bf16[4,4,64,256]{3,2,1,0:T(8,128)(2,1)S(1)} %bitcast.148), channel_id=1, source_target_pairs={{0,192},{64,0},{128,64},{192,128},{1,193},{65,1},{129,65},{193,129... | collective-permute-start | bytes 1572872 | tf_op jit(solution)/shard_map/ppermute | solution.py:232
  136.5 20.1 %copy-start.7 = (bf16[4,4,64,256]{3,2,1,0:T(8,128)(2,1)S(1)}, bf16[4,4,64,256]{3,2,1,0:T(8,128)(2,1)}, u32[]{:S(2)}) copy-start(bf16[4,4,64,256]{3,2,1,0:T(8,128)(2,1)} %copy-done.6) | copy-start | bytes 1572868
  150.3 11.6 %collective-permute-start.13 = (bf16[4,64,256]{2,1,0:T(8,128)(2,1)S(1)}, bf16[4,64,256]{2,1,0:T(8,128)(2,1)S(1)}, u32[]{:S(2)}, u32[]{:S(2)}) collective-permute-start(bf16[4,64,256]{2,1,0:T(8,128)(2,1)S(1)} %get-tuple-element.51), channel_id=1, source_target_pairs={{0,2},{1,3},{2,0},{3,1},{4,6},{5,7},{6,4},{7,5},{8,10},{9,11},{10,... | collective-permute-start | bytes 393224 | tf_op jit(solution)/shard_map/ppermute | solution.py:232
  152.1 10.6 %collective-permute-start.15 = (bf16[4,64,256]{2,1,0:T(8,128)(2,1)S(1)}, bf16[4,64,256]{2,1,0:T(8,128)(2,1)S(1)}, u32[]{:S(2)}, u32[]{:S(2)}) collective-permute-start(bf16[4,64,256]{2,1,0:T(8,128)(2,1)S(1)} %get-tuple-element.52), channel_id=1, source_target_pairs={{0,3},{1,0},{2,1},{3,2},{4,7},{5,4},{6,5},{7,6},{8,11},{9,8},{10,9... | collective-permute-start | bytes 393224 | tf_op jit(solution)/shard_map/ppermute | solution.py:232
  156.5 6.1 %collective-permute-start.14 = (bf16[4,64,256]{2,1,0:T(8,128)(2,1)S(1)}, bf16[4,64,256]{2,1,0:T(8,128)(2,1)S(1)}, u32[]{:S(2)}, u32[]{:S(2)}) collective-permute-start(bf16[4,64,256]{2,1,0:T(8,128)(2,1)S(1)} %get-tuple-element.53), channel_id=1, source_target_pairs={{0,1},{1,2},{2,3},{3,0},{4,5},{5,6},{6,7},{7,4},{8,9},{9,10},{10,1... | collective-permute-start | bytes 393224 | tf_op jit(solution)/shard_map/ppermute | solution.py:232
  158.0 7.8 %collective-permute-start.10 = (bf16[4,64,256]{2,1,0:T(8,128)(2,1)S(1)}, bf16[4,64,256]{2,1,0:T(8,128)(2,1)S(1)}, u32[]{:S(2)}, u32[]{:S(2)}) collective-permute-start(bf16[4,64,256]{2,1,0:T(8,128)(2,1)S(1)} %get-tuple-element.48), channel_id=1, source_target_pairs={{0,128},{64,192},{128,0},{192,64},{1,129},{65,193},{129,1},{193,65... | collective-permute-start | bytes 393224 | tf_op jit(solution)/shard_map/ppermute | solution.py:232
  160.3 6.7 %collective-permute-start.12 = (bf16[4,64,256]{2,1,0:T(8,128)(2,1)S(1)}, bf16[4,64,256]{2,1,0:T(8,128)(2,1)S(1)}, u32[]{:S(2)}, u32[]{:S(2)}) collective-permute-start(bf16[4,64,256]{2,1,0:T(8,128)(2,1)S(1)} %get-tuple-element.49), channel_id=1, source_target_pairs={{0,192},{64,0},{128,64},{192,128},{1,193},{65,1},{129,65},{193,129... | collective-permute-start | bytes 393224 | tf_op jit(solution)/shard_map/ppermute | solution.py:232
  161.9 6.2 %collective-permute-start.11 = (bf16[4,64,256]{2,1,0:T(8,128)(2,1)S(1)}, bf16[4,64,256]{2,1,0:T(8,128)(2,1)S(1)}, u32[]{:S(2)}, u32[]{:S(2)}) collective-permute-start(bf16[4,64,256]{2,1,0:T(8,128)(2,1)S(1)} %get-tuple-element.50), channel_id=1, source_target_pairs={{0,64},{64,128},{128,192},{192,0},{1,65},{65,129},{129,193},{193,1... | collective-permute-start | bytes 393224 | tf_op jit(solution)/shard_map/ppermute | solution.py:232
  168.9 17.6 %all-to-all-start.3 = ((bf16[8,64,256]{2,1,0:T(8,128)(2,1)}), bf16[8,64,256]{2,1,0:T(8,128)(2,1)S(1)}, u32[]{:S(2)}, u32[]{:S(2)}) async-start(bf16[8,64,256]{2,1,0:T(8,128)(2,1)} %pad_maximum_fusion), calls=%async_computation.3 | async-start | bytes 524288 | tf_op jit(solution)/shard_map/all_to_all | solution.py:227
Sparse Core Ops, SparseCore 0:
  28.7 54.2 all-gather.1
